TPU v7x, 128 devices: a whole 4x4x4 slice. The times are simulated.
128 devices in a mesh: img: 16 (over z, y), space: 8 (over x, core).
Axes of the slice: x: 4, y: 4, z: 4, core: 2. Of those that a mesh axis runs over, the one named last changes fastest.
Arguments:
- path: float32 [16, 8, 1024, 1024], P('img', None, 'space'), may hold values from -3 to 3
- tilt: float32 [8, 1024, 1024], P(None, 'space'), may hold values from -4 to 4
Outputs:
- new_path: float32 [16, 8, 1024, 1024], P('img', None, 'space')
All inputs are finite; a program needn't handle non-finite values.
Results may differ from a plain program's by a relative error of at most 0.0003.
Values sent between devices are 32-bit elements; how exact they have to be, the bound alone decides.
No kernel may reach another device: no remote copies, remote signals or barrier semaphores. Data moves between devices by JAX's collectives and lax.ppermute only.
A program may use at most 128 MiB of HBM per device.

v0:
```python
import jax
import jax.numpy as jnp
from jax import lax
from jax.sharding import PartitionSpec as P

STEPS = 2


KAPPA = 1.0
DT = 0.006
EPS = 1e-06


def extended(block, sides, width, periodic):
    for axis, dim in sides:
        count = lax.axis_size(axis)
        forward = [(i, i + 1) for i in range(count - 1)]
        if periodic:
            forward.append((count - 1, 0))
        backward = [(target, source) for source, target in forward]
        low = lax.ppermute(
            lax.slice_in_dim(block, block.shape[dim] - width, None, axis=dim), axis, forward
        )
        high = lax.ppermute(lax.slice_in_dim(block, 0, width, axis=dim), axis, backward)
        block = jnp.concatenate([low, block, high], axis=dim)
    return block


def shifted(block, axis, distance):
    devices = range(lax.axis_size(axis))
    route = [(i - distance, i) for i in devices if i - distance in devices]
    return lax.ppermute(block, axis, route)


def laplace(ext):
    core = ext[..., 1:-1, :]
    total = ext[..., 2:, :] + ext[..., :-2, :]
    total = total + jnp.roll(core, 1, axis=-1) + jnp.roll(core, -1, axis=-1)
    total = total + jnp.roll(core, 1, axis=-3) + jnp.roll(core, -1, axis=-3)
    return total - 6.0 * core


def spacing(dist):
    count = dist.shape[0]
    arc = jnp.cumsum(dist)
    target = jnp.arange(count).astype(dist.dtype) * (arc[count - 1] / (count - 1))
    slots = jnp.arange(count, dtype=jnp.int32)
    inside = (
        (slots[None, :] >= 1) & (slots[None, :] <= count - 2) & (arc[None, :] <= target[:, None])
    )
    lower = jnp.sum(inside.astype(jnp.int32), axis=1)
    pick_low = (slots[None, :] == lower[:, None]).astype(dist.dtype)
    pick_high = (slots[None, :] == lower[:, None] + 1).astype(dist.dtype)
    start = jnp.sum(pick_low * arc[None, :], axis=1)
    length = jnp.sum(pick_high * dist[None, :], axis=1)
    share = (target - start) / length
    return pick_low * (1.0 - share)[:, None] + pick_high * share[:, None]


def flow_force(phi, tilt):
    ext = extended(phi, (("space", 2),), 1, True)
    own = phi * phi * phi - phi - KAPPA * laplace(ext) - tilt
    potential = extended(own, (("space", 2),), 1, True)
    return laplace(potential)


def regroup(phi):
    gathered = lax.all_to_all(phi, "img", split_axis=2, concat_axis=0, tiled=True)
    return gathered


def restore(moved):
    result = lax.all_to_all(moved, "img", split_axis=0, concat_axis=2, tiled=True)
    return result


def per_device(path, tilt):
    count_own = path.shape[0]
    images = count_own * lax.axis_size("img")
    index = lax.axis_index("img") * count_own + jnp.arange(count_own, dtype=jnp.int32)
    interior = ((index > 0) & (index < images - 1))[:, None, None, None]
    phi = path
    for step in range(STEPS):
        near = extended(phi, (("img", 0),), 1, False)
        force = flow_force(phi, tilt)
        diff = near[2:] - near[:-2]
        squares, products = lax.psum(
            (jnp.sum(diff * diff, axis=(1, 2, 3)), jnp.sum(force * diff, axis=(1, 2, 3))), "space"
        )
        coef = (products / (squares + EPS))[:, None, None, None]
        direction = jnp.where(interior, force - coef * diff, force)
        phi = phi + DT * direction
    before = shifted(phi, "img", 1)
    chain = jnp.concatenate([before, phi], axis=0)
    gap = chain[1:] - chain[:-1]
    totals = lax.psum(jnp.sum(gap * gap, axis=(1, 2, 3)), "space")
    own = jnp.where(index > 0, jnp.sqrt(totals + EPS), 0.0)
    dist = lax.all_gather(own, "img", axis=0, tiled=True)
    gathered = regroup(phi)
    weights = spacing(dist)
    flat = gathered.reshape(gathered.shape[0], -1)
    moved = jnp.dot(
        weights, flat, precision=lax.Precision.HIGHEST, preferred_element_type=jnp.float32
    )
    return restore(moved.reshape(gathered.shape))


def solution(mesh):
    return jax.shard_map(
        per_device,
        mesh=mesh,
        in_specs=(P("img", None, "space", None), P(None, "space", None)),
        out_specs=P("img", None, "space", None),
        check_vma=False,
    )
```

profile of v0, /device:TPU:0, one launch (start us, length us, event | category | flops | bytes accessed | tf_op | source)
XLA Modules:
  0.0 574.4 jit_solution(18114391136671490443)
XLA Ops:
  0.0 6.6 %copy.28 = f32[1,8,128,1024]{3,1,0,2:T(8,128)} copy(f32[1,8,128,1024]{3,2,1,0:T(8,128)} %param.2) | data formatting | bytes 8388608 | tf_op args[0]
  7.9 6.5 %collective-permute-start.5 = (f32[1,8,128,1024]{3,1,0,2:T(8,128)}, f32[1,8,128,1024]{3,1,0,2:T(8,128)}, u32[]{:S(2)}, u32[]{:S(2)}) collective-permute-start(f32[1,8,128,1024]{3,1,0,2:T(8,128)} %copy.28), channel_id=1, source_target_pairs={{0,8},{8,16},{16,24},{24,32},{32,40},{40,48},{48,56},{56,64},{64,7... | collective-permute-start | bytes 12582920 | tf_op jit(solution)/shard_map/ppermute | solution.py:21
  16.9 8.6 %fusion.61 = (f32[1,7,128,1024]{3,1,0,2:T(8,128)}, f32[1,7,128,1024]{3,1,0,2:T(8,128)}) fusion(f32[1,8,128,1024]{3,1,0,2:T(8,128)} %copy.28), kind=kLoop, calls=%fused_computation.89 | loop fusion | bytes 14680064 | tf_op jit(solution)/shard_map/jit(_roll_static)/slice | solution.py:39
  26.9 8.0 %fusion.63 = (f32[1,8,128,1023]{3,1,0,2:T(8,128)}, f32[1,8,128,1023]{3,1,0,2:T(8,128)}) fusion(f32[1,8,128,1024]{3,1,0,2:T(8,128)} %copy.28), kind=kLoop, calls=%fused_computation.91 | loop fusion | bytes 16760832 | tf_op jit(solution)/shard_map/jit(_roll_static)/slice | solution.py:38
  37.3 15.0 %fusion.1 = f32[1,8,128,1024]{3,1,0,2:T(8,128)S(1)} fusion(f32[1,8,128,1024]{3,1,0,2:T(8,128)} %copy.28, f32[1,8,1,1024]{3,1,0,2:T(8,128)S(1)} %collective-permute-done.1, f32[1,8,1,1024]{3,1,0,2:T(8,128)S(1)} %collective-permute-done, f32[1,8,128,1023]{3,1,0,2:T(8,128)} %get-tuple-element.54, f32[1,8,128,1]{3,1,0,2:T(8,128)S(1)} %get-tuple-element.56, ...), kind=kLoop, calls=%fused_computation.5 | loop fusion | flops 18874368 | bytes 29425664 | tf_op jit(solution)/shard_map/sub | solution.py:62
  56.0 4.7 fusion.58
  60.6 4.3 fusion.60
  65.1 36.0 %collective-permute-done.4 = f32[1,8,128,1024]{3,1,0,2:T(8,128)} collective-permute-done((f32[1,8,128,1024]{3,1,0,2:T(8,128)}, f32[1,8,128,1024]{3,1,0,2:T(8,128)}, u32[]{:S(2)}, u32[]{:S(2)}) %collective-permute-start.4) | collective-permute-done | bytes 4194336 | tf_op jit(solution)/shard_map/ppermute | solution.py:24
  102.2 14.1 %multiply_reduce_fusion.3 = (f32[]{:T(128)}, f32[]{:T(128)}, f32[1,8,128,1024]{3,1,0,2:T(8,128)}, f32[1,8,128,1024]{3,1,0,2:T(8,128)}) fusion(f32[1,8,128,1024]{3,1,0,2:T(8,128)} %collective-permute-done.4, f32[1,8,128,1024]{3,1,0,2:T(8,128)} %collective-permute-done.5, f32[1,8,128,1024]{3,1,0,2:T(8,128)S(1)} %fusion.1, ...), kind=kLoop, calls=%fused_computation.51 | loop fusion | flops 18874368 | bytes 37814280 | tf_op jit(solution)/shard_map/reduce_sum | solution.py:88
  116.4 14.4 %all-reduce.2 = (f32[1]{0:T(128)}, f32[1]{0:T(128)}) all-reduce(f32[1]{0:T(128)} %bitcast.4, f32[1]{0:T(128)} %bitcast.5), channel_id=1, replica_groups=mesh['img'=16,'space'=8] {'space'}, use_global_device_ids=true, to_apply=%region_1.2 | all-reduce | flops 2 | bytes 16 | tf_op jit(solution)/shard_map/psum | solution.py:87
  132.1 8.0 %fusion.3 = f32[1,8,128,1024]{3,1,0,2:T(8,128)S(1)} fusion(f32[1,8,128,1024]{3,1,0,2:T(8,128)} %get-tuple-element.18, f32[1,8,128,1024]{3,1,0,2:T(8,128)} %get-tuple-element.17, f32[]{:T(128)} %bitcast.6, pred[]{:T(512)} %bitcast.2, f32[1,8,128,1024]{3,2,1,0:T(8,128)} %param.2), kind=kLoop, calls=%fused_computation.7 | loop fusion | flops 5242880 | bytes 16777220 | tf_op jit(solution)/shard_map/add | solution.py:92
  140.0 4.6 fusion.51
  145.9 7.0 %collective-permute-start.11 = (f32[1,8,128,1024]{3,1,0,2:T(8,128)S(1)}, f32[1,8,128,1024]{3,1,0,2:T(8,128)}, u32[]{:S(2)}, u32[]{:S(2)}) collective-permute-start(f32[1,8,128,1024]{3,1,0,2:T(8,128)S(1)} %fusion.3), channel_id=1, source_target_pairs={{0,8},{8,16},{16,24},{24,32},{32,40},{40,48},{48,56},{56,64},{64,7... | collective-permute-start | bytes 12582920 | tf_op jit(solution)/shard_map/ppermute | solution.py:21
  154.1 4.8 fusion.53
  159.1 11.7 %fusion.5 = f32[1,8,128,1024]{3,1,0,2:T(8,128)S(1)} fusion(f32[1,8,128,1024]{3,1,0,2:T(8,128)S(1)} %fusion.3, f32[1,8,1,1024]{3,1,0,2:T(8,128)S(1)} %collective-permute-done.7, f32[1,8,1,1024]{3,1,0,2:T(8,128)S(1)} %collective-permute-done.6, f32[1,8,128,1023]{3,1,0,2:T(8,128)} %get-tuple-element.34, f32[1,8,128,1]{3,1,0,2:T(8,128)S(1)} %get-tuple-element.36, ...), kind=kLoop, calls=%fused_computation.9 | loop fusion | flops 18874368 | bytes 29425664 | tf_op jit(solution)/shard_map/sub | solution.py:62
  174.0 4.7 fusion.48
  178.6 4.3 fusion.50
  183.1 55.5 %collective-permute-done.10 = f32[1,8,128,1024]{3,1,0,2:T(8,128)} collective-permute-done((f32[1,8,128,1024]{3,1,0,2:T(8,128)S(1)}, f32[1,8,128,1024]{3,1,0,2:T(8,128)}, u32[]{:S(2)}, u32[]{:S(2)}) %collective-permute-start.10) | collective-permute-done | bytes 4194336 | tf_op jit(solution)/shard_map/ppermute | solution.py:24
  239.7 14.0 %multiply_reduce_fusion.1 = (f32[]{:T(128)}, f32[]{:T(128)}, f32[1,8,128,1024]{3,1,0,2:T(8,128)}, f32[1,8,128,1024]{3,1,0,2:T(8,128)}) fusion(f32[1,8,128,1024]{3,1,0,2:T(8,128)} %collective-permute-done.10, f32[1,8,128,1024]{3,1,0,2:T(8,128)} %collective-permute-done.11, f32[1,8,128,1024]{3,1,0,2:T(8,128)S(1)} %fusion.5, ...), kind=kLoop, calls=%fused_computation.49 | loop fusion | flops 18874368 | bytes 37814280 | tf_op jit(solution)/shard_map/reduce_sum | solution.py:88
  253.7 13.5 %all-reduce.1 = (f32[1]{0:T(128)}, f32[1]{0:T(128)}) all-reduce(f32[1]{0:T(128)} %bitcast.7, f32[1]{0:T(128)} %bitcast.8), channel_id=1, replica_groups=mesh['img'=16,'space'=8] {'space'}, use_global_device_ids=true, to_apply=%region_5.6 | all-reduce | flops 2 | bytes 16 | tf_op jit(solution)/shard_map/psum | solution.py:87
  268.5 8.7 %fusion.7 = f32[1,8,128,1024]{3,1,0,2:T(8,128)} fusion(f32[1,8,128,1024]{3,1,0,2:T(8,128)} %copy-done, f32[1,8,128,1024]{3,1,0,2:T(8,128)} %get-tuple-element.16, f32[1,8,128,1024]{3,1,0,2:T(8,128)} %get-tuple-element.15, f32[]{:T(128)} %bitcast.9, pred[]{:T(512)} %bitcast.2), kind=kLoop, calls=%fused_computation.11 | loop fusion | flops 5242880 | bytes 16777220 | tf_op jit(solution)/shard_map/add | solution.py:92
  277.2 6.6 %collective-permute-start.12 = (f32[1,8,128,1024]{3,1,0,2:T(8,128)}, f32[1,8,128,1024]{3,1,0,2:T(8,128)}, u32[]{:S(2)}, u32[]{:S(2)}) collective-permute-start(f32[1,8,128,1024]{3,1,0,2:T(8,128)} %fusion.7), channel_id=1, source_target_pairs={{0,8},{8,16},{16,24},{24,32},{32,40},{40,48},{48,56},{56,64},{64,7... | collective-permute-start | bytes 12582920 | tf_op jit(solution)/shard_map/ppermute | solution.py:32
  283.8 12.4 %all-to-all-start = ((f32[1,8,128,1024]{3,1,0,2:T(8,128)}), f32[1,8,128,1024]{3,1,0,2:T(8,128)}, u32[]{:S(2)}, u32[]{:S(2)}) async-start(f32[1,8,128,1024]{3,1,0,2:T(8,128)} %fusion.7), calls=%async_computation | async-start | bytes 8388608 | tf_op jit(solution)/shard_map/all_to_all | solution.py:68
  296.9 141.4 %all-to-all-done = f32[1,8,128,1024]{3,1,0,2:T(8,128)} async-done(((f32[1,8,128,1024]{3,1,0,2:T(8,128)}), f32[1,8,128,1024]{3,1,0,2:T(8,128)}, u32[]{:S(2)}, u32[]{:S(2)}) %all-to-all-start) | async-done | bytes 4194336 | tf_op jit(solution)/shard_map/all_to_all | solution.py:68
  438.3 7.7 %copy.44 = f32[1,8,16,8,1024]{4,3,1,2,0:T(8,128)} copy(f32[1,8,16,8,1024]{4,1,3,2,0:T(8,128)} %bitcast.16) | data formatting | bytes 8388608 | tf_op jit(solution)/shard_map/all_to_all | solution.py:68
  446.0 3.9 reshape.72
  449.9 5.2 multiply_reduce_fusion
  455.1 14.1 %psum.39 = f32[1]{0:T(128)} all-reduce(f32[1]{0:T(128)} %bitcast.10), channel_id=1, replica_groups=mesh['img'=16,'space'=8] {'space'}, use_global_device_ids=true, to_apply=%region_9.10 | all-reduce | flops 1 | bytes 8 | tf_op jit(solution)/shard_map/psum | solution.py:96
  470.5 6.6 %copy.35 = f32[2,8,64,1024]{3,2,1,0:T(8,128)} copy(f32[2,8,64,1024]{3,1,2,0:T(8,128)} %bitcast.43) | data formatting | bytes 8388608
  477.2 35.7 %all-reduce = f32[16]{0:T(128)S(1)} all-reduce(f32[16]{0:T(128)S(1)} %select_dynamic-update-slice_fusion), channel_id=1, replica_groups=mesh['img'=16,'space'=8] {'img'}, use_global_device_ids=true, to_apply=%add | all-reduce | flops 16 | bytes 128
  514.7 8.4 %fusion.32 = f32[16,8,8,1024]{3,0,2,1:T(8,128)S(1)} fusion(f32[8,8,1024,16]{2,1,0,3:T(8,128)} %bitcast.42, f32[16]{0:T(128)S(1)} %get-tuple-element.14, f32[16]{0:T(128)S(1)} %get-tuple-element.13, s32[16]{0:T(128)S(1)} %broadcast_add_fusion, s32[16]{0:T(128)S(1)} %convert_reduce_fusion), kind=kOutput, calls=%fused_computation.45 | convolution fusion | flops 201327872 | bytes 8388864 | tf_op jit(solution)/shard_map/dot_general | solution.py:102
  525.6 46.1 %all_to_all.33 = f32[16,8,8,1024]{3,2,1,0:T(8,128)S(1)} all-to-all(f32[16,8,8,1024]{3,2,1,0:T(8,128)S(1)} %copy.32), channel_id=1, replica_groups=mesh['img'=16,'space'=8] {'img'}, dimensions={0} | all-to-all | bytes 8388608 | tf_op jit(solution)/shard_map/all_to_all | solution.py:73
  (54 shorter events, 27.6 us)
Async XLA Ops:
  6.6 94.4 %collective-permute-start.4 = (f32[1,8,128,1024]{3,1,0,2:T(8,128)}, f32[1,8,128,1024]{3,1,0,2:T(8,128)}, u32[]{:S(2)}, u32[]{:S(2)}) collective-permute-start(f32[1,8,128,1024]{3,1,0,2:T(8,128)} %copy.28), channel_id=1, source_target_pairs={{8,0},{16,8},{24,16},{32,24},{40,32},{48,40},{56,48},{64,56},{72,6... | collective-permute-start | bytes 12582920 | tf_op jit(solution)/shard_map/ppermute | solution.py:24
  7.9 94.3 %collective-permute-start.5 = (f32[1,8,128,1024]{3,1,0,2:T(8,128)}, f32[1,8,128,1024]{3,1,0,2:T(8,128)}, u32[]{:S(2)}, u32[]{:S(2)}) collective-permute-start(f32[1,8,128,1024]{3,1,0,2:T(8,128)} %copy.28), channel_id=1, source_target_pairs={{0,8},{8,16},{16,24},{24,32},{32,40},{40,48},{48,56},{56,64},{64,7... | collective-permute-start | bytes 12582920 | tf_op jit(solution)/shard_map/ppermute | solution.py:21
  15.2 22.1 %collective-permute-start = (f32[1,8,1,1024]{3,1,0,2:T(8,128)S(1)}, f32[1,8,1,1024]{3,1,0,2:T(8,128)S(1)}, u32[]{:S(2)}, u32[]{:S(2)}) collective-permute-start(f32[1,8,1,1024]{3,1,0,2:T(8,128)S(1)} %get-tuple-element.57), channel_id=1, source_target_pairs={{1,0},{2,1},{3,2},{4,3},{5,4},{6,5},{7,6},{0,7},{9,8},{10,9},{11,1... | collective-permute-start | bytes 98312 | tf_op jit(solution)/shard_map/ppermute | solution.py:24
  16.9 20.4 %collective-permute-start.1 = (f32[1,8,1,1024]{3,1,0,2:T(8,128)S(1)}, f32[1,8,1,1024]{3,1,0,2:T(8,128)S(1)}, u32[]{:S(2)}, u32[]{:S(2)}) collective-permute-start(f32[1,8,1,1024]{3,1,0,2:T(8,128)S(1)} %get-tuple-element.58), channel_id=1, source_target_pairs={{0,1},{1,2},{2,3},{3,4},{4,5},{5,6},{6,7},{7,0},{8,9},{9,10},{10,1... | collective-permute-start | bytes 98312 | tf_op jit(solution)/shard_map/ppermute | solution.py:21
  52.3 12.8 %collective-permute-start.2 = (f32[1,8,1,1024]{3,1,0,2:T(8,128)S(1)}, f32[1,8,1,1024]{3,1,0,2:T(8,128)S(1)}, u32[]{:S(2)}, u32[]{:S(2)}) collective-permute-start(f32[1,8,1,1024]{3,1,0,2:T(8,128)S(1)} %get-tuple-element.39), channel_id=1, source_target_pairs={{1,0},{2,1},{3,2},{4,3},{5,4},{6,5},{7,6},{0,7},{9,8},{10,9},{11,1... | collective-permute-start | bytes 98312 | tf_op jit(solution)/shard_map/ppermute | solution.py:24
  55.3 9.8 %collective-permute-start.3 = (f32[1,8,1,1024]{3,1,0,2:T(8,128)S(1)}, f32[1,8,1,1024]{3,1,0,2:T(8,128)S(1)}, u32[]{:S(2)}, u32[]{:S(2)}) collective-permute-start(f32[1,8,1,1024]{3,1,0,2:T(8,128)S(1)} %get-tuple-element.40), channel_id=1, source_target_pairs={{0,1},{1,2},{2,3},{3,4},{4,5},{5,6},{6,7},{7,0},{8,9},{9,10},{10,1... | collective-permute-start | bytes 98312 | tf_op jit(solution)/shard_map/ppermute | solution.py:21
  140.0 19.0 %copy-start = (f32[1,8,128,1024]{3,1,0,2:T(8,128)}, f32[1,8,128,1024]{3,1,0,2:T(8,128)S(1)}, u32[]{:S(2)}) copy-start(f32[1,8,128,1024]{3,1,0,2:T(8,128)S(1)} %fusion.3) | copy-start | bytes 12582916
  144.6 94.0 %collective-permute-start.10 = (f32[1,8,128,1024]{3,1,0,2:T(8,128)S(1)}, f32[1,8,128,1024]{3,1,0,2:T(8,128)}, u32[]{:S(2)}, u32[]{:S(2)}) collective-permute-start(f32[1,8,128,1024]{3,1,0,2:T(8,128)S(1)} %fusion.3), channel_id=1, source_target_pairs={{8,0},{16,8},{24,16},{32,24},{40,32},{48,40},{56,48},{64,56},{72,6... | collective-permute-start | bytes 12582920 | tf_op jit(solution)/shard_map/ppermute | solution.py:24
  145.9 93.8 %collective-permute-start.11 = (f32[1,8,128,1024]{3,1,0,2:T(8,128)S(1)}, f32[1,8,128,1024]{3,1,0,2:T(8,128)}, u32[]{:S(2)}, u32[]{:S(2)}) collective-permute-start(f32[1,8,128,1024]{3,1,0,2:T(8,128)S(1)} %fusion.3), channel_id=1, source_target_pairs={{0,8},{8,16},{16,24},{24,32},{32,40},{40,48},{48,56},{56,64},{64,7... | collective-permute-start | bytes 12582920 | tf_op jit(solution)/shard_map/ppermute | solution.py:21
  152.9 6.1 %collective-permute-start.6 = (f32[1,8,1,1024]{3,1,0,2:T(8,128)S(1)}, f32[1,8,1,1024]{3,1,0,2:T(8,128)S(1)}, u32[]{:S(2)}, u32[]{:S(2)}) collective-permute-start(f32[1,8,1,1024]{3,1,0,2:T(8,128)S(1)} %get-tuple-element.37), channel_id=1, source_target_pairs={{1,0},{2,1},{3,2},{4,3},{5,4},{6,5},{7,6},{0,7},{9,8},{10,9},{11,1... | collective-permute-start | bytes 98312 | tf_op jit(solution)/shard_map/ppermute | solution.py:24
  152.9 6.2 %collective-permute-start.7 = (f32[1,8,1,1024]{3,1,0,2:T(8,128)S(1)}, f32[1,8,1,1024]{3,1,0,2:T(8,128)S(1)}, u32[]{:S(2)}, u32[]{:S(2)}) collective-permute-start(f32[1,8,1,1024]{3,1,0,2:T(8,128)S(1)} %get-tuple-element.38), channel_id=1, source_target_pairs={{0,1},{1,2},{2,3},{3,4},{4,5},{5,6},{6,7},{7,0},{8,9},{9,10},{10,1... | collective-permute-start | bytes 98312 | tf_op jit(solution)/shard_map/ppermute | solution.py:21
  170.8 12.3 %collective-permute-start.8 = (f32[1,8,1,1024]{3,1,0,2:T(8,128)S(1)}, f32[1,8,1,1024]{3,1,0,2:T(8,128)S(1)}, u32[]{:S(2)}, u32[]{:S(2)}) collective-permute-start(f32[1,8,1,1024]{3,1,0,2:T(8,128)S(1)} %get-tuple-element.19), channel_id=1, source_target_pairs={{1,0},{2,1},{3,2},{4,3},{5,4},{6,5},{7,6},{0,7},{9,8},{10,9},{11,1... | collective-permute-start | bytes 98312 | tf_op jit(solution)/shard_map/ppermute | solution.py:24
  173.3 9.8 %collective-permute-start.9 = (f32[1,8,1,1024]{3,1,0,2:T(8,128)S(1)}, f32[1,8,1,1024]{3,1,0,2:T(8,128)S(1)}, u32[]{:S(2)}, u32[]{:S(2)}) collective-permute-start(f32[1,8,1,1024]{3,1,0,2:T(8,128)S(1)} %get-tuple-element.20), channel_id=1, source_target_pairs={{0,1},{1,2},{2,3},{3,4},{4,5},{5,6},{6,7},{7,0},{8,9},{9,10},{10,1... | collective-permute-start | bytes 98312 | tf_op jit(solution)/shard_map/ppermute | solution.py:21
  277.2 19.0 %copy-start.1 = (u32[128]{0:T(128)S(1)}, u32[128]{0:T(128)}, u32[]{:S(2)}) copy-start(u32[128]{0:T(128)} %constant.44) | copy-start | bytes 1540
  277.2 172.7 %collective-permute-start.12 = (f32[1,8,128,1024]{3,1,0,2:T(8,128)}, f32[1,8,128,1024]{3,1,0,2:T(8,128)}, u32[]{:S(2)}, u32[]{:S(2)}) collective-permute-start(f32[1,8,128,1024]{3,1,0,2:T(8,128)} %fusion.7), channel_id=1, source_target_pairs={{0,8},{8,16},{16,24},{24,32},{32,40},{40,48},{48,56},{56,64},{64,7... | collective-permute-start | bytes 12582920 | tf_op jit(solution)/shard_map/ppermute | solution.py:32
  283.8 154.5 %all-to-all-start = ((f32[1,8,128,1024]{3,1,0,2:T(8,128)}), f32[1,8,128,1024]{3,1,0,2:T(8,128)}, u32[]{:S(2)}, u32[]{:S(2)}) async-start(f32[1,8,128,1024]{3,1,0,2:T(8,128)} %fusion.7), calls=%async_computation | async-start | bytes 8388608 | tf_op jit(solution)/shard_map/all_to_all | solution.py:68
where the time goes:
time: 580 us; the launch traced here: 574 us
  waiting for transfers between devices  235 us (41%)
  blocking collectives  124 us (21%)
  local copies, waits for them, and re-layouts  81.9 us (14%)
  other arithmetic  78.6 us (14%)
  starting transfers between devices  42.7 us (7%)
  matrix products  8.41 us (1%)
    all_to_all x1, waiting for transfers between devices, regroup(): lax.all_to_all(phi, 'img', split_axis=2, concat_axis=0, tiled=True)  141 us
    ppermute x6, waiting for transfers between devices, extended(): lax.ppermute(lax.slice_in_dim(block, 0, width, axis=dim), axis, backward)  91.5 us
    all_to_all x1, blocking collectives, restore(): lax.all_to_all(moved, 'img', split_axis=0, concat_axis=2, tiled=True)  46.1 us
    unnamed x1, blocking collectives  35.7 us
    reduce_sum x2, other arithmetic, per_device(): jnp.sum(diff * diff, axis=(1, 2, 3))  28.2 us
    psum x2, blocking collectives, per_device(): lax.psum((jnp.sum(diff * diff, axis=(1, 2, 3)), jnp.sum(force * diff, axi...  27.9 us
    sub x2, other arithmetic, flow_force(): own = phi * phi * phi - phi - KAPPA * laplace(ext) - tilt  26.7 us
    slice x10, local copies, waits for them, and re-layouts, laplace(): total = total + jnp.roll(core, 1, axis=-3) + jnp.roll(core, -1, axis=-3)  26 us
  transfers between devices with their start and end apart: 14, of which 5 were waited for; matrix products, arithmetic and copies ran while one was open for 15% of the time, Pallas kernels for 0%

commit v1 on v0

v1 whole, which is shorter than its diff:
```python
import functools

import jax
import jax.numpy as jnp
from jax import lax
from jax.experimental import pallas as pl
from jax.experimental.pallas import tpu as pltpu
from jax.sharding import PartitionSpec as P

DT = 0.006
EPS = 1e-06
RIM = 4
LANES = 128
GROUP = 16
VMEM_LIMIT = 48 * 1024 * 1024

vmem = pl.BlockSpec(memory_space=pltpu.VMEM)
smem = pl.BlockSpec(memory_space=pltpu.SMEM)


def lane_of(shape):
    return lax.broadcasted_iota(jnp.int32, shape, len(shape) - 1)


def strip_of(before, own, after, planes):
    shape = own(0).shape
    lane = lane_of(shape)
    strip = jnp.zeros(shape, jnp.float32)
    for p in range(planes):
        mid = own(p)
        left = pltpu.roll(jnp.where(lane >= LANES - RIM, before(p), mid), (GROUP * p + RIM) % LANES, 1)
        right = pltpu.roll(jnp.where(lane >= LANES - RIM, mid, after(p)), (GROUP * p + 3 * RIM) % LANES, 1)
        place = lane - GROUP * p
        strip = jnp.where((place >= 0) & (place < 2 * RIM), left, strip)
        strip = jnp.where((place >= 2 * RIM) & (place < 4 * RIM), right, strip)
    return strip


def pack_kernel(own_ref, low_ref, high_ref, out_ref):
    planes, rows, cols = own_ref.shape
    half = rows // 2
    blocks = cols // LANES
    for c in range(blocks):
        cut = slice(c * LANES, (c + 1) * LANES)
        for p in range(planes):
            out_ref[c, p, :RIM] = low_ref[p, -RIM:, cut]
            out_ref[c, p, RIM:] = own_ref[p, : half + RIM, cut]
            out_ref[blocks + c, p, : half + RIM] = own_ref[p, half - RIM :, cut]
            out_ref[blocks + c, p, half + RIM :] = high_ref[p, :RIM, cut]

    def strips(k, carry):
        row = (k // blocks) * blocks
        c = k % blocks
        before = row + (c + blocks - 1) % blocks
        after = row + (c + 1) % blocks
        out_ref[k, planes] = strip_of(
            lambda p: out_ref[before, p], lambda p: out_ref[k, p], lambda p: out_ref[after, p], planes
        )
        return carry

    lax.fori_loop(0, 2 * blocks, strips, 0)


def pack(own, low, high):
    planes, rows, cols = own.shape
    return pl.pallas_call(
        pack_kernel,
        out_shape=jax.ShapeDtypeStruct((2 * cols // LANES, planes + 1, rows // 2 + 2 * RIM, LANES), jnp.float32),
        in_specs=[vmem] * 3,
        out_specs=vmem,
        compiler_params=pltpu.CompilerParams(vmem_limit_bytes=VMEM_LIMIT),
        name="pack",
    )(own, low, high)


def pack_one_kernel(place_ref, own_ref, low_ref, high_ref, out_ref, near):
    planes, rows, cols = own_ref.shape
    half = rows // 2
    blocks = cols // LANES
    place = place_ref[0]
    c = place % blocks
    for at, shift in enumerate((blocks - 1, 0, 1)):
        cut = pl.ds(pl.multiple_of(((c + shift) % blocks) * LANES, LANES), LANES)

        @pl.when(place < blocks)
        def _():
            for p in range(planes):
                near[at, p, :RIM] = low_ref[p, -RIM:, cut]
                near[at, p, RIM:] = own_ref[p, : half + RIM, cut]

        @pl.when(place >= blocks)
        def _():
            for p in range(planes):
                near[at, p, : half + RIM] = own_ref[p, half - RIM :, cut]
                near[at, p, half + RIM :] = high_ref[p, :RIM, cut]

    for p in range(planes):
        out_ref[p] = near[1, p]
    out_ref[planes] = strip_of(lambda p: near[0, p], lambda p: near[1, p], lambda p: near[2, p], planes)


def pack_one(place, own, low, high):
    planes, rows, cols = own.shape
    block = (rows // 2 + 2 * RIM, LANES)
    return pl.pallas_call(
        pack_one_kernel,
        out_shape=jax.ShapeDtypeStruct((planes + 1, *block), jnp.float32),
        in_specs=[smem] + [vmem] * 3,
        out_specs=vmem,
        scratch_shapes=[pltpu.VMEM((3, planes, *block), jnp.float32)],
        compiler_params=pltpu.CompilerParams(vmem_limit_bytes=VMEM_LIMIT),
        name="pack_one",
    )(place, own, low, high)


def rows_sum(x):
    rows = x.shape[0]
    return pltpu.roll(x, 1, 0) + pltpu.roll(x, rows - 1, 0)


def laplace_strip(s):
    total = pltpu.roll(s, GROUP, 1) + pltpu.roll(s, LANES - GROUP, 1)
    total = total + pltpu.roll(s, 1, 1) + pltpu.roll(s, LANES - 1, 1)
    return total + rows_sum(s) - 6.0 * s


def laplace_plane(x, below, above, strip, p):
    lane = lane_of(x.shape)
    left = jnp.where(lane == 0, pltpu.roll(strip, (LANES - GROUP * p - (RIM - 1)) % LANES, 1), pltpu.roll(x, 1, 1))
    right = jnp.where(
        lane == LANES - 1, pltpu.roll(strip, (LANES - 1 - GROUP * p - 3 * RIM) % LANES, 1), pltpu.roll(x, LANES - 1, 1)
    )
    return (below + above) + rows_sum(x) + (left + right) - 6.0 * x


def potential(field, tilt_ref, mu):
    planes = mu.shape[0] - 1
    strip = field(planes)
    mu[planes] = strip * strip * strip - strip - laplace_strip(strip) - tilt_ref[planes]
    for p in range(planes):
        x = field(p)
        lap = laplace_plane(x, field((p - 1) % planes), field((p + 1) % planes), strip, p)
        mu[p] = x * x * x - x - lap - tilt_ref[p]


def force_plane(mu, p):
    planes = mu.shape[0] - 1
    return laplace_plane(mu[p], mu[(p - 1) % planes], mu[(p + 1) % planes], mu[planes], p)


def fold(x):
    total = x[:8]
    for at in range(8, x.shape[0], 8):
        total = total + x[at : at + 8]
    return total


def inner(shape):
    row = lax.broadcasted_iota(jnp.int32, shape, 0)
    return (row >= RIM) & (row < shape[0] - RIM)


def write_sums(acc, out_ref):
    kinds, images = acc.shape[:2]
    row = jnp.zeros((1, LANES), jnp.float32)
    lane = lane_of((images, LANES))
    image = lax.broadcasted_iota(jnp.int32, (images, LANES), 0)
    for q in range(kinds):
        part = jnp.sum(acc[q], axis=1)
        part = jnp.sum(part, axis=1, keepdims=True)
        row = row + jnp.sum(jnp.where(lane == images * q + image, part, 0.0), axis=0, keepdims=True)
    out_ref[...] = row


def first_kernel(phi_ref, tilt_ref, moved_ref, sums_ref, mu, acc):
    images, parts, rows, lanes = phi_ref.shape
    planes = parts - 1
    keep = inner((rows, lanes))

    def body(i, carry):
        after = jnp.minimum(i + 1, images - 1)
        before = jnp.maximum(i - 1, 0)
        potential(lambda p: phi_ref[i, p], tilt_ref, mu)
        moved_ref[i, planes] = phi_ref[i, planes] + DT * laplace_strip(mu[planes])
        product = jnp.zeros((8, lanes), jnp.float32)
        square = jnp.zeros((8, lanes), jnp.float32)
        for p in range(planes):
            force = force_plane(mu, p)
            moved_ref[i, p] = phi_ref[i, p] + DT * force
            diff = jnp.where(keep, phi_ref[after, p] - phi_ref[before, p], 0.0)
            product = product + fold(force * diff)
            square = square + fold(diff * diff)
        acc[0, i] = product
        acc[1, i] = square
        return carry

    lax.fori_loop(0, images, body, 0)
    write_sums(acc, sums_ref)


def first_step(phi, tilt):
    images, parts, rows, lanes = phi.shape
    return pl.pallas_call(
        first_kernel,
        out_shape=[
            jax.ShapeDtypeStruct(phi.shape, jnp.float32),
            jax.ShapeDtypeStruct((1, LANES), jnp.float32),
        ],
        in_specs=[vmem] * 2,
        out_specs=[vmem] * 2,
        scratch_shapes=[
            pltpu.VMEM((parts, rows, lanes), jnp.float32),
            pltpu.VMEM((2, images, 8, lanes), jnp.float32),
        ],
        compiler_params=pltpu.CompilerParams(vmem_limit_bytes=VMEM_LIMIT),
        name="first_step",
    )(phi, tilt)


def second_kernel(coef_ref, phi_ref, moved_ref, tilt_ref, one_ref, two_ref, sums_ref, mu, acc):
    images, parts, rows, lanes = phi_ref.shape
    planes = parts - 1
    keep = inner((rows, lanes))

    def update(i, carry):
        after = jnp.minimum(i + 1, images - 1)
        before = jnp.maximum(i - 1, 0)
        scale = DT * coef_ref[i]
        for p in range(parts):
            one_ref[i, p] = moved_ref[i, p] - scale * (phi_ref[after, p] - phi_ref[before, p])
        return carry

    lax.fori_loop(0, images, update, 0)

    def body(i, carry):
        after = jnp.minimum(i + 1, images - 1)
        before = jnp.maximum(i - 1, 0)
        earlier = jnp.maximum(i - 2, 0)
        potential(lambda p: one_ref[i, p], tilt_ref, mu)
        coef = coef_ref[i]
        sums = [jnp.zeros((8, lanes), jnp.float32)] * 6
        for p in range(planes):
            force = force_plane(mu, p)
            x = one_ref[i, p]
            low = one_ref[before, p]
            diff = jnp.where(keep, one_ref[after, p] - low, 0.0)
            diff_before = x - one_ref[earlier, p]
            two = x + DT * (force - coef * diff)
            two_ref[i, p] = two
            gap = jnp.where(keep, two - two_ref[before, p], 0.0)
            terms = (force * diff, diff * diff, gap * gap, gap * diff, gap * diff_before, diff * diff_before)
            sums = [total + fold(term) for total, term in zip(sums, terms)]
        for q in range(6):
            acc[q, i] = sums[q]
        return carry

    lax.fori_loop(0, images, body, 0)
    write_sums(acc, sums_ref)


def second_step(coef, phi, moved, tilt):
    images, parts, rows, lanes = phi.shape
    return pl.pallas_call(
        second_kernel,
        out_shape=[
            jax.ShapeDtypeStruct(phi.shape, jnp.float32),
            jax.ShapeDtypeStruct((images, parts - 1, rows, lanes), jnp.float32),
            jax.ShapeDtypeStruct((1, LANES), jnp.float32),
        ],
        in_specs=[smem] + [vmem] * 3,
        out_specs=[vmem] * 3,
        scratch_shapes=[
            pltpu.VMEM((parts, rows, lanes), jnp.float32),
            pltpu.VMEM((6, images, 8, lanes), jnp.float32),
        ],
        compiler_params=pltpu.CompilerParams(vmem_limit_bytes=VMEM_LIMIT),
        name="second_step",
    )(coef, phi, moved, tilt)


def mix_kernel(change_ref, lower_ref, share_ref, one_ref, two_ref, out_ref, final):
    images, planes, rows, lanes = two_ref.shape

    def finish(i, carry):
        after = jnp.minimum(i + 1, images - 1)
        before = jnp.maximum(i - 1, 0)
        scale = DT * change_ref[i]
        for p in range(planes):
            final[i, p] = two_ref[i, p] - scale * (one_ref[after, p] - one_ref[before, p])
        return carry

    lax.fori_loop(0, images, finish, 0)

    def body(j, carry):
        lower = lower_ref[j]
        share = share_ref[j]
        for p in range(planes):
            mixed = (1.0 - share) * final[lower, p] + share * final[lower + 1, p]
            out_ref[j, p] = mixed[RIM : rows - RIM]
        return carry

    lax.fori_loop(0, images, body, 0)


def mix(change, lower, share, one, two):
    images, planes, rows, lanes = two.shape
    return pl.pallas_call(
        mix_kernel,
        out_shape=jax.ShapeDtypeStruct((images, planes, rows - 2 * RIM, lanes), jnp.float32),
        in_specs=[smem] * 3 + [vmem] * 2,
        out_specs=vmem,
        scratch_shapes=[pltpu.VMEM(two.shape, jnp.float32)],
        compiler_params=pltpu.CompilerParams(vmem_limit_bytes=VMEM_LIMIT),
        name="mix",
    )(change, lower, share, one, two)


def spacing(dist):
    count = dist.shape[0]
    arc = jnp.cumsum(dist)
    target = jnp.arange(count).astype(dist.dtype) * (arc[count - 1] / (count - 1))
    slots = jnp.arange(count, dtype=jnp.int32)
    inside = (
        (slots[None, :] >= 1) & (slots[None, :] <= count - 2) & (arc[None, :] <= target[:, None])
    )
    lower = jnp.sum(inside.astype(jnp.int32), axis=1)
    pick_low = (slots[None, :] == lower[:, None]).astype(dist.dtype)
    pick_high = (slots[None, :] == lower[:, None] + 1).astype(dist.dtype)
    start = jnp.sum(pick_low * arc[None, :], axis=1)
    length = jnp.sum(pick_high * dist[None, :], axis=1)
    return lower, (target - start) / length


def total_over_all(row, axes):
    count = lax.axis_size(axes)
    spread = jnp.broadcast_to(row[None], (count, *row.shape))
    gathered = lax.all_to_all(spread, axes, split_axis=0, concat_axis=0, tiled=True)
    return jnp.sum(gathered, axis=(0, 1))


def rim_rows(block, axis):
    count = lax.axis_size(axis)
    ahead = [(i, (i + 1) % count) for i in range(count)]
    back = [(target, source) for source, target in ahead]
    return lax.ppermute(block[..., -8:, :], axis, ahead), lax.ppermute(block[..., :8, :], axis, back)


def per_device(axes, path, tilt):
    images = lax.axis_size("img")
    slot = jnp.arange(images)
    interior = (slot > 0) & (slot < images - 1)
    low, high = rim_rows(path[0], "space")
    tilt_low, tilt_high = rim_rows(tilt, "space")
    place = lax.axis_index("img").astype(jnp.int32)[None]
    packed = pack(path[0], low, high)
    tilt_block = pack_one(place, tilt, tilt_low, tilt_high)
    phi = lax.all_to_all(packed, "img", split_axis=0, concat_axis=0, tiled=True)
    moved, sums = first_step(phi, tilt_block)
    sums = total_over_all(sums, axes)
    coef = jnp.where(interior, sums[:images] / (sums[images : 2 * images] + EPS), 0.0)
    one, two, sums = second_step(coef, phi, moved, tilt_block)
    sums = total_over_all(sums, axes)[: 6 * images].reshape(6, images)
    products, squares, gaps, gap_diff, gap_before, diff_before = sums
    change = jnp.where(interior, products / (squares + EPS) - coef, 0.0)
    change_before = jnp.concatenate([jnp.zeros((1,), jnp.float32), change[:-1]])
    squares_before = jnp.concatenate([jnp.zeros((1,), jnp.float32), squares[:-1]])
    cross = change * gap_diff - change_before * gap_before
    tangent = change * change * squares + change_before * change_before * squares_before
    tangent = tangent - 2.0 * change * change_before * diff_before
    length = jnp.maximum(gaps - 2.0 * DT * cross + DT * DT * tangent, 0.0)
    dist = jnp.where(slot > 0, jnp.sqrt(length + EPS), 0.0)
    lower, share = spacing(dist)
    mixed = mix(change, lower, share, one, two)
    back = lax.all_to_all(mixed, "img", split_axis=0, concat_axis=0, tiled=True)
    count, planes, rows, lanes = back.shape
    back = back.reshape(2, count // 2, planes, rows, lanes).transpose(2, 0, 3, 1, 4)
    return back.reshape(1, planes, 2 * rows, count // 2 * lanes)


def solution(mesh):
    return jax.shard_map(
        functools.partial(per_device, tuple(mesh.axis_names)),
        mesh=mesh,
        in_specs=(P("img", None, "space", None), P(None, "space", None)),
        out_specs=P("img", None, "space", None),
        check_vma=False,
    )
```

time: 580 us -> 251 us (0.43)
  waiting for transfers between devices: 235 us -> 86.9 us
  other arithmetic: 78.6 us -> 0.86 us
  local copies, waits for them, and re-layouts: 81.9 us -> 22.5 us
  blocking collectives: 124 us -> 70.8 us
  Pallas kernels: 0 us -> 49.5 us
  starting transfers between devices: 42.7 us -> 18.9 us
  matrix products: 8.41 us -> 0 us
    ppermute x13 -> x4, waiting for transfers between devices: 93.8 us -> 8.11 us  [the longest x2 8.1 us: rim_rows(): lax.ppermute(block[..., -8:, :], axis, ahead)]
    all_to_all x1 -> x2, waiting for transfers between devices: 141 us -> 78.8 us  [the longest x1 69.6 us: per_device(): phi = lax.all_to_all(packed, 'img', split_axis=0, concat_axis=0, tiled=True)]
    pallas_call x0 -> x5, Pallas kernels: none -> 49.5 us  [the longest x1 21.1 us: second_step(): pl.pallas_call(second_kernel, out_shape=[jax.ShapeDtypeStruct(phi.shape,...]
    slice x22 -> x3, local copies, waits for them, and re-layouts: 50.9 us -> 2.2 us  [the longest x2 2.13 us: rim_rows(): block[..., :8, :]]
    psum x3 -> x0, blocking collectives: 42 us -> none  [the longest x2 27.9 us: per_device(): lax.psum((jnp.sum(diff * diff, axis=(1, 2, 3)), jnp.sum(force * diff, axi...]
    unnamed x1 -> x0, blocking collectives: 35.7 us -> none
    reduce_sum x3 -> x2, other arithmetic: 33.3 us -> 0.06 us  [total_over_all(): return jnp.sum(gathered, axis=(0, 1))]
    sub x3 -> x0, other arithmetic: 26.7 us -> none  [the longest x2 26.7 us: flow_force(): own = phi * phi * phi - phi - KAPPA * laplace(ext) - tilt]
  transfers between devices with their start and end apart: 14 -> 6, of which waited for: 5 -> 4; matrix products, arithmetic and copies ran while one was open for 15% -> 0% of each run, Pallas kernels for 0% -> 0%
where the time goes in v1:
time: 251 us; the launch traced here: 250 us
  waiting for transfers between devices  86.9 us (35%)
  blocking collectives  70.8 us (28%)
  Pallas kernels  49.5 us (20%)
  local copies, waits for them, and re-layouts  22.5 us (9%)
  starting transfers between devices  18.9 us (8%)
    all_to_all x1, waiting for transfers between devices, per_device(): phi = lax.all_to_all(packed, 'img', split_axis=0, concat_axis=0, tiled=True)  69.6 us
    all_to_all x1, blocking collectives, per_device(): back = lax.all_to_all(mixed, 'img', split_axis=0, concat_axis=0, tiled=True)  53.8 us
    pallas_call x1, Pallas kernels, second_step(): pl.pallas_call(second_kernel, out_shape=[jax.ShapeDtypeStruct(phi.shape,...  21.1 us
    all_to_all x1, blocking collectives, total_over_all(): lax.all_to_all(spread, axes, split_axis=0, concat_axis=0, tiled=True)  17.1 us
    pallas_call x1, Pallas kernels, first_step(): pl.pallas_call(first_kernel, out_shape=[jax.ShapeDtypeStruct(phi.shape, j...  15.8 us
    all_to_all x1, waiting for transfers between devices, total_over_all(): lax.all_to_all(spread, axes, split_axis=0, concat_axis=0, tiled=True)  9.21 us
    unnamed x8, local copies, waits for them, and re-layouts  8.88 us
    all_to_all x1, starting transfers between devices, per_device(): phi = lax.all_to_all(packed, 'img', split_axis=0, concat_axis=0, tiled=True)  8.21 us
  transfers between devices with their start and end apart: 6, of which 4 were waited for; matrix products, arithmetic and copies ran while one was open for 0% of the time, Pallas kernels for 0%

profile of v1, /device:TPU:0, one launch (start us, length us, event | category | flops | bytes accessed | tf_op | source)
XLA Modules:
  0.0 250.3 jit_solution(3945765225703699216)
XLA Ops:
  0.0 1.1 fusion.3
  1.1 2.9 %collective-permute-start.1 = (f32[8,8,1024]{2,1,0:T(8,128)S(1)}, f32[8,8,1024]{2,1,0:T(8,128)S(1)}, u32[]{:S(2)}, u32[]{:S(2)}) collective-permute-start(f32[8,8,1024]{2,1,0:T(8,128)S(1)} %get-tuple-element.17), channel_id=1, source_target_pairs={{1,0},{2,1},{3,2},{4,3},{5,4},{6,5},{7,6},{0,7},{9,8},{10,9},{11,1... | collective-permute-start | bytes 786440 | tf_op jit(solution)/shard_map/ppermute | solution.py:345
  4.0 4.1 %collective-permute-done.low_ref = f32[8,8,1024]{2,1,0:T(8,128)S(1)} collective-permute-done((f32[8,8,1024]{2,1,0:T(8,128)S(1)}, f32[8,8,1024]{2,1,0:T(8,128)S(1)}, u32[]{:S(2)}, u32[]{:S(2)}) %collective-permute-start) | collective-permute-done | bytes 262176 | tf_op jit(solution)/shard_map/ppermute | solution.py:345
  8.1 2.2 copy-done.1
  10.3 6.6 %pack.1 = f32[16,9,72,128]{3,2,1,0:T(8,128)} custom-call(f32[8,128,1024]{2,1,0:T(8,128)S(1)} %bitcast.15, f32[8,8,1024]{2,1,0:T(8,128)S(1)} %collective-permute-done.low_ref, f32[8,8,1024]{2,1,0:T(8,128)S(1)} %collective-permute-done.1.high_ref), custom_call_target="tpu_custom_call" | custom-call | tf_op jit(solution)/shard_map/pack/pallas_call | solution.py:66
  16.9 8.2 %all-to-all-start = ((f32[16,9,72,128]{3,2,1,0:T(8,128)}), f32[16,9,72,128]{3,2,1,0:T(8,128)}, u32[]{:S(2)}, u32[]{:S(2)}) async-start(f32[16,9,72,128]{3,2,1,0:T(8,128)} %pack.1), calls=%async_computation | async-start | bytes 10616832 | tf_op jit(solution)/shard_map/all_to_all | solution.py:357
  25.1 1.1 fusion.2
  26.2 0.1 collective-permute-start.2
  26.3 2.9 %collective-permute-start.3 = (f32[8,8,1024]{2,1,0:T(8,128)S(1)}, f32[8,8,1024]{2,1,0:T(8,128)S(1)}, u32[]{:S(2)}, u32[]{:S(2)}) collective-permute-start(f32[8,8,1024]{2,1,0:T(8,128)S(1)} %get-tuple-element.15), channel_id=1, source_target_pairs={{1,0},{2,1},{3,2},{4,3},{5,4},{6,5},{7,6},{0,7},{9,8},{10,9},{11,1... | collective-permute-start | bytes 786440 | tf_op jit(solution)/shard_map/ppermute | solution.py:345
  29.2 4.1 %collective-permute-done.2.low_ref = f32[8,8,1024]{2,1,0:T(8,128)S(1)} collective-permute-done((f32[8,8,1024]{2,1,0:T(8,128)S(1)}, f32[8,8,1024]{2,1,0:T(8,128)S(1)}, u32[]{:S(2)}, u32[]{:S(2)}) %collective-permute-start.2) | collective-permute-done | bytes 262176 | tf_op jit(solution)/shard_map/ppermute | solution.py:345
  33.2 2.2 copy-done.2
  35.4 0.4 pack_one.1.tilt_ref
  35.8 69.6 %all-to-all-done.phi_ref = f32[16,9,72,128]{3,2,1,0:T(8,128)} async-done(((f32[16,9,72,128]{3,2,1,0:T(8,128)}), f32[16,9,72,128]{3,2,1,0:T(8,128)}, u32[]{:S(2)}, u32[]{:S(2)}) %all-to-all-start) | async-done | bytes 5308448 | tf_op jit(solution)/shard_map/all_to_all | solution.py:357
  105.4 15.8 %first_step.1 = (f32[16,9,72,128]{3,2,1,0:T(8,128)S(1)}, f32[1,128]{1,0:T(1,128)S(1)}) custom-call(f32[16,9,72,128]{3,2,1,0:T(8,128)} %all-to-all-done.phi_ref, f32[9,72,128]{2,1,0:T(8,128)S(1)} %pack_one.1.tilt_ref), custom_call_target="tpu_custom_call" | custom-call | tf_op jit(solution)/shard_map/first_step/pallas_call | solution.py:203
  121.2 2.4 copy-done
  123.7 17.1 %all_to_all.20 = f32[128,1,128]{2,1,0:T(1,128)S(1)} all-to-all(f32[128,1,128]{2,1,0:T(1,128)S(1)} %broadcast_in_dim.18), channel_id=1, replica_groups=mesh['img'=16,'space'=8] {'img','space'}, dimensions={0} | all-to-all | bytes 131072 | tf_op jit(solution)/shard_map/all_to_all | solution.py:337
  140.9 21.1 %second_step.1 = (f32[16,9,72,128]{3,2,1,0:T(8,128)}, f32[16,8,72,128]{3,2,1,0:T(8,128)S(1)}, f32[1,128]{1,0:T(1,128)S(1)}) custom-call(f32[16]{0:T(128)S(1)} %divide_select_fusion.coef_ref, f32[16,9,72,128]{3,2,1,0:T(8,128)} %all-to-all-done.phi_ref, f32[16,9,72,128]{3,2,1,0:T(8,128)} %copy-done, f32[9,72,128]{2,1,0:T(8,128)S(1)} %pack_one.1.tilt_ref), custom_call_target="tpu_custom_call" | custom-call | tf_op jit(solution)/shard_map/second_step/pallas_call | solution.py:263
  162.0 2.1 copy-done.3
  164.1 0.7 broadcast_in_dim.40
  164.7 4.8 %all-to-all-start.2 = ((f32[128,1,128]{2,1,0:T(1,128)}), f32[128,1,128]{2,1,0:T(1,128)S(1)}, u32[]{:S(2)}, u32[]{:S(2)}) async-start(f32[128,1,128]{2,1,0:T(1,128)} %broadcast_in_dim.40), calls=%async_computation.2 | async-start | bytes 131072 | tf_op jit(solution)/shard_map/all_to_all | solution.py:337
  169.6 9.2 %all-to-all-done.2 = f32[128,1,128]{2,1,0:T(1,128)S(1)} async-done(((f32[128,1,128]{2,1,0:T(1,128)}), f32[128,1,128]{2,1,0:T(1,128)S(1)}, u32[]{:S(2)}, u32[]{:S(2)}) %all-to-all-start.2) | async-done | bytes 65568 | tf_op jit(solution)/shard_map/all_to_all | solution.py:337
  178.8 0.1 subtract_select_fusion.change_ref
  179.0 0.1 compare_select_fusion
  179.1 0.1 copy.11
  179.2 0.5 slice.53
  180.4 0.1 reduce
  180.5 0.2 convert_reduce_fusion.lower_ref
  180.7 0.2 select_reduce_fusion
  180.9 5.5 %mix.1 = f32[16,8,64,128]{3,2,1,0:T(8,128)S(1)} custom-call(f32[16]{0:T(128)S(1)} %subtract_select_fusion.change_ref, s32[16]{0:T(128)S(1)} %convert_reduce_fusion.lower_ref, f32[16]{0:T(128)S(1)} %subtract_divide_fusion.share_ref, f32[16,9,72,128]{3,2,1,0:T(8,128)} %get-tuple-element.13.one_ref, f32[16,8,72,128]{3,2,1,0:T(8,128)} %copy-done.3), custom_call_target="tpu_custom_call" | custom-call | tf_op jit(solution)/shard_map/mix/pallas_call | solution.py:307
  186.4 53.8 %all_to_all.21 = f32[16,8,64,128]{3,2,1,0:T(8,128)S(1)} all-to-all(f32[16,8,64,128]{3,2,1,0:T(8,128)S(1)} %mix.1), channel_id=1, replica_groups=mesh['img'=16,'space'=8] {'img'}, dimensions={0} | all-to-all | bytes 8388608 | tf_op jit(solution)/shard_map/all_to_all | solution.py:374
  240.2 5.2 %copy.12 = f32[8,2,64,8,128]{4,3,2,1,0:T(8,128)} copy(f32[8,2,64,8,128]{4,2,0,3,1:T(8,128)S(1)} %bitcast.19) | data formatting | bytes 8388608 | tf_op jit(solution)/shard_map/transpose | solution.py:376
  245.4 4.9 %reshape.59 = f32[1,8,128,1024]{3,2,1,0:T(8,128)} reshape(f32[8,2,64,8,128]{4,3,2,1,0:T(8,128)} %copy.12) | data formatting | bytes 8388608 | tf_op jit(solution)/shard_map/reshape | solution.py:377
  (17 shorter events, 0.3 us)
Async XLA Ops:
  1.1 7.0 %collective-permute-start = (f32[8,8,1024]{2,1,0:T(8,128)S(1)}, f32[8,8,1024]{2,1,0:T(8,128)S(1)}, u32[]{:S(2)}, u32[]{:S(2)}) collective-permute-start(f32[8,8,1024]{2,1,0:T(8,128)S(1)} %get-tuple-element.18), channel_id=1, source_target_pairs={{0,1},{1,2},{2,3},{3,4},{4,5},{5,6},{6,7},{7,0},{8,9},{9,10},{10,1... | collective-permute-start | bytes 786440 | tf_op jit(solution)/shard_map/ppermute | solution.py:345
  1.1 7.0 %collective-permute-start.1 = (f32[8,8,1024]{2,1,0:T(8,128)S(1)}, f32[8,8,1024]{2,1,0:T(8,128)S(1)}, u32[]{:S(2)}, u32[]{:S(2)}) collective-permute-start(f32[8,8,1024]{2,1,0:T(8,128)S(1)} %get-tuple-element.17), channel_id=1, source_target_pairs={{1,0},{2,1},{3,2},{4,3},{5,4},{6,5},{7,6},{0,7},{9,8},{10,9},{11,1... | collective-permute-start | bytes 786440 | tf_op jit(solution)/shard_map/ppermute | solution.py:345
  8.1 2.2 copy-start.1
  16.9 88.5 %all-to-all-start = ((f32[16,9,72,128]{3,2,1,0:T(8,128)}), f32[16,9,72,128]{3,2,1,0:T(8,128)}, u32[]{:S(2)}, u32[]{:S(2)}) async-start(f32[16,9,72,128]{3,2,1,0:T(8,128)} %pack.1), calls=%async_computation | async-start | bytes 10616832 | tf_op jit(solution)/shard_map/all_to_all | solution.py:357
  26.2 7.0 %collective-permute-start.2 = (f32[8,8,1024]{2,1,0:T(8,128)S(1)}, f32[8,8,1024]{2,1,0:T(8,128)S(1)}, u32[]{:S(2)}, u32[]{:S(2)}) collective-permute-start(f32[8,8,1024]{2,1,0:T(8,128)S(1)} %get-tuple-element.16), channel_id=1, source_target_pairs={{0,1},{1,2},{2,3},{3,4},{4,5},{5,6},{6,7},{7,0},{8,9},{9,10},{10,1... | collective-permute-start | bytes 786440 | tf_op jit(solution)/shard_map/ppermute | solution.py:345
  26.3 6.9 %collective-permute-start.3 = (f32[8,8,1024]{2,1,0:T(8,128)S(1)}, f32[8,8,1024]{2,1,0:T(8,128)S(1)}, u32[]{:S(2)}, u32[]{:S(2)}) collective-permute-start(f32[8,8,1024]{2,1,0:T(8,128)S(1)} %get-tuple-element.15), channel_id=1, source_target_pairs={{1,0},{2,1},{3,2},{4,3},{5,4},{6,5},{7,6},{0,7},{9,8},{10,9},{11,1... | collective-permute-start | bytes 786440 | tf_op jit(solution)/shard_map/ppermute | solution.py:345
  33.2 2.2 copy-start.2
  121.2 2.4 copy-start
  162.0 2.1 copy-start.3
  164.7 14.0 %all-to-all-start.2 = ((f32[128,1,128]{2,1,0:T(1,128)}), f32[128,1,128]{2,1,0:T(1,128)S(1)}, u32[]{:S(2)}, u32[]{:S(2)}) async-start(f32[128,1,128]{2,1,0:T(1,128)} %broadcast_in_dim.40), calls=%async_computation.2 | async-start | bytes 131072 | tf_op jit(solution)/shard_map/all_to_all | solution.py:337

commit v2 on v1

v2 whole, which is shorter than its diff:
```python
import functools

import jax
import jax.numpy as jnp
from jax import lax
from jax.experimental import pallas as pl
from jax.experimental.pallas import tpu as pltpu
from jax.sharding import PartitionSpec as P

DT = 0.006
EPS = 1e-06
RIM = 4
TILE = 8
LANES = 128
GROUP = 16
MIB = 1024 * 1024

vmem = pl.BlockSpec(memory_space=pltpu.VMEM)
smem = pl.BlockSpec(memory_space=pltpu.SMEM)
anywhere = pl.BlockSpec(memory_space=pl.ANY)


def lane_of(shape):
    return lax.broadcasted_iota(jnp.int32, shape, len(shape) - 1)


def row_of(shape):
    return lax.broadcasted_iota(jnp.int32, shape, len(shape) - 2)


def edges(tile, p, total):
    place = lane_of(tile.shape) - GROUP * p
    moved = pltpu.roll(tile, GROUP * p + RIM, 1)
    return jnp.where((place >= 0) & (place < 2 * RIM), moved, total)


def strip_of(before, own, after):
    lane = lane_of(own.shape)
    k = lane % GROUP
    left = jnp.where(k < RIM, before, own)
    right = jnp.where(k < RIM, own, after)
    both = jnp.where(k < 2 * RIM, left, pltpu.roll(right, 2 * RIM, 1))
    group = lane - k
    odd = jnp.where(k < 13, group + 8 + (k + 3) // 2, (group + GROUP) % LANES + 8 + (k - 13) // 2)
    source = jnp.where(k % 2 == 0, group + k // 2, odd)
    return jnp.take_along_axis(both, source, axis=1, mode="promise_in_bounds")


def pack_kernel(path_ref, out_ref, held, edge, strips, load_sem, core_sem, strip_sem):
    planes, rows, cols = path_ref.shape
    half = rows // 2
    blocks = cols // LANES
    loads = [pltpu.make_async_copy(path_ref.at[p], held.at[p], load_sem.at[p]) for p in range(planes)]
    for copy in loads:
        copy.start()
    cores = []
    for k in range(2 * blocks):
        r, c = divmod(k, blocks)
        piece = path_ref.at[:, pl.ds(r * half, half), pl.ds(c * LANES, LANES)]
        cores.append(pltpu.make_async_copy(piece, out_ref.at[k, pl.ds(0, planes), pl.ds(0, half)], core_sem.at[k]))
    for copy in cores:
        copy.start()
    for p in range(planes):
        loads[p].wait()
        for c in range(blocks):
            tile = held[p, :, c * LANES : (c + 1) * LANES]
            edge[c] = edges(tile, p, jnp.zeros_like(tile) if p == 0 else edge[c])
    for c in range(blocks):
        strip = strip_of(edge[(c - 1) % blocks], edge[c], edge[(c + 1) % blocks])
        strips[c] = strip[:half]
        strips[blocks + c] = strip[half:]
    copy = pltpu.make_async_copy(strips, out_ref.at[:, planes, pl.ds(0, half)], strip_sem)
    copy.start()
    copy.wait()
    for copy in cores:
        copy.wait()


def pack(path):
    planes, rows, cols = path.shape
    count, half = 2 * cols // LANES, rows // 2
    return pl.pallas_call(
        pack_kernel,
        out_shape=jax.ShapeDtypeStruct((count, planes + 1, half + TILE, LANES), jnp.float32),
        in_specs=[anywhere],
        out_specs=anywhere,
        scratch_shapes=[
            pltpu.VMEM((planes, rows, cols), jnp.float32),
            pltpu.VMEM((count // 2, rows, LANES), jnp.float32),
            pltpu.VMEM((count, half, LANES), jnp.float32),
            pltpu.SemaphoreType.DMA((planes,)),
            pltpu.SemaphoreType.DMA((count,)),
            pltpu.SemaphoreType.DMA,
        ],
        compiler_params=pltpu.CompilerParams(vmem_limit_bytes=12 * MIB),
        cost_estimate=pl.CostEstimate(flops=10_000_000, bytes_accessed=16 * MIB, transcendentals=0),
        name="pack",
    )(path)


def rims_kernel(
    place_ref, path_ref, above_ref, below_ref, tilt_ref, packed_ref, out_ref, tilt_out, own, rims, core, side, edge, sem, out_sem
):
    planes, rows, cols = path_ref.shape
    half = rows // 2
    blocks = cols // LANES
    place = place_ref[0]
    c = place % blocks
    upper = place < blocks
    start = pl.multiple_of((place // blocks) * half, half)
    beside = pl.multiple_of(half - TILE * (place // blocks), TILE)
    middle = path_ref.at[:, pl.ds(half - TILE, 2 * TILE)]
    loads = [
        pltpu.make_async_copy(middle, own.at[:, pl.ds(0, 2 * TILE)], sem.at[0]),
        pltpu.make_async_copy(above_ref.at[0], own.at[:, pl.ds(2 * TILE, TILE)], sem.at[1]),
        pltpu.make_async_copy(below_ref.at[0], own.at[:, pl.ds(3 * TILE, TILE)], sem.at[2]),
    ]
    for at, shift in enumerate((blocks - 1, 0, 1)):
        cut = pl.ds(pl.multiple_of(((c + shift) % blocks) * LANES, LANES), LANES)
        pieces = (
            (tilt_ref.at[:, pl.ds(start, half), cut], core.at[at]),
            (tilt_ref.at[:, pl.ds(beside, TILE), cut], side.at[at, 0]),
            (above_ref.at[1, :, :, cut], side.at[at, 1]),
            (below_ref.at[1, :, :, cut], side.at[at, 2]),
        )
        for k, (source, target) in enumerate(pieces):
            loads.append(pltpu.make_async_copy(source, target, sem.at[3 + 4 * at + k]))
    for copy in loads:
        copy.start()
    for copy in loads:
        copy.wait()
    under = row_of((TILE, LANES)) < RIM
    for r in range(2):
        for b in range(blocks):
            cut = slice(b * LANES, (b + 1) * LANES)
            total = jnp.zeros((TILE, LANES), jnp.float32)
            for p in range(planes):
                if r == 0:
                    tile = jnp.where(under, own[p, TILE : 2 * TILE, cut], own[p, 2 * TILE : 3 * TILE, cut])
                else:
                    tile = jnp.where(under, own[p, 3 * TILE :, cut], own[p, :TILE, cut])
                rims[r * blocks + b, p] = tile
                total = edges(tile, p, total)
            edge[pl.ds(b * TILE, TILE)] = total
        for b in range(blocks):
            tiles = [edge[pl.ds(((b + shift) % blocks) * TILE, TILE)] for shift in (-1, 0, 1)]
            rims[r * blocks + b, planes] = strip_of(*tiles)
    out = pltpu.make_async_copy(rims, out_ref.at[:, :, pl.ds(half, TILE)], out_sem)
    out.start()
    sums = []
    for at in range(3):
        total = jnp.zeros((half + TILE, LANES), jnp.float32)
        for p in range(planes):
            next_to = jnp.where(upper, side[at, 0, p], side[at, 2, p])
            last = jnp.where(upper, side[at, 1, p], side[at, 0, p])
            rim = jnp.where(under, next_to, last)
            full = jnp.concatenate([core[at, p], rim], axis=0)
            if at == 1:
                tilt_out[p] = full
            total = edges(full, p, total)
        sums.append(total)
    tilt_out[planes] = strip_of(*sums)
    out.wait()


def rims(place, path, above, below, tilt, packed):
    planes, rows, cols = path.shape
    count, half = 2 * cols // LANES, rows // 2
    return pl.pallas_call(
        rims_kernel,
        out_shape=[
            jax.ShapeDtypeStruct(packed.shape, jnp.float32),
            jax.ShapeDtypeStruct((planes + 1, half + TILE, LANES), jnp.float32),
        ],
        in_specs=[smem] + [anywhere] * 5,
        out_specs=[anywhere, vmem],
        input_output_aliases={5: 0},
        scratch_shapes=[
            pltpu.VMEM((planes, 4 * TILE, cols), jnp.float32),
            pltpu.VMEM((count, planes + 1, TILE, LANES), jnp.float32),
            pltpu.VMEM((3, planes, half, LANES), jnp.float32),
            pltpu.VMEM((3, 3, planes, TILE, LANES), jnp.float32),
            pltpu.VMEM((cols // LANES * TILE, LANES), jnp.float32),
            pltpu.SemaphoreType.DMA((15,)),
            pltpu.SemaphoreType.DMA,
        ],
        compiler_params=pltpu.CompilerParams(vmem_limit_bytes=8 * MIB),
        cost_estimate=pl.CostEstimate(flops=1_000_000, bytes_accessed=4 * MIB, transcendentals=0),
        name="rims",
    )(place, path, above, below, tilt, packed)


def rows_sum(x):
    return pltpu.roll(x, 1, 0) + pltpu.roll(x, x.shape[0] - 1, 0)


def laplace_strip(s):
    total = pltpu.roll(s, GROUP, 1) + pltpu.roll(s, LANES - GROUP, 1)
    total = total + pltpu.roll(s, 2, 1) + pltpu.roll(s, LANES - 2, 1)
    return total + rows_sum(s) - 6.0 * s


def laplace_plane(x, below, above, strip, p):
    lane = lane_of(x.shape)
    beside = pltpu.roll(strip, (LANES - GROUP * p - 6) % LANES, 1)
    left = jnp.where(lane == 0, beside, pltpu.roll(x, 1, 1))
    right = jnp.where(lane == LANES - 1, beside, pltpu.roll(x, LANES - 1, 1))
    return (below + above) + rows_sum(x) + (left + right) - 6.0 * x


def potential(field, tilt_ref, mu):
    planes = mu.shape[0] - 1
    strip = field(planes)
    mu[planes] = strip * strip * strip - strip - laplace_strip(strip) - tilt_ref[planes]
    for p in range(planes):
        x = field(p)
        lap = laplace_plane(x, field((p - 1) % planes), field((p + 1) % planes), strip, p)
        mu[p] = x * x * x - x - lap - tilt_ref[p]


def force_plane(mu, p):
    planes = mu.shape[0] - 1
    return laplace_plane(mu[p], mu[(p - 1) % planes], mu[(p + 1) % planes], mu[planes], p)


def fold(x):
    total = x[:TILE]
    for at in range(TILE, x.shape[0], TILE):
        total = total + x[at : at + TILE]
    return total


def write_sums(acc, out_ref):
    kinds, images = acc.shape[:2]
    row = jnp.zeros((1, LANES), jnp.float32)
    lane = lane_of((images, LANES))
    image = row_of((images, LANES))
    for q in range(kinds):
        part = jnp.sum(acc[q], axis=1)
        part = jnp.sum(part, axis=1, keepdims=True)
        row = row + jnp.sum(jnp.where(lane == images * q + image, part, 0.0), axis=0, keepdims=True)
    out_ref[...] = jnp.broadcast_to(row[None], out_ref.shape)


def read_sums(sums_ref):
    parts = [sums_ref[k] for k in range(TILE)]
    for k in range(TILE, sums_ref.shape[0]):
        parts[k % TILE] = parts[k % TILE] + sums_ref[k]
    while len(parts) > 1:
        parts = [a + b for a, b in zip(parts[::2], parts[1::2], strict=True)]
    return parts[0]


def spread(row, images):
    shape = (images, LANES)
    picked = jnp.where(lane_of(shape) == row_of(shape), row, 0.0)
    return jnp.broadcast_to(jnp.sum(picked, axis=1, keepdims=True), shape)


def tangent_share(row, images):
    lane = lane_of(row.shape)
    coef = row / (pltpu.roll(row, LANES - images, 1) + EPS)
    return jnp.where((lane > 0) & (lane < images - 1), coef, 0.0)


def first_kernel(phi_ref, tilt_ref, moved_ref, sums_ref, mu, acc):
    images, parts, rows, lanes = phi_ref.shape
    planes = parts - 1
    core = rows - TILE

    def body(i, carry):
        after = jnp.minimum(i + 1, images - 1)
        before = jnp.maximum(i - 1, 0)
        potential(lambda p: phi_ref[i, p], tilt_ref, mu)
        moved_ref[i, planes] = phi_ref[i, planes] + DT * laplace_strip(mu[planes])
        product = jnp.zeros((TILE, lanes), jnp.float32)
        square = jnp.zeros((TILE, lanes), jnp.float32)
        for p in range(planes):
            force = force_plane(mu, p)
            moved_ref[i, p] = phi_ref[i, p] + DT * force
            diff = phi_ref[after, p, :core] - phi_ref[before, p, :core]
            product = product + fold(force[:core] * diff)
            square = square + fold(diff * diff)
        acc[0, i] = product
        acc[1, i] = square
        return carry

    lax.fori_loop(0, images, body, 0)
    write_sums(acc, sums_ref)


def first_step(phi, tilt, devices):
    images, parts, rows, lanes = phi.shape
    return pl.pallas_call(
        first_kernel,
        out_shape=[
            jax.ShapeDtypeStruct(phi.shape, jnp.float32),
            jax.ShapeDtypeStruct((devices, 1, LANES), jnp.float32),
        ],
        in_specs=[vmem] * 2,
        out_specs=[vmem] * 2,
        scratch_shapes=[
            pltpu.VMEM((parts, rows, lanes), jnp.float32),
            pltpu.VMEM((2, images, TILE, lanes), jnp.float32),
        ],
        compiler_params=pltpu.CompilerParams(vmem_limit_bytes=16 * MIB),
        name="first_step",
    )(phi, tilt)


def second_kernel(given_ref, phi_ref, moved_ref, tilt_ref, one_ref, two_ref, coef_ref, sums_ref, mu, acc, coefs):
    images, parts, rows, lanes = phi_ref.shape
    planes = parts - 1
    core = rows - TILE
    coef_row = tangent_share(read_sums(given_ref), images)
    coef_ref[...] = coef_row
    coefs[...] = spread(coef_row, images)

    def update(i, carry):
        after = jnp.minimum(i + 1, images - 1)
        before = jnp.maximum(i - 1, 0)
        scale = DT * coefs[pl.ds(i, 1)]
        for p in range(parts):
            one_ref[i, p] = moved_ref[i, p] - scale * (phi_ref[after, p] - phi_ref[before, p])
        return carry

    lax.fori_loop(0, images, update, 0)

    def body(i, carry):
        after = jnp.minimum(i + 1, images - 1)
        before = jnp.maximum(i - 1, 0)
        earlier = jnp.maximum(i - 2, 0)
        potential(lambda p: one_ref[i, p], tilt_ref, mu)
        coef = coefs[pl.ds(i, 1)]
        sums = [jnp.zeros((TILE, lanes), jnp.float32)] * 6
        for p in range(planes):
            force = force_plane(mu, p)[:core]
            x = one_ref[i, p, :core]
            diff = one_ref[after, p, :core] - one_ref[before, p, :core]
            diff_before = x - one_ref[earlier, p, :core]
            two = x + DT * (force - coef * diff)
            two_ref[i, p] = two
            gap = two - two_ref[before, p]
            terms = (force * diff, diff * diff, gap * gap, gap * diff, gap * diff_before, diff * diff_before)
            sums = [total + fold(term) for total, term in zip(sums, terms, strict=True)]
        for q in range(6):
            acc[q, i] = sums[q]
        return carry

    lax.fori_loop(0, images, body, 0)
    write_sums(acc, sums_ref)


def second_step(given, phi, moved, tilt):
    images, parts, rows, lanes = phi.shape
    return pl.pallas_call(
        second_kernel,
        out_shape=[
            jax.ShapeDtypeStruct(phi.shape, jnp.float32),
            jax.ShapeDtypeStruct((images, parts - 1, rows - TILE, lanes), jnp.float32),
            jax.ShapeDtypeStruct((1, LANES), jnp.float32),
            jax.ShapeDtypeStruct(given.shape, jnp.float32),
        ],
        in_specs=[vmem] * 4,
        out_specs=[vmem] * 4,
        scratch_shapes=[
            pltpu.VMEM((parts, rows, lanes), jnp.float32),
            pltpu.VMEM((6, images, TILE, lanes), jnp.float32),
            pltpu.VMEM((images, lanes), jnp.float32),
        ],
        compiler_params=pltpu.CompilerParams(vmem_limit_bytes=26 * MIB),
        name="second_step",
    )(given, phi, moved, tilt)


def spacing(row, coef, images):
    def quantity(q):
        return pltpu.roll(row, (LANES - images * q) % LANES, 1)

    lane = lane_of(row.shape)
    change = jnp.where((lane > 0) & (lane < images - 1), tangent_share(row, images) - coef, 0.0)
    squares, gaps, gap_diff, gap_before, diff_before = (quantity(q) for q in range(1, 6))
    change_before = pltpu.roll(change, 1, 1)
    squares_before = pltpu.roll(squares, 1, 1)
    cross = change * gap_diff - change_before * gap_before
    tangent = change * change * squares + change_before * change_before * squares_before
    tangent = tangent - 2.0 * change * change_before * diff_before
    length = jnp.maximum(gaps - 2.0 * DT * cross + DT * DT * tangent, 0.0)
    dist = jnp.where((lane > 0) & (lane < images), jnp.sqrt(length + EPS), 0.0)

    shape = (images, LANES)
    slot = lane_of(shape)
    image = row_of(shape)
    arc = jnp.sum(jnp.where(image <= slot, spread(dist, images), 0.0), axis=0, keepdims=True)
    total = jnp.sum(dist, axis=1, keepdims=True)
    target = image.astype(jnp.float32) * (total / (images - 1))
    inside = (slot >= 1) & (slot <= images - 2) & (arc <= target)
    lower = jnp.sum(jnp.where(inside, 1.0, 0.0), axis=1, keepdims=True)
    where = slot.astype(jnp.float32)
    start = jnp.sum(jnp.where(where == lower, arc, 0.0), axis=1, keepdims=True)
    step = jnp.sum(jnp.where(where == lower + 1.0, dist, 0.0), axis=1, keepdims=True)
    return change, lower, (target - start) / step


def mix_kernel(given_ref, coef_ref, one_ref, two_ref, out_ref, final, changes, shares):
    images, planes, core, lanes = two_ref.shape
    change, lower, share = spacing(read_sums(given_ref), coef_ref[...], images)
    changes[...] = spread(change, images)
    shares[...] = share
    image = row_of(lower.shape)
    lowers = [jnp.sum(jnp.where(image == j, lower, 0.0)).astype(jnp.int32) for j in range(images)]

    def finish(i, carry):
        after = jnp.minimum(i + 1, images - 1)
        before = jnp.maximum(i - 1, 0)
        scale = DT * changes[pl.ds(i, 1)]
        for p in range(planes):
            final[i, p] = two_ref[i, p] - scale * (one_ref[after, p, :core] - one_ref[before, p, :core])
        return carry

    lax.fori_loop(0, images, finish, 0)
    for j in range(images):
        portion = shares[j : j + 1]
        for p in range(planes):
            out_ref[j, p] = (1.0 - portion) * final[lowers[j], p] + portion * final[lowers[j] + 1, p]


def mix(given, coef, one, two):
    images, planes, core, lanes = two.shape
    return pl.pallas_call(
        mix_kernel,
        out_shape=jax.ShapeDtypeStruct(two.shape, jnp.float32),
        in_specs=[vmem] * 4,
        out_specs=vmem,
        scratch_shapes=[
            pltpu.VMEM(two.shape, jnp.float32),
            pltpu.VMEM((images, lanes), jnp.float32),
            pltpu.VMEM((images, lanes), jnp.float32),
        ],
        compiler_params=pltpu.CompilerParams(vmem_limit_bytes=20 * MIB),
        name="mix",
    )(given, coef, one, two)


def place_kernel(blocks_ref, out_ref, sem):
    count, planes, half, lanes = blocks_ref.shape
    copies = []
    for k in range(count):
        r, c = divmod(k, count // 2)
        piece = out_ref.at[0, :, pl.ds(r * half, half), pl.ds(c * lanes, lanes)]
        copies.append(pltpu.make_async_copy(blocks_ref.at[k], piece, sem.at[k]))
    for copy in copies:
        copy.start()
    for copy in copies:
        copy.wait()


def put_in_place(blocks):
    count, planes, half, lanes = blocks.shape
    return pl.pallas_call(
        place_kernel,
        out_shape=jax.ShapeDtypeStruct((1, planes, 2 * half, count // 2 * lanes), jnp.float32),
        in_specs=[anywhere],
        out_specs=anywhere,
        scratch_shapes=[pltpu.SemaphoreType.DMA((count,))],
        compiler_params=pltpu.CompilerParams(vmem_limit_bytes=MIB),
        name="put_in_place",
    )(blocks)


def exchange(block, axes):
    return lax.all_to_all(block, axes, split_axis=0, concat_axis=0, tiled=True)


def rim_rows(path, tilt, axis):
    count = lax.axis_size(axis)
    ahead = [(i, (i + 1) % count) for i in range(count)]
    back = [(target, source) for source, target in ahead]
    first = jnp.concatenate([path[..., :TILE, :], tilt[None, ..., :TILE, :]])
    last = jnp.concatenate([path[..., -TILE:, :], tilt[None, ..., -TILE:, :]])
    return lax.ppermute(last, axis, ahead), lax.ppermute(first, axis, back)


def per_device(axes, path, tilt):
    devices = lax.axis_size(axes)
    place = lax.axis_index("img").astype(jnp.int32)[None]
    above, below = rim_rows(path, tilt, "space")
    packed = pack(path[0])
    packed, tilt_block = rims(place, path[0], above, below, tilt, packed)
    packed, tilt_block = lax.optimization_barrier((packed, tilt_block))
    phi = exchange(packed, "img")
    moved, sums = first_step(phi, tilt_block, devices)
    one, two, coef, sums = second_step(exchange(sums, axes), phi, moved, tilt_block)
    mixed = mix(exchange(sums, axes), coef, one, two)
    return put_in_place(exchange(mixed, "img"))


def solution(mesh):
    return jax.shard_map(
        functools.partial(per_device, tuple(mesh.axis_names)),
        mesh=mesh,
        in_specs=(P("img", None, "space", None), P(None, "space", None)),
        out_specs=P("img", None, "space", None),
        check_vma=False,
    )
```

time: 251 us -> 197 us (0.78)
  waiting for transfers between devices: 86.9 us -> 1.16 us
  blocking collectives: 70.8 us -> 156 us
  local copies, waits for them, and re-layouts: 22.5 us -> 4.32 us
  Pallas kernels: 49.5 us -> 31.6 us
  starting transfers between devices: 18.9 us -> 2.97 us
    all_to_all x2 -> x4, blocking collectives: 70.8 us -> 156 us  [exchange(): return lax.all_to_all(block, axes, split_axis=0, concat_axis=0, tiled=True)]
    all_to_all x2 -> x0, waiting for transfers between devices: 78.8 us -> none  [the longest x1 69.6 us: per_device(): phi = lax.all_to_all(packed, 'img', split_axis=0, concat_axis=0, tiled=True)]
    all_to_all x2 -> x0, starting transfers between devices: 13 us -> none  [the longest x1 8.21 us: per_device(): phi = lax.all_to_all(packed, 'img', split_axis=0, concat_axis=0, tiled=True)]
    pallas_call x1, Pallas kernels: 21.1 us -> 12.4 us  [second_step(): pl.pallas_call(second_kernel, out_shape=[jax.ShapeDtypeStruct(phi.shape,...]
    ppermute x4 -> x2, waiting for transfers between devices: 8.11 us -> 1.16 us  [rim_rows(): return (lax.ppermute(last, axis, ahead), lax.ppermute(first, axis, back))]
    unnamed x8 -> x4, local copies, waits for them, and re-layouts: 8.88 us -> 2.19 us
    pallas_call x1, Pallas kernels: 15.8 us -> 10.6 us  [first_step(): pl.pallas_call(first_kernel, out_shape=[jax.ShapeDtypeStruct(phi.shape, j...]
    transpose x1 -> x0, local copies, waits for them, and re-layouts: 5.2 us -> none  [per_device(): back.reshape(2, count // 2, planes, rows, lanes).transpose(2, 0, 3, 1, 4)]
  transfers between devices with their start and end apart: 6 -> 2, of which waited for: 4 -> 1; matrix products, arithmetic and copies ran while one was open for 0% -> 0% of each run, Pallas kernels for 0% -> 2%
where the time goes in v2:
time: 197 us; the launch traced here: 196 us
  blocking collectives  156 us (79%)
  Pallas kernels  31.6 us (16%)
  local copies, waits for them, and re-layouts  4.32 us (2%)
  starting transfers between devices  2.97 us (2%)
    all_to_all x4, blocking collectives, exchange(): return lax.all_to_all(block, axes, split_axis=0, concat_axis=0, tiled=True)  156 us
    pallas_call x1, Pallas kernels, second_step(): pl.pallas_call(second_kernel, out_shape=[jax.ShapeDtypeStruct(phi.shape,...  12.4 us
    pallas_call x1, Pallas kernels, first_step(): pl.pallas_call(first_kernel, out_shape=[jax.ShapeDtypeStruct(phi.shape, j...  10.6 us
  transfers between devices with their start and end apart: 2, of which 1 were waited for; matrix products, arithmetic and copies ran while one was open for 0% of the time, Pallas kernels for 2%

profile of v2, /device:TPU:0, one launch (start us, length us, event | category | flops | bytes accessed | tf_op | source)
XLA Modules:
  0.0 196.4 jit_solution(17863955506253544221)
XLA Ops:
  0.0 1.1 fusion
  1.1 1.1 slice_bitcast_fusion
  2.2 0.0 collective-permute-start
  2.3 3.0 %collective-permute-start.1 = (f32[2,8,8,1024]{3,2,1,0:T(8,128)S(1)}, f32[2,8,8,1024]{3,2,1,0:T(8,128)S(1)}, u32[]{:S(2)}, u32[]{:S(2)}) collective-permute-start(f32[2,8,8,1024]{3,2,1,0:T(8,128)S(1)} %pad_maximum_fusion.1), channel_id=1, source_target_pairs={{1,0},{2,1},{3,2},{4,3},{5,4},{6,5},{7,6},{0,7},{9,8},{10,9},{11,1... | collective-permute-start | bytes 1572872 | tf_op jit(solution)/shard_map/ppermute | solution.py:481
  5.2 0.0 copy-start
  5.2 2.2 %copy-done = f32[1,8,128,1024]{3,2,1,0:T(8,128)S(1)} copy-done((f32[1,8,128,1024]{3,2,1,0:T(8,128)S(1)}, f32[1,8,128,1024]{3,2,1,0:T(8,128)}, u32[]{:S(2)}) %copy-start) | copy-done | bytes 4194328
  7.4 0.0 copy-start.1
  7.4 3.5 %pack.1.packed_ref = f32[16,9,72,128]{3,2,1,0:T(8,128)S(1)} custom-call(f32[8,128,1024]{2,1,0:T(8,128)S(1)} %bitcast.6), custom_call_target="tpu_custom_call" | custom-call | flops 10000000 | bytes 16777216 | tf_op jit(solution)/shard_map/pack/pallas_call | solution.py:82
  10.9 1.2 collective-permute-done.above_ref
  12.0 0.0 collective-permute-done.1.below_ref
  12.0 0.0 copy-done.1
  12.0 1.3 rims.1
  13.3 71.8 %all_to_all.20.phi_ref = f32[16,9,72,128]{3,2,1,0:T(8,128)S(1)} all-to-all(f32[16,9,72,128]{3,2,1,0:T(8,128)S(1)} %get-tuple-element.13), channel_id=1, replica_groups=mesh['img'=16,'space'=8] {'img'}, dimensions={0} | all-to-all | bytes 10616832 | tf_op jit(solution)/shard_map/all_to_all | solution.py:472
  85.1 10.6 %first_step.1 = (f32[16,9,72,128]{3,2,1,0:T(8,128)S(1)}, f32[128,1,128]{2,1,0:T(1,128)S(1)}) custom-call(f32[16,9,72,128]{3,2,1,0:T(8,128)S(1)} %all_to_all.20.phi_ref, f32[9,72,128]{2,1,0:T(8,128)S(1)} %get-tuple-element.14.tilt_ref), custom_call_target="tpu_custom_call" | custom-call | tf_op jit(solution)/shard_map/first_step/pallas_call | solution.py:294
  95.6 16.8 %all_to_all.21.given_ref = f32[128,1,128]{2,1,0:T(1,128)S(1)} all-to-all(f32[128,1,128]{2,1,0:T(1,128)S(1)} %get-tuple-element.15), channel_id=1, replica_groups=mesh['img'=16,'space'=8] {'img','space'}, dimensions={0} | all-to-all | bytes 131072 | tf_op jit(solution)/shard_map/all_to_all | solution.py:472
  112.4 12.4 %second_step.1 = (f32[16,9,72,128]{3,2,1,0:T(8,128)S(1)}, f32[16,8,64,128]{3,2,1,0:T(8,128)S(1)}, f32[1,128]{1,0:T(1,128)S(1)}, f32[128,1,128]{2,1,0:T(1,128)S(1)}) custom-call(f32[128,1,128]{2,1,0:T(1,128)S(1)} %all_to_all.21.given_ref, f32[16,9,72,128]{3,2,1,0:T(8,128)S(1)} %all_to_all.20.phi_ref, f32[16,9,72,128]{3,2,1,0:T(8,128)S(1)} %get-tuple-element.16.moved_ref, ...), custom_call_target="tpu_custom_call" | custom-call | tf_op jit(solution)/shard_map/second_step/pallas_call | solution.py:356
  124.8 13.9 %all_to_all.22.given_ref = f32[128,1,128]{2,1,0:T(1,128)S(1)} all-to-all(f32[128,1,128]{2,1,0:T(1,128)S(1)} %get-tuple-element.17), channel_id=1, replica_groups=mesh['img'=16,'space'=8] {'img','space'}, dimensions={0} | all-to-all | bytes 131072 | tf_op jit(solution)/shard_map/all_to_all | solution.py:472
  138.7 1.8 mix.1
  140.5 53.8 %all_to_all.23.blocks_ref = f32[16,8,64,128]{3,2,1,0:T(8,128)S(1)} all-to-all(f32[16,8,64,128]{3,2,1,0:T(8,128)S(1)} %mix.1), channel_id=1, replica_groups=mesh['img'=16,'space'=8] {'img'}, dimensions={0} | all-to-all | bytes 8388608 | tf_op jit(solution)/shard_map/all_to_all | solution.py:472
  194.3 2.1 %put_in_place.1 = f32[1,8,128,1024]{3,2,1,0:T(8,128)} custom-call(f32[16,8,64,128]{3,2,1,0:T(8,128)S(1)} %all_to_all.23.blocks_ref), custom_call_target="tpu_custom_call" | custom-call | tf_op jit(solution)/shard_map/put_in_place/pallas_call | solution.py:460
  (2 shorter events, 0.1 us)
Async XLA Ops:
  2.2 9.8 %collective-permute-start = (f32[2,8,8,1024]{3,2,1,0:T(8,128)S(1)}, f32[2,8,8,1024]{3,2,1,0:T(8,128)S(1)}, u32[]{:S(2)}, u32[]{:S(2)}) collective-permute-start(f32[2,8,8,1024]{3,2,1,0:T(8,128)S(1)} %pad_maximum_fusion), channel_id=1, source_target_pairs={{0,1},{1,2},{2,3},{3,4},{4,5},{5,6},{6,7},{7,0},{8,9},{9,10},{10,1... | collective-permute-start | bytes 1572872 | tf_op jit(solution)/shard_map/ppermute | solution.py:481
  2.3 9.8 %collective-permute-start.1 = (f32[2,8,8,1024]{3,2,1,0:T(8,128)S(1)}, f32[2,8,8,1024]{3,2,1,0:T(8,128)S(1)}, u32[]{:S(2)}, u32[]{:S(2)}) collective-permute-start(f32[2,8,8,1024]{3,2,1,0:T(8,128)S(1)} %pad_maximum_fusion.1), channel_id=1, source_target_pairs={{1,0},{2,1},{3,2},{4,3},{5,4},{6,5},{7,6},{0,7},{9,8},{10,9},{11,1... | collective-permute-start | bytes 1572872 | tf_op jit(solution)/shard_map/ppermute | solution.py:481
  5.2 2.2 %copy-start = (f32[1,8,128,1024]{3,2,1,0:T(8,128)S(1)}, f32[1,8,128,1024]{3,2,1,0:T(8,128)}, u32[]{:S(2)}) copy-start(f32[1,8,128,1024]{3,2,1,0:T(8,128)} %param.2) | copy-start | bytes 12582916
  7.4 4.6 %copy-start.1 = (f32[8,128,1024]{2,1,0:T(8,128)S(1)}, f32[8,128,1024]{2,1,0:T(8,128)}, u32[]{:S(2)}) copy-start(f32[8,128,1024]{2,1,0:T(8,128)} %tilt_ref.1) | copy-start | bytes 12582916

commit v3 on v2

--- a/solution.py
+++ b/solution.py
@@ -46,148 +46,156 @@
     return jnp.take_along_axis(both, source, axis=1, mode="promise_in_bounds")
 
 
-def pack_kernel(path_ref, out_ref, held, edge, strips, load_sem, core_sem, strip_sem):
-    planes, rows, cols = path_ref.shape
-    half = rows // 2
-    blocks = cols // LANES
-    loads = [pltpu.make_async_copy(path_ref.at[p], held.at[p], load_sem.at[p]) for p in range(planes)]
-    for copy in loads:
-        copy.start()
-    cores = []
-    for k in range(2 * blocks):
-        r, c = divmod(k, blocks)
-        piece = path_ref.at[:, pl.ds(r * half, half), pl.ds(c * LANES, LANES)]
-        cores.append(pltpu.make_async_copy(piece, out_ref.at[k, pl.ds(0, planes), pl.ds(0, half)], core_sem.at[k]))
-    for copy in cores:
-        copy.start()
-    for p in range(planes):
-        loads[p].wait()
-        for c in range(blocks):
-            tile = held[p, :, c * LANES : (c + 1) * LANES]
-            edge[c] = edges(tile, p, jnp.zeros_like(tile) if p == 0 else edge[c])
-    for c in range(blocks):
-        strip = strip_of(edge[(c - 1) % blocks], edge[c], edge[(c + 1) % blocks])
-        strips[c] = strip[:half]
-        strips[blocks + c] = strip[half:]
-    copy = pltpu.make_async_copy(strips, out_ref.at[:, planes, pl.ds(0, half)], strip_sem)
-    copy.start()
-    copy.wait()
-    for copy in cores:
-        copy.wait()
-
-
-def pack(path):
-    planes, rows, cols = path.shape
-    count, half = 2 * cols // LANES, rows // 2
-    return pl.pallas_call(
-        pack_kernel,
-        out_shape=jax.ShapeDtypeStruct((count, planes + 1, half + TILE, LANES), jnp.float32),
-        in_specs=[anywhere],
-        out_specs=anywhere,
-        scratch_shapes=[
-            pltpu.VMEM((planes, rows, cols), jnp.float32),
-            pltpu.VMEM((count // 2, rows, LANES), jnp.float32),
-            pltpu.VMEM((count, half, LANES), jnp.float32),
-            pltpu.SemaphoreType.DMA((planes,)),
-            pltpu.SemaphoreType.DMA((count,)),
-            pltpu.SemaphoreType.DMA,
-        ],
-        compiler_params=pltpu.CompilerParams(vmem_limit_bytes=12 * MIB),
-        cost_estimate=pl.CostEstimate(flops=10_000_000, bytes_accessed=16 * MIB, transcendentals=0),
-        name="pack",
-    )(path)
-
-
-def rims_kernel(
-    place_ref, path_ref, above_ref, below_ref, tilt_ref, packed_ref, out_ref, tilt_out, own, rims, core, side, edge, sem, out_sem
-):
+def pack_kernel(place_ref, path_ref, tilt_ref, out_ref, tilt_out, edge, core_sem, rim_sem, tilt_sem):
     planes, rows, cols = path_ref.shape
     half = rows // 2
     blocks = cols // LANES
     place = place_ref[0]
-    c = place % blocks
-    upper = place < blocks
+    copies = []
+    for k in range(2 * blocks):
+        r, c = divmod(k, blocks)
+        cut = pl.ds(c * LANES, LANES)
+        core = out_ref.at[k, pl.ds(0, planes), pl.ds(0, half)]
+        rim = out_ref.at[k, pl.ds(0, planes), pl.ds(half, TILE)]
+        own = pl.ds(half - TILE * r, TILE)
+        copies.append(pltpu.make_async_copy(path_ref.at[:, pl.ds(r * half, half), cut], core, core_sem.at[k]))
+        copies.append(pltpu.make_async_copy(path_ref.at[:, own, cut], rim, rim_sem.at[k]))
+    rest = []
     start = pl.multiple_of((place // blocks) * half, half)
     beside = pl.multiple_of(half - TILE * (place // blocks), TILE)
-    middle = path_ref.at[:, pl.ds(half - TILE, 2 * TILE)]
-    loads = [
-        pltpu.make_async_copy(middle, own.at[:, pl.ds(0, 2 * TILE)], sem.at[0]),
-        pltpu.make_async_copy(above_ref.at[0], own.at[:, pl.ds(2 * TILE, TILE)], sem.at[1]),
-        pltpu.make_async_copy(below_ref.at[0], own.at[:, pl.ds(3 * TILE, TILE)], sem.at[2]),
-    ]
     for at, shift in enumerate((blocks - 1, 0, 1)):
-        cut = pl.ds(pl.multiple_of(((c + shift) % blocks) * LANES, LANES), LANES)
-        pieces = (
-            (tilt_ref.at[:, pl.ds(start, half), cut], core.at[at]),
-            (tilt_ref.at[:, pl.ds(beside, TILE), cut], side.at[at, 0]),
-            (above_ref.at[1, :, :, cut], side.at[at, 1]),
-            (below_ref.at[1, :, :, cut], side.at[at, 2]),
-        )
-        for k, (source, target) in enumerate(pieces):
-            loads.append(pltpu.make_async_copy(source, target, sem.at[3 + 4 * at + k]))
-    for copy in loads:
+        cut = pl.ds(pl.multiple_of(((place + shift) % blocks) * LANES, LANES), LANES)
+        core = tilt_out.at[at, :, pl.ds(0, half)]
+        rim = tilt_out.at[at, :, pl.ds(half, TILE)]
+        rest.append(pltpu.make_async_copy(tilt_ref.at[:, pl.ds(start, half), cut], core, tilt_sem.at[2 * at]))
+        rest.append(pltpu.make_async_copy(tilt_ref.at[:, pl.ds(beside, TILE), cut], rim, tilt_sem.at[2 * at + 1]))
+    for copy in copies + rest:
         copy.start()
-    for copy in loads:
+    for r in range(2):
+        for c in range(blocks):
+            k = r * blocks + c
+            copies[2 * k].wait()
+            copies[2 * k + 1].wait()
+            total = jnp.zeros((half, LANES), jnp.float32)
+            for p in range(planes):
+                total = edges(out_ref[k, p, :half], p, total)
+            edge[c] = total
+        for c in range(blocks):
+            strip = strip_of(edge[(c - 1) % blocks], edge[c], edge[(c + 1) % blocks])
+            out_ref[r * blocks + c, planes, :half] = strip
+    for copy in rest:
         copy.wait()
+
+
+def pack(place, path, tilt):
+    planes, rows, cols = path.shape
+    count, half = 2 * cols // LANES, rows // 2
+    return pl.pallas_call(
+        pack_kernel,
+        out_shape=[
+            pltpu.VMEM((count, planes + 1, half + TILE, LANES), jnp.float32),
+            pltpu.VMEM((3, planes, half + TILE, LANES), jnp.float32),
+        ],
+        in_specs=[smem] + [anywhere] * 2,
+        out_specs=[vmem] * 2,
+        scratch_shapes=[
+            pltpu.VMEM((count // 2, half, LANES), jnp.float32),
+            pltpu.SemaphoreType.DMA((count,)),
+            pltpu.SemaphoreType.DMA((count,)),
+            pltpu.SemaphoreType.DMA((6,)),
+        ],
+        compiler_params=pltpu.CompilerParams(vmem_limit_bytes=12 * MIB),
+        cost_estimate=pl.CostEstimate(flops=10_000_000, bytes_accessed=16 * MIB, transcendentals=0),
+        name="pack",
+    )(place, path, tilt)
+
+
+def rim_kernel(path_ref, tilt_ref, first_ref, last_ref, held, sem):
+    rows = path_ref.shape[1]
+    copies = []
+    for k, ref in enumerate((path_ref, tilt_ref)):
+        for at, start in enumerate((0, rows - TILE)):
+            copies.append(pltpu.make_async_copy(ref.at[:, pl.ds(start, TILE)], held.at[k, at], sem.at[2 * k + at]))
+    for copy in copies:
+        copy.start()
+    for copy in copies:
+        copy.wait()
+    for p in range(path_ref.shape[0]):
+        upper = row_of(held.shape[3:]) < RIM
+        first_ref[p] = jnp.where(upper, held[0, 0, p], pltpu.roll(held[1, 0, p], RIM, 0))
+        last_ref[p] = jnp.where(upper, pltpu.roll(held[0, 1, p], RIM, 0), held[1, 1, p])
+
+
+def rim_rows(path, tilt):
+    planes, rows, cols = path.shape
+    return pl.pallas_call(
+        rim_kernel,
+        out_shape=[jax.ShapeDtypeStruct((planes, TILE, cols), jnp.float32)] * 2,
+        in_specs=[anywhere] * 2,
+        out_specs=[vmem] * 2,
+        scratch_shapes=[pltpu.VMEM((2, 2, planes, TILE, cols), jnp.float32), pltpu.SemaphoreType.DMA((4,))],
+        compiler_params=pltpu.CompilerParams(vmem_limit_bytes=4 * MIB),
+        name="rim_rows",
+    )(path, tilt)
+
+
+def rims_kernel(place_ref, above_ref, below_ref, tilt_ref, packed_ref, out_ref, tilt_out, edge):
+    planes, _, cols = above_ref.shape
+    count = out_ref.shape[0]
+    half = out_ref.shape[2] - TILE
+    blocks = count // 2
+    place = place_ref[0]
+    upper = place < blocks
     under = row_of((TILE, LANES)) < RIM
     for r in range(2):
-        for b in range(blocks):
-            cut = slice(b * LANES, (b + 1) * LANES)
+        for c in range(blocks):
+            k = r * blocks + c
+            cut = slice(c * LANES, (c + 1) * LANES)
             total = jnp.zeros((TILE, LANES), jnp.float32)
             for p in range(planes):
+                own = packed_ref[k, p, half:]
                 if r == 0:
-                    tile = jnp.where(under, own[p, TILE : 2 * TILE, cut], own[p, 2 * TILE : 3 * TILE, cut])
+                    tile = jnp.where(under, own, pltpu.roll(above_ref[p, :, cut], RIM, 0))
                 else:
-                    tile = jnp.where(under, own[p, 3 * TILE :, cut], own[p, :TILE, cut])
-                rims[r * blocks + b, p] = tile
+                    tile = jnp.where(under, below_ref[p, :, cut], own)
+                out_ref[k, p, half:] = tile
                 total = edges(tile, p, total)
-            edge[pl.ds(b * TILE, TILE)] = total
-        for b in range(blocks):
-            tiles = [edge[pl.ds(((b + shift) % blocks) * TILE, TILE)] for shift in (-1, 0, 1)]
-            rims[r * blocks + b, planes] = strip_of(*tiles)
-    out = pltpu.make_async_copy(rims, out_ref.at[:, :, pl.ds(half, TILE)], out_sem)
-    out.start()
+            edge[c] = total
+        for c in range(blocks):
+            strip = strip_of(edge[(c - 1) % blocks], edge[c], edge[(c + 1) % blocks])
+            out_ref[r * blocks + c, planes, half:] = strip
     sums = []
-    for at in range(3):
+    for at, shift in enumerate((blocks - 1, 0, 1)):
+        cut = pl.ds(pl.multiple_of(((place + shift) % blocks) * LANES, LANES), LANES)
         total = jnp.zeros((half + TILE, LANES), jnp.float32)
         for p in range(planes):
-            next_to = jnp.where(upper, side[at, 0, p], side[at, 2, p])
-            last = jnp.where(upper, side[at, 1, p], side[at, 0, p])
-            rim = jnp.where(under, next_to, last)
-            full = jnp.concatenate([core[at, p], rim], axis=0)
+            own = tilt_ref[at, p, half:]
+            next_to = jnp.where(upper, own, pltpu.roll(below_ref[p, :, cut], RIM, 0))
+            last = jnp.where(upper, above_ref[p, :, cut], own)
+            full = jnp.concatenate([tilt_ref[at, p, :half], jnp.where(under, next_to, last)], axis=0)
             if at == 1:
                 tilt_out[p] = full
             total = edges(full, p, total)
         sums.append(total)
     tilt_out[planes] = strip_of(*sums)
-    out.wait()
-
-
-def rims(place, path, above, below, tilt, packed):
-    planes, rows, cols = path.shape
-    count, half = 2 * cols // LANES, rows // 2
+
+
+def rims(place, above, below, tilt, packed):
+    planes, _, cols = above.shape
     return pl.pallas_call(
         rims_kernel,
         out_shape=[
-            jax.ShapeDtypeStruct(packed.shape, jnp.float32),
-            jax.ShapeDtypeStruct((planes + 1, half + TILE, LANES), jnp.float32),
-        ],
-        in_specs=[smem] + [anywhere] * 5,
-        out_specs=[anywhere, vmem],
-        input_output_aliases={5: 0},
-        scratch_shapes=[
-            pltpu.VMEM((planes, 4 * TILE, cols), jnp.float32),
-            pltpu.VMEM((count, planes + 1, TILE, LANES), jnp.float32),
-            pltpu.VMEM((3, planes, half, LANES), jnp.float32),
-            pltpu.VMEM((3, 3, planes, TILE, LANES), jnp.float32),
-            pltpu.VMEM((cols // LANES * TILE, LANES), jnp.float32),
-            pltpu.SemaphoreType.DMA((15,)),
-            pltpu.SemaphoreType.DMA,
-        ],
-        compiler_params=pltpu.CompilerParams(vmem_limit_bytes=8 * MIB),
+            pltpu.VMEM(packed.shape, jnp.float32),
+            pltpu.VMEM((planes + 1, *packed.shape[2:]), jnp.float32),
+        ],
+        in_specs=[smem] + [vmem] * 4,
+        out_specs=[vmem] * 2,
+        input_output_aliases={4: 0},
+        scratch_shapes=[pltpu.VMEM((cols // LANES, TILE, LANES), jnp.float32)],
+        compiler_params=pltpu.CompilerParams(vmem_limit_bytes=12 * MIB),
         cost_estimate=pl.CostEstimate(flops=1_000_000, bytes_accessed=4 * MIB, transcendentals=0),
         name="rims",
-    )(place, path, above, below, tilt, packed)
+    )(place, above, below, tilt, packed)
 
 
 def rows_sum(x):
@@ -285,7 +293,7 @@
         acc[1, i] = square
         return carry
 
-    lax.fori_loop(0, images, body, 0)
+    lax.fori_loop(0, images, body, 0, unroll=2)
     write_sums(acc, sums_ref)
 
 
@@ -347,7 +355,7 @@
             acc[q, i] = sums[q]
         return carry
 
-    lax.fori_loop(0, images, body, 0)
+    lax.fori_loop(0, images, body, 0, unroll=2)
     write_sums(acc, sums_ref)
 
 
@@ -472,21 +480,18 @@
     return lax.all_to_all(block, axes, split_axis=0, concat_axis=0, tiled=True)
 
 
-def rim_rows(path, tilt, axis):
-    count = lax.axis_size(axis)
-    ahead = [(i, (i + 1) % count) for i in range(count)]
-    back = [(target, source) for source, target in ahead]
-    first = jnp.concatenate([path[..., :TILE, :], tilt[None, ..., :TILE, :]])
-    last = jnp.concatenate([path[..., -TILE:, :], tilt[None, ..., -TILE:, :]])
-    return lax.ppermute(last, axis, ahead), lax.ppermute(first, axis, back)
-
-
 def per_device(axes, path, tilt):
     devices = lax.axis_size(axes)
     place = lax.axis_index("img").astype(jnp.int32)[None]
-    above, below = rim_rows(path, tilt, "space")
-    packed = pack(path[0])
-    packed, tilt_block = rims(place, path[0], above, below, tilt, packed)
+    own = pltpu.with_memory_space_constraint(path[0], pltpu.HBM)
+    tilt = pltpu.with_memory_space_constraint(tilt, pltpu.HBM)
+    first, last = rim_rows(own, tilt)
+    count = lax.axis_size("space")
+    ahead = [(i, (i + 1) % count) for i in range(count)]
+    above = lax.ppermute(last, "space", ahead)
+    below = lax.ppermute(first, "space", [(target, source) for source, target in ahead])
+    packed, tilt_near = pack(place, own, tilt)
+    packed, tilt_block = rims(place, above, below, tilt_near, packed)
     packed, tilt_block = lax.optimization_barrier((packed, tilt_block))
     phi = exchange(packed, "img")
     moved, sums = first_step(phi, tilt_block, devices)

time: 197 us -> 192 us (0.975)
  local copies, waits for them, and re-layouts: 4.32 us -> 0 us
    unnamed x4 -> x0, local copies, waits for them, and re-layouts: 2.19 us -> none
    pallas_call x2 -> x3, Pallas kernels: 4.72 us -> 6.63 us  [the longest x1 4.45 us: pack(): pl.pallas_call(pack_kernel, out_shape=[pltpu.VMEM((count, planes + 1, hal...]
  transfers between devices with their start and end apart: 2 -> 2, of which waited for: 1 -> 0; matrix products, arithmetic and copies ran while one was open for 0% -> 0% of each run, Pallas kernels for 2% -> 2%
where the time goes in v3:
time: 192 us
  blocking collectives  156 us (81%)
  Pallas kernels  32.6 us (17%)
  starting transfers between devices  2.96 us (2%)
    all_to_all x4, blocking collectives, exchange(): return lax.all_to_all(block, axes, split_axis=0, concat_axis=0, tiled=True)  156 us
    pallas_call x1, Pallas kernels, second_step(): pl.pallas_call(second_kernel, out_shape=[jax.ShapeDtypeStruct(phi.shape,...  11.8 us
    pallas_call x1, Pallas kernels, first_step(): pl.pallas_call(first_kernel, out_shape=[jax.ShapeDtypeStruct(phi.shape, j...  10.2 us
    pallas_call x1, Pallas kernels, pack(): pl.pallas_call(pack_kernel, out_shape=[pltpu.VMEM((count, planes + 1, hal...  4.45 us
  transfers between devices with their start and end apart: 2, of which 0 were waited for; matrix products, arithmetic and copies ran while one was open for 0% of the time, Pallas kernels for 2%

profile of v3, /device:TPU:0, one launch (start us, length us, event | category | flops | bytes accessed | tf_op | source)
XLA Modules:
  0.0 191.5 jit_solution(14454555152653618659)
XLA Ops:
  0.0 1.3 rim_rows.1
  1.3 0.0 collective-permute-start
  1.3 2.9 %collective-permute-start.1 = (f32[8,8,1024]{2,1,0:T(8,128)S(1)}, f32[8,8,1024]{2,1,0:T(8,128)S(1)}, u32[]{:S(2)}, u32[]{:S(2)}) collective-permute-start(f32[8,8,1024]{2,1,0:T(8,128)S(1)} %get-tuple-element.18), channel_id=1, source_target_pairs={{1,0},{2,1},{3,2},{4,3},{5,4},{6,5},{7,6},{0,7},{9,8},{10,9},{11,1... | collective-permute-start | bytes 786440 | tf_op jit(solution)/shard_map/ppermute | solution.py:492
  4.3 4.5 %pack.1 = (f32[16,9,72,128]{3,2,1,0:T(8,128)S(1)}, f32[3,8,72,128]{3,2,1,0:T(8,128)S(1)}) custom-call(s32[1]{0:T(128)} %bitcast.place_ref, f32[8,128,1024]{2,1,0:T(8,128)} %bitcast.3, f32[8,128,1024]{2,1,0:T(8,128)} %tilt_ref.3), custom_call_target="tpu_custom_call" | custom-call | flops 10000000 | bytes 16777216 | tf_op jit(solution)/shard_map/pack/pallas_call | solution.py:93
  8.7 0.0 collective-permute-done.above_ref
  8.7 0.0 collective-permute-done.1.below_ref
  8.7 0.9 rims.1
  9.6 70.9 %all_to_all.20.phi_ref = f32[16,9,72,128]{3,2,1,0:T(8,128)S(1)} all-to-all(f32[16,9,72,128]{3,2,1,0:T(8,128)S(1)} %get-tuple-element.21), channel_id=1, replica_groups=mesh['img'=16,'space'=8] {'img'}, dimensions={0} | all-to-all | bytes 10616832 | tf_op jit(solution)/shard_map/all_to_all | solution.py:480
  80.5 10.2 %first_step.1 = (f32[16,9,72,128]{3,2,1,0:T(8,128)S(1)}, f32[128,1,128]{2,1,0:T(1,128)S(1)}) custom-call(f32[16,9,72,128]{3,2,1,0:T(8,128)S(1)} %all_to_all.20.phi_ref, f32[9,72,128]{2,1,0:T(8,128)S(1)} %get-tuple-element.22.tilt_ref), custom_call_target="tpu_custom_call" | custom-call | tf_op jit(solution)/shard_map/first_step/pallas_call | solution.py:302
  90.7 17.3 %all_to_all.21.given_ref = f32[128,1,128]{2,1,0:T(1,128)S(1)} all-to-all(f32[128,1,128]{2,1,0:T(1,128)S(1)} %get-tuple-element.23), channel_id=1, replica_groups=mesh['img'=16,'space'=8] {'img','space'}, dimensions={0} | all-to-all | bytes 131072 | tf_op jit(solution)/shard_map/all_to_all | solution.py:480
  108.0 11.8 %second_step.1 = (f32[16,9,72,128]{3,2,1,0:T(8,128)S(1)}, f32[16,8,64,128]{3,2,1,0:T(8,128)S(1)}, f32[1,128]{1,0:T(1,128)S(1)}, f32[128,1,128]{2,1,0:T(1,128)S(1)}) custom-call(f32[128,1,128]{2,1,0:T(1,128)S(1)} %all_to_all.21.given_ref, f32[16,9,72,128]{3,2,1,0:T(8,128)S(1)} %all_to_all.20.phi_ref, f32[16,9,72,128]{3,2,1,0:T(8,128)S(1)} %get-tuple-element.24.moved_ref, ...), custom_call_target="tpu_custom_call" | custom-call | tf_op jit(solution)/shard_map/second_step/pallas_call | solution.py:364
  119.9 13.9 %all_to_all.22.given_ref = f32[128,1,128]{2,1,0:T(1,128)S(1)} all-to-all(f32[128,1,128]{2,1,0:T(1,128)S(1)} %get-tuple-element.25), channel_id=1, replica_groups=mesh['img'=16,'space'=8] {'img','space'}, dimensions={0} | all-to-all | bytes 131072 | tf_op jit(solution)/shard_map/all_to_all | solution.py:480
  133.8 1.8 mix.1
  135.6 53.8 %all_to_all.23.blocks_ref = f32[16,8,64,128]{3,2,1,0:T(8,128)S(1)} all-to-all(f32[16,8,64,128]{3,2,1,0:T(8,128)S(1)} %mix.1), channel_id=1, replica_groups=mesh['img'=16,'space'=8] {'img'}, dimensions={0} | all-to-all | bytes 8388608 | tf_op jit(solution)/shard_map/all_to_all | solution.py:480
  189.4 2.1 %put_in_place.1 = f32[1,8,128,1024]{3,2,1,0:T(8,128)} custom-call(f32[16,8,64,128]{3,2,1,0:T(8,128)S(1)} %all_to_all.23.blocks_ref), custom_call_target="tpu_custom_call" | custom-call | tf_op jit(solution)/shard_map/put_in_place/pallas_call | solution.py:468
Async XLA Ops:
  1.3 7.4 %collective-permute-start = (f32[8,8,1024]{2,1,0:T(8,128)S(1)}, f32[8,8,1024]{2,1,0:T(8,128)S(1)}, u32[]{:S(2)}, u32[]{:S(2)}) collective-permute-start(f32[8,8,1024]{2,1,0:T(8,128)S(1)} %get-tuple-element.17), channel_id=1, source_target_pairs={{0,1},{1,2},{2,3},{3,4},{4,5},{5,6},{6,7},{7,0},{8,9},{9,10},{10,1... | collective-permute-start | bytes 786440 | tf_op jit(solution)/shard_map/ppermute | solution.py:491
  1.3 7.4 %collective-permute-start.1 = (f32[8,8,1024]{2,1,0:T(8,128)S(1)}, f32[8,8,1024]{2,1,0:T(8,128)S(1)}, u32[]{:S(2)}, u32[]{:S(2)}) collective-permute-start(f32[8,8,1024]{2,1,0:T(8,128)S(1)} %get-tuple-element.18), channel_id=1, source_target_pairs={{1,0},{2,1},{3,2},{4,3},{5,4},{6,5},{7,6},{0,7},{9,8},{10,9},{11,1... | collective-permute-start | bytes 786440 | tf_op jit(solution)/shard_map/ppermute | solution.py:492

commit v4 on v3

--- a/solution.py
+++ b/solution.py
@@ -202,33 +202,67 @@
     return pltpu.roll(x, 1, 0) + pltpu.roll(x, x.shape[0] - 1, 0)
 
 
-def laplace_strip(s):
+def neighbours_strip(s):
     total = pltpu.roll(s, GROUP, 1) + pltpu.roll(s, LANES - GROUP, 1)
     total = total + pltpu.roll(s, 2, 1) + pltpu.roll(s, LANES - 2, 1)
-    return total + rows_sum(s) - 6.0 * s
-
-
-def laplace_plane(x, below, above, strip, p):
+    return total + rows_sum(s)
+
+
+def split(x):
+    high = x.astype(jnp.bfloat16)
+    rest = x - high.astype(jnp.float32)
+    middle = rest.astype(jnp.bfloat16)
+    low = (rest - middle.astype(jnp.float32)).astype(jnp.bfloat16)
+    return jnp.concatenate([high, middle, low], axis=1)
+
+
+def write_band(band):
+    shape = band.shape
+    apart = row_of(shape) % LANES - lane_of(shape)
+    band[...] = jnp.where((apart == 1) | (apart == -1), 1.0, 0.0).astype(jnp.bfloat16)
+
+
+def beside_all(planes, band, beside):
+    count, rows, lanes = planes.shape
+    parts = split(planes.reshape(count * rows, lanes))
+    total = jnp.dot(parts, band[...], preferred_element_type=jnp.float32)
+    beside[...] = total.reshape(planes.shape)
+
+
+def neighbours_given(x, below, above, strip, p, within):
+    lane = lane_of(x.shape)
+    rim = pltpu.roll(strip, (LANES - GROUP * p - 6) % LANES, 1)
+    rim = jnp.where((lane == 0) | (lane == LANES - 1), rim, 0.0)
+    return (below + above) + rows_sum(x) + (within + rim)
+
+
+def neighbours_plane(x, below, above, strip, p):
     lane = lane_of(x.shape)
     beside = pltpu.roll(strip, (LANES - GROUP * p - 6) % LANES, 1)
     left = jnp.where(lane == 0, beside, pltpu.roll(x, 1, 1))
     right = jnp.where(lane == LANES - 1, beside, pltpu.roll(x, LANES - 1, 1))
-    return (below + above) + rows_sum(x) + (left + right) - 6.0 * x
-
-
-def potential(field, tilt_ref, mu):
+    return (below + above) + rows_sum(x) + (left + right)
+
+
+def potential(field, whole, tilt_ref, mu, band, beside):
     planes = mu.shape[0] - 1
     strip = field(planes)
-    mu[planes] = strip * strip * strip - strip - laplace_strip(strip) - tilt_ref[planes]
+    mu[planes] = strip * (strip * strip + 5.0) - (neighbours_strip(strip) + tilt_ref[planes])
+    if whole is not None:
+        beside_all(whole, band, beside)
     for p in range(planes):
         x = field(p)
-        lap = laplace_plane(x, field((p - 1) % planes), field((p + 1) % planes), strip, p)
-        mu[p] = x * x * x - x - lap - tilt_ref[p]
+        below, above = field((p - 1) % planes), field((p + 1) % planes)
+        if whole is None:
+            around = neighbours_plane(x, below, above, strip, p)
+        else:
+            around = neighbours_given(x, below, above, strip, p, beside[p])
+        mu[p] = x * (x * x + 5.0) - (around + tilt_ref[p])
 
 
 def force_plane(mu, p):
     planes = mu.shape[0] - 1
-    return laplace_plane(mu[p], mu[(p - 1) % planes], mu[(p + 1) % planes], mu[planes], p)
+    return neighbours_plane(mu[p], mu[(p - 1) % planes], mu[(p + 1) % planes], mu[planes], p) - 6.0 * mu[p]
 
 
 def fold(x):
@@ -271,16 +305,17 @@
     return jnp.where((lane > 0) & (lane < images - 1), coef, 0.0)
 
 
-def first_kernel(phi_ref, tilt_ref, moved_ref, sums_ref, mu, acc):
+def first_kernel(phi_ref, tilt_ref, moved_ref, sums_ref, mu, acc, band, beside):
     images, parts, rows, lanes = phi_ref.shape
     planes = parts - 1
     core = rows - TILE
+    write_band(band)
 
     def body(i, carry):
         after = jnp.minimum(i + 1, images - 1)
         before = jnp.maximum(i - 1, 0)
-        potential(lambda p: phi_ref[i, p], tilt_ref, mu)
-        moved_ref[i, planes] = phi_ref[i, planes] + DT * laplace_strip(mu[planes])
+        potential(lambda p: phi_ref[i, p], phi_ref[i, :planes], tilt_ref, mu, band, beside)
+        moved_ref[i, planes] = phi_ref[i, planes] + DT * (neighbours_strip(mu[planes]) - 6.0 * mu[planes])
         product = jnp.zeros((TILE, lanes), jnp.float32)
         square = jnp.zeros((TILE, lanes), jnp.float32)
         for p in range(planes):
@@ -310,6 +345,8 @@
         scratch_shapes=[
             pltpu.VMEM((parts, rows, lanes), jnp.float32),
             pltpu.VMEM((2, images, TILE, lanes), jnp.float32),
+            pltpu.VMEM((3 * LANES, LANES), jnp.bfloat16),
+            pltpu.VMEM((parts - 1, rows, lanes), jnp.float32),
         ],
         compiler_params=pltpu.CompilerParams(vmem_limit_bytes=16 * MIB),
         name="first_step",
@@ -324,21 +361,21 @@
     coef_ref[...] = coef_row
     coefs[...] = spread(coef_row, images)
 
-    def update(i, carry):
+    def update(i):
         after = jnp.minimum(i + 1, images - 1)
         before = jnp.maximum(i - 1, 0)
         scale = DT * coefs[pl.ds(i, 1)]
         for p in range(parts):
             one_ref[i, p] = moved_ref[i, p] - scale * (phi_ref[after, p] - phi_ref[before, p])
-        return carry
-
-    lax.fori_loop(0, images, update, 0)
+
+    update(0)
 
     def body(i, carry):
         after = jnp.minimum(i + 1, images - 1)
         before = jnp.maximum(i - 1, 0)
         earlier = jnp.maximum(i - 2, 0)
-        potential(lambda p: one_ref[i, p], tilt_ref, mu)
+        update(after)
+        potential(lambda p: one_ref[i, p], None, tilt_ref, mu, None, None)
         coef = coefs[pl.ds(i, 1)]
         sums = [jnp.zeros((TILE, lanes), jnp.float32)] * 6
         for p in range(planes):
@@ -355,7 +392,7 @@
             acc[q, i] = sums[q]
         return carry
 
-    lax.fori_loop(0, images, body, 0, unroll=2)
+    lax.fori_loop(0, images, body, 0, unroll=4)
     write_sums(acc, sums_ref)
 
 

time: 192 us -> 189 us (0.984)
  Pallas kernels: 32.6 us -> 29.8 us
where the time goes in v4:
time: 189 us
  blocking collectives  156 us (83%)
  Pallas kernels  29.8 us (16%)
  starting transfers between devices  2.96 us (2%)
    all_to_all x4, blocking collectives, exchange(): return lax.all_to_all(block, axes, split_axis=0, concat_axis=0, tiled=True)  156 us
    pallas_call x1, Pallas kernels, second_step(): pl.pallas_call(second_kernel, out_shape=[jax.ShapeDtypeStruct(phi.shape,...  10.9 us
    pallas_call x1, Pallas kernels, first_step(): pl.pallas_call(first_kernel, out_shape=[jax.ShapeDtypeStruct(phi.shape, j...  8.34 us
    pallas_call x1, Pallas kernels, pack(): pl.pallas_call(pack_kernel, out_shape=[pltpu.VMEM((count, planes + 1, hal...  4.45 us
  transfers between devices with their start and end apart: 2, of which 0 were waited for; matrix products, arithmetic and copies ran while one was open for 0% of the time, Pallas kernels for 2%

profile of v4, /device:TPU:0, one launch (start us, length us, event | category | flops | bytes accessed | tf_op | source)
XLA Modules:
  0.0 188.8 jit_solution(4809662296571808524)
XLA Ops:
  0.0 1.3 rim_rows.1
  1.3 0.0 collective-permute-start
  1.3 2.9 %collective-permute-start.1 = (f32[8,8,1024]{2,1,0:T(8,128)S(1)}, f32[8,8,1024]{2,1,0:T(8,128)S(1)}, u32[]{:S(2)}, u32[]{:S(2)}) collective-permute-start(f32[8,8,1024]{2,1,0:T(8,128)S(1)} %get-tuple-element.18), channel_id=1, source_target_pairs={{1,0},{2,1},{3,2},{4,3},{5,4},{6,5},{7,6},{0,7},{9,8},{10,9},{11,1... | collective-permute-start | bytes 786440 | tf_op jit(solution)/shard_map/ppermute | solution.py:529
  4.3 4.5 %pack.1 = (f32[16,9,72,128]{3,2,1,0:T(8,128)S(1)}, f32[3,8,72,128]{3,2,1,0:T(8,128)S(1)}) custom-call(s32[1]{0:T(128)} %bitcast.place_ref, f32[8,128,1024]{2,1,0:T(8,128)} %bitcast.3, f32[8,128,1024]{2,1,0:T(8,128)} %tilt_ref.3), custom_call_target="tpu_custom_call" | custom-call | flops 10000000 | bytes 16777216 | tf_op jit(solution)/shard_map/pack/pallas_call | solution.py:93
  8.7 0.0 collective-permute-done.above_ref
  8.7 0.0 collective-permute-done.1.below_ref
  8.7 0.9 rims.1
  9.6 70.9 %all_to_all.20.phi_ref = f32[16,9,72,128]{3,2,1,0:T(8,128)S(1)} all-to-all(f32[16,9,72,128]{3,2,1,0:T(8,128)S(1)} %get-tuple-element.21), channel_id=1, replica_groups=mesh['img'=16,'space'=8] {'img'}, dimensions={0} | all-to-all | bytes 10616832 | tf_op jit(solution)/shard_map/all_to_all | solution.py:517
  80.5 8.3 %first_step.1 = (f32[16,9,72,128]{3,2,1,0:T(8,128)S(1)}, f32[128,1,128]{2,1,0:T(1,128)S(1)}) custom-call(f32[16,9,72,128]{3,2,1,0:T(8,128)S(1)} %all_to_all.20.phi_ref, f32[9,72,128]{2,1,0:T(8,128)S(1)} %get-tuple-element.22.tilt_ref), custom_call_target="tpu_custom_call" | custom-call | tf_op jit(solution)/shard_map/first_step/pallas_call | solution.py:337
  88.9 17.3 %all_to_all.21.given_ref = f32[128,1,128]{2,1,0:T(1,128)S(1)} all-to-all(f32[128,1,128]{2,1,0:T(1,128)S(1)} %get-tuple-element.23), channel_id=1, replica_groups=mesh['img'=16,'space'=8] {'img','space'}, dimensions={0} | all-to-all | bytes 131072 | tf_op jit(solution)/shard_map/all_to_all | solution.py:517
  106.2 10.9 %second_step.1 = (f32[16,9,72,128]{3,2,1,0:T(8,128)S(1)}, f32[16,8,64,128]{3,2,1,0:T(8,128)S(1)}, f32[1,128]{1,0:T(1,128)S(1)}, f32[128,1,128]{2,1,0:T(1,128)S(1)}) custom-call(f32[128,1,128]{2,1,0:T(1,128)S(1)} %all_to_all.21.given_ref, f32[16,9,72,128]{3,2,1,0:T(8,128)S(1)} %all_to_all.20.phi_ref, f32[16,9,72,128]{3,2,1,0:T(8,128)S(1)} %get-tuple-element.24.moved_ref, ...), custom_call_target="tpu_custom_call" | custom-call | tf_op jit(solution)/shard_map/second_step/pallas_call | solution.py:401
  117.1 13.9 %all_to_all.22.given_ref = f32[128,1,128]{2,1,0:T(1,128)S(1)} all-to-all(f32[128,1,128]{2,1,0:T(1,128)S(1)} %get-tuple-element.25), channel_id=1, replica_groups=mesh['img'=16,'space'=8] {'img','space'}, dimensions={0} | all-to-all | bytes 131072 | tf_op jit(solution)/shard_map/all_to_all | solution.py:517
  131.0 1.8 mix.1
  132.9 53.8 %all_to_all.23.blocks_ref = f32[16,8,64,128]{3,2,1,0:T(8,128)S(1)} all-to-all(f32[16,8,64,128]{3,2,1,0:T(8,128)S(1)} %mix.1), channel_id=1, replica_groups=mesh['img'=16,'space'=8] {'img'}, dimensions={0} | all-to-all | bytes 8388608 | tf_op jit(solution)/shard_map/all_to_all | solution.py:517
  186.6 2.1 %put_in_place.1 = f32[1,8,128,1024]{3,2,1,0:T(8,128)} custom-call(f32[16,8,64,128]{3,2,1,0:T(8,128)S(1)} %all_to_all.23.blocks_ref), custom_call_target="tpu_custom_call" | custom-call | tf_op jit(solution)/shard_map/put_in_place/pallas_call | solution.py:505
Async XLA Ops:
  1.3 7.4 %collective-permute-start = (f32[8,8,1024]{2,1,0:T(8,128)S(1)}, f32[8,8,1024]{2,1,0:T(8,128)S(1)}, u32[]{:S(2)}, u32[]{:S(2)}) collective-permute-start(f32[8,8,1024]{2,1,0:T(8,128)S(1)} %get-tuple-element.17), channel_id=1, source_target_pairs={{0,1},{1,2},{2,3},{3,4},{4,5},{5,6},{6,7},{7,0},{8,9},{9,10},{10,1... | collective-permute-start | bytes 786440 | tf_op jit(solution)/shard_map/ppermute | solution.py:528
  1.3 7.4 %collective-permute-start.1 = (f32[8,8,1024]{2,1,0:T(8,128)S(1)}, f32[8,8,1024]{2,1,0:T(8,128)S(1)}, u32[]{:S(2)}, u32[]{:S(2)}) collective-permute-start(f32[8,8,1024]{2,1,0:T(8,128)S(1)} %get-tuple-element.18), channel_id=1, source_target_pairs={{1,0},{2,1},{3,2},{4,3},{5,4},{6,5},{7,6},{0,7},{9,8},{10,9},{11,1... | collective-permute-start | bytes 786440 | tf_op jit(solution)/shard_map/ppermute | solution.py:529

commit v5 on v4

--- a/solution.py
+++ b/solution.py
@@ -14,6 +14,7 @@
 LANES = 128
 GROUP = 16
 MIB = 1024 * 1024
+SLOTS = 4
 
 vmem = pl.BlockSpec(memory_space=pltpu.VMEM)
 smem = pl.BlockSpec(memory_space=pltpu.SMEM)
@@ -46,43 +47,65 @@
     return jnp.take_along_axis(both, source, axis=1, mode="promise_in_bounds")
 
 
-def pack_kernel(place_ref, path_ref, tilt_ref, out_ref, tilt_out, edge, core_sem, rim_sem, tilt_sem):
+def own_plane(shape):
+    lane = lane_of(shape)
+    k = lane % GROUP
+    group = lane // GROUP
+    even = (k % 2 == 0) & (k >= 2 * RIM)
+    here = even | (k == 1) | (k == 3)
+    there = (k == 13) | (k == 15)
+    return jnp.where(here, group, jnp.where(there, (group + 1) % (LANES // GROUP), -1))
+
+
+def outer(before, after):
+    lane = lane_of(before.shape)
+    k = lane % GROUP
+    both = jnp.where(k < RIM, before, after)
+    source = lane - k + jnp.where(k % 2 == 0, k // 2, (k + 3) // 2) % (2 * RIM)
+    return jnp.take_along_axis(both, source, axis=1, mode="promise_in_bounds")
+
+
+def beside(first, second):
+    return jnp.where(own_plane(first.shape) < 0, first, pltpu.roll(second, 2 * RIM, 1))
+
+
+def pack_kernel(place_ref, path_ref, tilt_ref, out_ref, tilt_out, held, edge, load_sem, tilt_sem):
     planes, rows, cols = path_ref.shape
     half = rows // 2
+    ring = half + TILE
+    near = (ring // TILE + 1) // 2 * TILE
     blocks = cols // LANES
     place = place_ref[0]
-    copies = []
-    for k in range(2 * blocks):
-        r, c = divmod(k, blocks)
-        cut = pl.ds(c * LANES, LANES)
-        core = out_ref.at[k, pl.ds(0, planes), pl.ds(0, half)]
-        rim = out_ref.at[k, pl.ds(0, planes), pl.ds(half, TILE)]
-        own = pl.ds(half - TILE * r, TILE)
-        copies.append(pltpu.make_async_copy(path_ref.at[:, pl.ds(r * half, half), cut], core, core_sem.at[k]))
-        copies.append(pltpu.make_async_copy(path_ref.at[:, own, cut], rim, rim_sem.at[k]))
+    loads = [pltpu.make_async_copy(path_ref.at[p], held.at[p], load_sem.at[p]) for p in range(planes)]
     rest = []
     start = pl.multiple_of((place // blocks) * half, half)
-    beside = pl.multiple_of(half - TILE * (place // blocks), TILE)
+    next_to = pl.multiple_of(half - TILE * (place // blocks), TILE)
     for at, shift in enumerate((blocks - 1, 0, 1)):
         cut = pl.ds(pl.multiple_of(((place + shift) % blocks) * LANES, LANES), LANES)
         core = tilt_out.at[at, :, pl.ds(0, half)]
         rim = tilt_out.at[at, :, pl.ds(half, TILE)]
         rest.append(pltpu.make_async_copy(tilt_ref.at[:, pl.ds(start, half), cut], core, tilt_sem.at[2 * at]))
-        rest.append(pltpu.make_async_copy(tilt_ref.at[:, pl.ds(beside, TILE), cut], rim, tilt_sem.at[2 * at + 1]))
-    for copy in copies + rest:
+        rest.append(pltpu.make_async_copy(tilt_ref.at[:, pl.ds(next_to, TILE), cut], rim, tilt_sem.at[2 * at + 1]))
+    for copy in loads + rest:
         copy.start()
-    for r in range(2):
+    for p in range(planes):
+        loads[p].wait()
         for c in range(blocks):
-            k = r * blocks + c
-            copies[2 * k].wait()
-            copies[2 * k + 1].wait()
-            total = jnp.zeros((half, LANES), jnp.float32)
-            for p in range(planes):
-                total = edges(out_ref[k, p, :half], p, total)
-            edge[c] = total
-        for c in range(blocks):
-            strip = strip_of(edge[(c - 1) % blocks], edge[c], edge[(c + 1) % blocks])
-            out_ref[r * blocks + c, planes, :half] = strip
+            cut = slice(c * LANES, (c + 1) * LANES)
+            tile = held[p, :, cut]
+            edge[c] = edges(tile, p, jnp.zeros_like(tile) if p == 0 else edge[c])
+            for r in range(2):
+                out_ref[r * blocks + c, ring * p : ring * p + half] = tile[r * half : (r + 1) * half]
+                own = half - TILE * r
+                out_ref[r * blocks + c, ring * p + half : ring * (p + 1)] = tile[own : own + TILE]
+    for c in range(blocks):
+        columns = outer(edge[(c - 1) % blocks], edge[(c + 1) % blocks])
+        for r in range(2):
+            part = columns[r * half : (r + 1) * half]
+            at = ring * planes
+            far = half - near
+            out_ref[r * blocks + c, at : at + far] = beside(part[:far], part[near:])
+            out_ref[r * blocks + c, at + far : at + near] = part[far:near]
     for copy in rest:
         copy.wait()
 
@@ -90,21 +113,23 @@
 def pack(place, path, tilt):
     planes, rows, cols = path.shape
     count, half = 2 * cols // LANES, rows // 2
+    ring = half + TILE
+    near = (ring // TILE + 1) // 2 * TILE
     return pl.pallas_call(
         pack_kernel,
         out_shape=[
-            pltpu.VMEM((count, planes + 1, half + TILE, LANES), jnp.float32),
-            pltpu.VMEM((3, planes, half + TILE, LANES), jnp.float32),
+            pltpu.VMEM((count, ring * planes + near, LANES), jnp.float32),
+            pltpu.VMEM((3, planes, ring, LANES), jnp.float32),
         ],
         in_specs=[smem] + [anywhere] * 2,
         out_specs=[vmem] * 2,
         scratch_shapes=[
-            pltpu.VMEM((count // 2, half, LANES), jnp.float32),
-            pltpu.SemaphoreType.DMA((count,)),
-            pltpu.SemaphoreType.DMA((count,)),
+            pltpu.VMEM((planes, rows, cols), jnp.float32),
+            pltpu.VMEM((count // 2, rows, LANES), jnp.float32),
+            pltpu.SemaphoreType.DMA((planes,)),
             pltpu.SemaphoreType.DMA((6,)),
         ],
-        compiler_params=pltpu.CompilerParams(vmem_limit_bytes=12 * MIB),
+        compiler_params=pltpu.CompilerParams(vmem_limit_bytes=14 * MIB),
         cost_estimate=pl.CostEstimate(flops=10_000_000, bytes_accessed=16 * MIB, transcendentals=0),
         name="pack",
     )(place, path, tilt)
@@ -142,7 +167,9 @@
 def rims_kernel(place_ref, above_ref, below_ref, tilt_ref, packed_ref, out_ref, tilt_out, edge):
     planes, _, cols = above_ref.shape
     count = out_ref.shape[0]
-    half = out_ref.shape[2] - TILE
+    ring = tilt_out.shape[1]
+    half = ring - TILE
+    near = out_ref.shape[1] - ring * planes
     blocks = count // 2
     place = place_ref[0]
     upper = place < blocks
@@ -153,17 +180,20 @@
             cut = slice(c * LANES, (c + 1) * LANES)
             total = jnp.zeros((TILE, LANES), jnp.float32)
             for p in range(planes):
-                own = packed_ref[k, p, half:]
+                at = slice(ring * p + half, ring * (p + 1))
+                own = packed_ref[k, at]
                 if r == 0:
                     tile = jnp.where(under, own, pltpu.roll(above_ref[p, :, cut], RIM, 0))
                 else:
                     tile = jnp.where(under, below_ref[p, :, cut], own)
-                out_ref[k, p, half:] = tile
+                out_ref[k, at] = tile
                 total = edges(tile, p, total)
             edge[c] = total
         for c in range(blocks):
-            strip = strip_of(edge[(c - 1) % blocks], edge[c], edge[(c + 1) % blocks])
-            out_ref[r * blocks + c, planes, half:] = strip
+            columns = outer(edge[(c - 1) % blocks], edge[(c + 1) % blocks])
+            at = ring * planes + half - near
+            place_at = slice(at, at + TILE)
+            out_ref[r * blocks + c, place_at] = beside(packed_ref[r * blocks + c, place_at], columns)
     sums = []
     for at, shift in enumerate((blocks - 1, 0, 1)):
         cut = pl.ds(pl.multiple_of(((place + shift) % blocks) * LANES, LANES), LANES)
@@ -186,7 +216,7 @@
         rims_kernel,
         out_shape=[
             pltpu.VMEM(packed.shape, jnp.float32),
-            pltpu.VMEM((planes + 1, *packed.shape[2:]), jnp.float32),
+            pltpu.VMEM((planes + 1, tilt.shape[2], LANES), jnp.float32),
         ],
         in_specs=[smem] + [vmem] * 4,
         out_specs=[vmem] * 2,
@@ -217,16 +247,15 @@
 
 
 def write_band(band):
-    shape = band.shape
-    apart = row_of(shape) % LANES - lane_of(shape)
-    band[...] = jnp.where((apart == 1) | (apart == -1), 1.0, 0.0).astype(jnp.bfloat16)
-
-
-def beside_all(planes, band, beside):
-    count, rows, lanes = planes.shape
-    parts = split(planes.reshape(count * rows, lanes))
-    total = jnp.dot(parts, band[...], preferred_element_type=jnp.float32)
-    beside[...] = total.reshape(planes.shape)
+    shape = (band.shape[0], LANES)
+    row = row_of(shape) % LANES
+    lane = lane_of(shape)
+    apart = row - lane
+    band[:, :LANES] = jnp.where((apart == 1) | (apart == -1), 1.0, 0.0).astype(jnp.bfloat16)
+    k = lane % GROUP
+    right = jnp.where(k > 2 * RIM, k - 13, k + 3) // 2 + LANES - RIM
+    column = jnp.where(k % 2 == 0, k // 2 - RIM, right)
+    band[:, LANES:] = jnp.where((row == column) & (own_plane(shape) >= 0), 1.0, 0.0).astype(jnp.bfloat16)
 
 
 def neighbours_given(x, below, above, strip, p, within):
@@ -244,19 +273,17 @@
     return (below + above) + rows_sum(x) + (left + right)
 
 
-def potential(field, whole, tilt_ref, mu, band, beside):
+def potential(field, sides, tilt_ref, mu):
     planes = mu.shape[0] - 1
     strip = field(planes)
     mu[planes] = strip * (strip * strip + 5.0) - (neighbours_strip(strip) + tilt_ref[planes])
-    if whole is not None:
-        beside_all(whole, band, beside)
     for p in range(planes):
         x = field(p)
         below, above = field((p - 1) % planes), field((p + 1) % planes)
-        if whole is None:
+        if sides is None:
             around = neighbours_plane(x, below, above, strip, p)
         else:
-            around = neighbours_given(x, below, above, strip, p, beside[p])
+            around = neighbours_given(x, below, above, strip, p, sides(p))
         mu[p] = x * (x * x + 5.0) - (around + tilt_ref[p])
 
 
@@ -305,56 +332,87 @@
     return jnp.where((lane > 0) & (lane < images - 1), coef, 0.0)
 
 
-def first_kernel(phi_ref, tilt_ref, moved_ref, sums_ref, mu, acc, band, beside):
-    images, parts, rows, lanes = phi_ref.shape
+def first_kernel(phi_ref, tilt_ref, moved_ref, strip_ref, sums_ref, mu, acc, band, sides, strips):
+    images, parts, rows, lanes = moved_ref.shape
     planes = parts - 1
     core = rows - TILE
+    near = phi_ref.shape[1] - rows * planes
     write_band(band)
-
-    def body(i, carry):
+    owner = own_plane((rows, lanes))
+
+    def plane(i, p):
+        return phi_ref[i, rows * p : rows * (p + 1)]
+
+    def prepare(i, slot):
+        sides[slot] = jnp.dot(split(phi_ref[i, : rows * planes]), band[...], preferred_element_type=jnp.float32)
+        columns = phi_ref[i, rows * planes :]
+        far = pltpu.roll(columns[: rows - near], lanes - 2 * RIM, 1)
+        strip = jnp.concatenate([columns, far], axis=0)
+        for p in range(planes):
+            strip = jnp.where(owner == p, sides[slot, rows * p : rows * (p + 1), lanes:], strip)
+        strips[slot] = strip
+        strip_ref[i] = strip
+
+    def step(i, slot):
         after = jnp.minimum(i + 1, images - 1)
         before = jnp.maximum(i - 1, 0)
-        potential(lambda p: phi_ref[i, p], phi_ref[i, :planes], tilt_ref, mu, band, beside)
-        moved_ref[i, planes] = phi_ref[i, planes] + DT * (neighbours_strip(mu[planes]) - 6.0 * mu[planes])
+
+        def field(p):
+            return strips[slot] if p == planes else plane(i, p)
+
+        potential(field, lambda p: sides[slot, rows * p : rows * (p + 1), :lanes], tilt_ref, mu.at[slot])
+        moved_ref[i, planes] = field(planes) + DT * (neighbours_strip(mu[slot, planes]) - 6.0 * mu[slot, planes])
         product = jnp.zeros((TILE, lanes), jnp.float32)
         square = jnp.zeros((TILE, lanes), jnp.float32)
         for p in range(planes):
-            force = force_plane(mu, p)
-            moved_ref[i, p] = phi_ref[i, p] + DT * force
-            diff = phi_ref[after, p, :core] - phi_ref[before, p, :core]
+            force = force_plane(mu.at[slot], p)
+            moved_ref[i, p] = field(p) + DT * force
+            at = slice(rows * p, rows * p + core)
+            diff = phi_ref[after, at] - phi_ref[before, at]
             product = product + fold(force[:core] * diff)
             square = square + fold(diff * diff)
         acc[0, i] = product
         acc[1, i] = square
+
+    slots = mu.shape[0]
+
+    def body(t, carry):
+        for slot in range(slots):
+            prepare(jnp.minimum(slots * t + slot + 1, images - 1), (slot + 1) % slots)
+            step(slots * t + slot, slot)
         return carry
 
-    lax.fori_loop(0, images, body, 0, unroll=2)
+    prepare(0, 0)
+    lax.fori_loop(0, images // slots, body, 0)
     write_sums(acc, sums_ref)
 
 
 def first_step(phi, tilt, devices):
-    images, parts, rows, lanes = phi.shape
+    images = phi.shape[0]
+    parts, rows, lanes = tilt.shape
     return pl.pallas_call(
         first_kernel,
         out_shape=[
-            jax.ShapeDtypeStruct(phi.shape, jnp.float32),
+            jax.ShapeDtypeStruct((images, parts, rows, lanes), jnp.float32),
+            jax.ShapeDtypeStruct((images, rows, lanes), jnp.float32),
             jax.ShapeDtypeStruct((devices, 1, LANES), jnp.float32),
         ],
         in_specs=[vmem] * 2,
-        out_specs=[vmem] * 2,
+        out_specs=[vmem] * 3,
         scratch_shapes=[
-            pltpu.VMEM((parts, rows, lanes), jnp.float32),
+            pltpu.VMEM((SLOTS, parts, rows, lanes), jnp.float32),
             pltpu.VMEM((2, images, TILE, lanes), jnp.float32),
-            pltpu.VMEM((3 * LANES, LANES), jnp.bfloat16),
-            pltpu.VMEM((parts - 1, rows, lanes), jnp.float32),
-        ],
-        compiler_params=pltpu.CompilerParams(vmem_limit_bytes=16 * MIB),
+            pltpu.VMEM((3 * LANES, 2 * LANES), jnp.bfloat16),
+            pltpu.VMEM((SLOTS, (parts - 1) * rows, 2 * LANES), jnp.float32),
+            pltpu.VMEM((SLOTS, rows, lanes), jnp.float32),
+        ],
+        compiler_params=pltpu.CompilerParams(vmem_limit_bytes=20 * MIB),
         name="first_step",
     )(phi, tilt)
 
 
-def second_kernel(given_ref, phi_ref, moved_ref, tilt_ref, one_ref, two_ref, coef_ref, sums_ref, mu, acc, coefs):
-    images, parts, rows, lanes = phi_ref.shape
+def second_kernel(given_ref, phi_ref, strip_ref, moved_ref, tilt_ref, one_ref, two_ref, coef_ref, sums_ref, mu, acc, coefs):
+    images, parts, rows, lanes = moved_ref.shape
     planes = parts - 1
     core = rows - TILE
     coef_row = tangent_share(read_sums(given_ref), images)
@@ -365,8 +423,10 @@
         after = jnp.minimum(i + 1, images - 1)
         before = jnp.maximum(i - 1, 0)
         scale = DT * coefs[pl.ds(i, 1)]
-        for p in range(parts):
-            one_ref[i, p] = moved_ref[i, p] - scale * (phi_ref[after, p] - phi_ref[before, p])
+        for p in range(planes):
+            at = slice(rows * p, rows * (p + 1))
+            one_ref[i, p] = moved_ref[i, p] - scale * (phi_ref[after, at] - phi_ref[before, at])
+        one_ref[i, planes] = moved_ref[i, planes] - scale * (strip_ref[after] - strip_ref[before])
 
     update(0)
 
@@ -375,7 +435,7 @@
         before = jnp.maximum(i - 1, 0)
         earlier = jnp.maximum(i - 2, 0)
         update(after)
-        potential(lambda p: one_ref[i, p], None, tilt_ref, mu, None, None)
+        potential(lambda p: one_ref[i, p], None, tilt_ref, mu)
         coef = coefs[pl.ds(i, 1)]
         sums = [jnp.zeros((TILE, lanes), jnp.float32)] * 6
         for p in range(planes):
@@ -396,17 +456,17 @@
     write_sums(acc, sums_ref)
 
 
-def second_step(given, phi, moved, tilt):
-    images, parts, rows, lanes = phi.shape
+def second_step(given, phi, strips, moved, tilt):
+    images, parts, rows, lanes = moved.shape
     return pl.pallas_call(
         second_kernel,
         out_shape=[
-            jax.ShapeDtypeStruct(phi.shape, jnp.float32),
+            jax.ShapeDtypeStruct(moved.shape, jnp.float32),
             jax.ShapeDtypeStruct((images, parts - 1, rows - TILE, lanes), jnp.float32),
             jax.ShapeDtypeStruct((1, LANES), jnp.float32),
             jax.ShapeDtypeStruct(given.shape, jnp.float32),
         ],
-        in_specs=[vmem] * 4,
+        in_specs=[vmem] * 5,
         out_specs=[vmem] * 4,
         scratch_shapes=[
             pltpu.VMEM((parts, rows, lanes), jnp.float32),
@@ -415,7 +475,7 @@
         ],
         compiler_params=pltpu.CompilerParams(vmem_limit_bytes=26 * MIB),
         name="second_step",
-    )(given, phi, moved, tilt)
+    )(given, phi, strips, moved, tilt)
 
 
 def spacing(row, coef, images):
@@ -531,8 +591,8 @@
     packed, tilt_block = rims(place, above, below, tilt_near, packed)
     packed, tilt_block = lax.optimization_barrier((packed, tilt_block))
     phi = exchange(packed, "img")
-    moved, sums = first_step(phi, tilt_block, devices)
-    one, two, coef, sums = second_step(exchange(sums, axes), phi, moved, tilt_block)
+    moved, strips, sums = first_step(phi, tilt_block, devices)
+    one, two, coef, sums = second_step(exchange(sums, axes), phi, strips, moved, tilt_block)
     mixed = mix(exchange(sums, axes), coef, one, two)
     return put_in_place(exchange(mixed, "img"))
 

time: 189 us -> 187 us (0.989)
  blocking collectives: 156 us -> 154 us
    all_to_all x4, blocking collectives: 156 us -> 154 us  [exchange(): return lax.all_to_all(block, axes, split_axis=0, concat_axis=0, tiled=True)]
  transfers between devices with their start and end apart: 2 -> 2, of which waited for: 0 -> 1; matrix products, arithmetic and copies ran while one was open for 0% -> 0% of each run, Pallas kernels for 2% -> 2%
where the time goes in v5:
time: 187 us
  blocking collectives  154 us (82%)
  Pallas kernels  29.5 us (16%)
  starting transfers between devices  2.96 us (2%)
    all_to_all x4, blocking collectives, exchange(): return lax.all_to_all(block, axes, split_axis=0, concat_axis=0, tiled=True)  154 us
    pallas_call x1, Pallas kernels, second_step(): pl.pallas_call(second_kernel, out_shape=[jax.ShapeDtypeStruct(moved.shape...  11 us
    pallas_call x1, Pallas kernels, first_step(): pl.pallas_call(first_kernel, out_shape=[jax.ShapeDtypeStruct((images, par...  8.84 us
  transfers between devices with their start and end apart: 2, of which 1 were waited for; matrix products, arithmetic and copies ran while one was open for 0% of the time, Pallas kernels for 2%

profile of v5, /device:TPU:0, one launch (start us, length us, event | category | flops | bytes accessed | tf_op | source)
XLA Modules:
  0.0 186.7 jit_solution(6019842158870676135)
XLA Ops:
  0.0 1.3 rim_rows.1
  1.3 0.0 collective-permute-start
  1.3 2.9 %collective-permute-start.1 = (f32[8,8,1024]{2,1,0:T(8,128)S(1)}, f32[8,8,1024]{2,1,0:T(8,128)S(1)}, u32[]{:S(2)}, u32[]{:S(2)}) collective-permute-start(f32[8,8,1024]{2,1,0:T(8,128)S(1)} %get-tuple-element.19), channel_id=1, source_target_pairs={{1,0},{2,1},{3,2},{4,3},{5,4},{6,5},{7,6},{0,7},{9,8},{10,9},{11,1... | collective-permute-start | bytes 786440 | tf_op jit(solution)/shard_map/ppermute | solution.py:589
  4.3 3.5 %pack.1 = (f32[16,616,128]{2,1,0:T(8,128)S(1)}, f32[3,8,72,128]{3,2,1,0:T(8,128)S(1)}) custom-call(s32[1]{0:T(128)} %bitcast.place_ref, f32[8,128,1024]{2,1,0:T(8,128)} %bitcast.3, f32[8,128,1024]{2,1,0:T(8,128)} %tilt_ref.3), custom_call_target="tpu_custom_call" | custom-call | flops 10000000 | bytes 16777216 | tf_op jit(solution)/shard_map/pack/pallas_call | solution.py:118
  7.7 0.6 collective-permute-done.above_ref
  8.3 0.0 collective-permute-done.1.below_ref
  8.3 0.9 rims.1
  9.2 68.8 %all_to_all.20.phi_ref = f32[16,616,128]{2,1,0:T(8,128)S(1)} all-to-all(f32[16,616,128]{2,1,0:T(8,128)S(1)} %get-tuple-element.22), channel_id=1, replica_groups=mesh['img'=16,'space'=8] {'img'}, dimensions={0} | all-to-all | bytes 10092544 | tf_op jit(solution)/shard_map/all_to_all | solution.py:577
  78.0 8.8 %first_step.1 = (f32[16,9,72,128]{3,2,1,0:T(8,128)S(1)}, f32[16,72,128]{2,1,0:T(8,128)S(1)}, f32[128,1,128]{2,1,0:T(1,128)S(1)}) custom-call(f32[16,616,128]{2,1,0:T(8,128)S(1)} %all_to_all.20.phi_ref, f32[9,72,128]{2,1,0:T(8,128)S(1)} %get-tuple-element.23.tilt_ref), custom_call_target="tpu_custom_call" | custom-call | tf_op jit(solution)/shard_map/first_step/pallas_call | solution.py:393
  86.9 17.2 %all_to_all.21.given_ref = f32[128,1,128]{2,1,0:T(1,128)S(1)} all-to-all(f32[128,1,128]{2,1,0:T(1,128)S(1)} %get-tuple-element.24), channel_id=1, replica_groups=mesh['img'=16,'space'=8] {'img','space'}, dimensions={0} | all-to-all | bytes 131072 | tf_op jit(solution)/shard_map/all_to_all | solution.py:577
  104.1 11.0 %second_step.1 = (f32[16,9,72,128]{3,2,1,0:T(8,128)S(1)}, f32[16,8,64,128]{3,2,1,0:T(8,128)S(1)}, f32[1,128]{1,0:T(1,128)S(1)}, f32[128,1,128]{2,1,0:T(1,128)S(1)}) custom-call(f32[128,1,128]{2,1,0:T(1,128)S(1)} %all_to_all.21.given_ref, f32[16,616,128]{2,1,0:T(8,128)S(1)} %all_to_all.20.phi_ref, f32[16,72,128]{2,1,0:T(8,128)S(1)} %get-tuple-element.25.strip_ref, ...), custom_call_target="tpu_custom_call" | custom-call | tf_op jit(solution)/shard_map/second_step/pallas_call | solution.py:461
  115.1 13.9 %all_to_all.22.given_ref = f32[128,1,128]{2,1,0:T(1,128)S(1)} all-to-all(f32[128,1,128]{2,1,0:T(1,128)S(1)} %get-tuple-element.27), channel_id=1, replica_groups=mesh['img'=16,'space'=8] {'img','space'}, dimensions={0} | all-to-all | bytes 131072 | tf_op jit(solution)/shard_map/all_to_all | solution.py:577
  129.0 1.8 mix.1
  130.8 53.8 %all_to_all.23.blocks_ref = f32[16,8,64,128]{3,2,1,0:T(8,128)S(1)} all-to-all(f32[16,8,64,128]{3,2,1,0:T(8,128)S(1)} %mix.1), channel_id=1, replica_groups=mesh['img'=16,'space'=8] {'img'}, dimensions={0} | all-to-all | bytes 8388608 | tf_op jit(solution)/shard_map/all_to_all | solution.py:577
  184.6 2.1 %put_in_place.1 = f32[1,8,128,1024]{3,2,1,0:T(8,128)} custom-call(f32[16,8,64,128]{3,2,1,0:T(8,128)S(1)} %all_to_all.23.blocks_ref), custom_call_target="tpu_custom_call" | custom-call | tf_op jit(solution)/shard_map/put_in_place/pallas_call | solution.py:565
Async XLA Ops:
  1.3 7.0 %collective-permute-start = (f32[8,8,1024]{2,1,0:T(8,128)S(1)}, f32[8,8,1024]{2,1,0:T(8,128)S(1)}, u32[]{:S(2)}, u32[]{:S(2)}) collective-permute-start(f32[8,8,1024]{2,1,0:T(8,128)S(1)} %get-tuple-element.18), channel_id=1, source_target_pairs={{0,1},{1,2},{2,3},{3,4},{4,5},{5,6},{6,7},{7,0},{8,9},{9,10},{10,1... | collective-permute-start | bytes 786440 | tf_op jit(solution)/shard_map/ppermute | solution.py:588
  1.3 7.0 %collective-permute-start.1 = (f32[8,8,1024]{2,1,0:T(8,128)S(1)}, f32[8,8,1024]{2,1,0:T(8,128)S(1)}, u32[]{:S(2)}, u32[]{:S(2)}) collective-permute-start(f32[8,8,1024]{2,1,0:T(8,128)S(1)} %get-tuple-element.19), channel_id=1, source_target_pairs={{1,0},{2,1},{3,2},{4,3},{5,4},{6,5},{7,6},{0,7},{9,8},{10,9},{11,1... | collective-permute-start | bytes 786440 | tf_op jit(solution)/shard_map/ppermute | solution.py:589

commit v6 on v5

--- a/solution.py
+++ b/solution.py
@@ -69,7 +69,7 @@
     return jnp.where(own_plane(first.shape) < 0, first, pltpu.roll(second, 2 * RIM, 1))
 
 
-def pack_kernel(place_ref, path_ref, tilt_ref, out_ref, tilt_out, held, edge, load_sem, tilt_sem):
+def pack_kernel(place_ref, path_ref, tilt_ref, out_ref, tilt_out, rim_out, held, near_tilt, edge, load_sem, tilt_sem):
     planes, rows, cols = path_ref.shape
     half = rows // 2
     ring = half + TILE
@@ -82,8 +82,8 @@
     next_to = pl.multiple_of(half - TILE * (place // blocks), TILE)
     for at, shift in enumerate((blocks - 1, 0, 1)):
         cut = pl.ds(pl.multiple_of(((place + shift) % blocks) * LANES, LANES), LANES)
-        core = tilt_out.at[at, :, pl.ds(0, half)]
-        rim = tilt_out.at[at, :, pl.ds(half, TILE)]
+        core = near_tilt.at[at, :, pl.ds(0, half)]
+        rim = near_tilt.at[at, :, pl.ds(half, TILE)]
         rest.append(pltpu.make_async_copy(tilt_ref.at[:, pl.ds(start, half), cut], core, tilt_sem.at[2 * at]))
         rest.append(pltpu.make_async_copy(tilt_ref.at[:, pl.ds(next_to, TILE), cut], rim, tilt_sem.at[2 * at + 1]))
     for copy in loads + rest:
@@ -108,6 +108,15 @@
             out_ref[r * blocks + c, at + far : at + near] = part[far:near]
     for copy in rest:
         copy.wait()
+    sums = []
+    for at in range(3):
+        rim_out[at] = near_tilt[at, :, half:]
+        total = jnp.zeros((half, LANES), jnp.float32)
+        for p in range(planes):
+            total = edges(near_tilt[at, p, :half], p, total)
+        sums.append(total)
+    tilt_out[:planes] = near_tilt[1]
+    tilt_out[planes, :half] = strip_of(*sums)
 
 
 def pack(place, path, tilt):
@@ -119,12 +128,14 @@
         pack_kernel,
         out_shape=[
             pltpu.VMEM((count, ring * planes + near, LANES), jnp.float32),
-            pltpu.VMEM((3, planes, ring, LANES), jnp.float32),
+            pltpu.VMEM((planes + 1, ring, LANES), jnp.float32),
+            pltpu.VMEM((3, planes, TILE, LANES), jnp.float32),
         ],
         in_specs=[smem] + [anywhere] * 2,
-        out_specs=[vmem] * 2,
+        out_specs=[vmem] * 3,
         scratch_shapes=[
             pltpu.VMEM((planes, rows, cols), jnp.float32),
+            pltpu.VMEM((3, planes, ring, LANES), jnp.float32),
             pltpu.VMEM((count // 2, rows, LANES), jnp.float32),
             pltpu.SemaphoreType.DMA((planes,)),
             pltpu.SemaphoreType.DMA((6,)),
@@ -135,57 +146,75 @@
     )(place, path, tilt)
 
 
-def rim_kernel(path_ref, tilt_ref, first_ref, last_ref, held, sem):
-    rows = path_ref.shape[1]
+def rim_kernel(place_ref, path_ref, tilt_ref, first_ref, last_ref, side_ref, held, near, sem, near_sem):
+    planes, rows, cols = path_ref.shape
+    blocks = cols // LANES
+    place = place_ref[0]
+    upper = place < blocks
+    start = pl.multiple_of((1 - place // blocks) * (rows - TILE), TILE)
     copies = []
-    for k, ref in enumerate((path_ref, tilt_ref)):
-        for at, start in enumerate((0, rows - TILE)):
-            copies.append(pltpu.make_async_copy(ref.at[:, pl.ds(start, TILE)], held.at[k, at], sem.at[2 * k + at]))
+    for at, row in enumerate((0, rows - TILE)):
+        copies.append(pltpu.make_async_copy(path_ref.at[:, pl.ds(row, TILE)], held.at[at], sem.at[at]))
+    for at, shift in enumerate((blocks - 1, 0, 1)):
+        cut = pl.ds(pl.multiple_of(((place + shift) % blocks) * LANES, LANES), LANES)
+        copies.append(pltpu.make_async_copy(tilt_ref.at[:, pl.ds(start, TILE), cut], near.at[at], near_sem.at[at]))
     for copy in copies:
         copy.start()
     for copy in copies:
         copy.wait()
-    for p in range(path_ref.shape[0]):
-        upper = row_of(held.shape[3:]) < RIM
-        first_ref[p] = jnp.where(upper, held[0, 0, p], pltpu.roll(held[1, 0, p], RIM, 0))
-        last_ref[p] = jnp.where(upper, pltpu.roll(held[0, 1, p], RIM, 0), held[1, 1, p])
-
-
-def rim_rows(path, tilt):
+    under = row_of((TILE, cols // 2)) < RIM
+    for p in range(planes):
+        left, right = slice(0, cols // 2), slice(cols // 2, cols)
+        first_ref[p] = jnp.where(under, held[0, p, :, left], pltpu.roll(held[0, p, :, right], RIM, 0))
+        last_ref[p] = jnp.where(under, pltpu.roll(held[1, p, :, left], RIM, 0), held[1, p, :, right])
+        tiles = [jnp.where(upper, pltpu.roll(near[at, p], RIM, 0), near[at, p]) for at in range(3)]
+        side_ref[p, :, :LANES] = jnp.where(under[:, :LANES], tiles[0], pltpu.roll(tiles[1], RIM, 0))
+        side_ref[p, :, LANES:] = tiles[2]
+
+
+def rim_rows(place, path, tilt):
     planes, rows, cols = path.shape
+    half = jax.ShapeDtypeStruct((planes, TILE, cols // 2), jnp.float32)
     return pl.pallas_call(
         rim_kernel,
-        out_shape=[jax.ShapeDtypeStruct((planes, TILE, cols), jnp.float32)] * 2,
-        in_specs=[anywhere] * 2,
-        out_specs=[vmem] * 2,
-        scratch_shapes=[pltpu.VMEM((2, 2, planes, TILE, cols), jnp.float32), pltpu.SemaphoreType.DMA((4,))],
+        out_shape=[half, half, jax.ShapeDtypeStruct((planes, TILE, 2 * LANES), jnp.float32)],
+        in_specs=[smem] + [anywhere] * 2,
+        out_specs=[vmem] * 3,
+        scratch_shapes=[
+            pltpu.VMEM((2, planes, TILE, cols), jnp.float32),
+            pltpu.VMEM((3, planes, TILE, LANES), jnp.float32),
+            pltpu.SemaphoreType.DMA((2,)),
+            pltpu.SemaphoreType.DMA((3,)),
+        ],
         compiler_params=pltpu.CompilerParams(vmem_limit_bytes=4 * MIB),
         name="rim_rows",
-    )(path, tilt)
-
-
-def rims_kernel(place_ref, above_ref, below_ref, tilt_ref, packed_ref, out_ref, tilt_out, edge):
-    planes, _, cols = above_ref.shape
+    )(place, path, tilt)
+
+
+def rims_kernel(
+    place_ref, above_ref, below_ref, side_ref, tilt_rim, tilt_ref, packed_ref, out_ref, tilt_out, edge
+):
+    planes, _, width = above_ref.shape
     count = out_ref.shape[0]
     ring = tilt_out.shape[1]
     half = ring - TILE
     near = out_ref.shape[1] - ring * planes
     blocks = count // 2
-    place = place_ref[0]
-    upper = place < blocks
+    upper = place_ref[0] < blocks
     under = row_of((TILE, LANES)) < RIM
     for r in range(2):
         for c in range(blocks):
             k = r * blocks + c
-            cut = slice(c * LANES, (c + 1) * LANES)
+            turned = c * LANES // width
+            cut = slice(c * LANES - turned * width, (c + 1) * LANES - turned * width)
             total = jnp.zeros((TILE, LANES), jnp.float32)
             for p in range(planes):
                 at = slice(ring * p + half, ring * (p + 1))
                 own = packed_ref[k, at]
-                if r == 0:
-                    tile = jnp.where(under, own, pltpu.roll(above_ref[p, :, cut], RIM, 0))
-                else:
-                    tile = jnp.where(under, below_ref[p, :, cut], own)
+                other = above_ref[p, :, cut] if r == 0 else below_ref[p, :, cut]
+                if turned != 1 - r:
+                    other = pltpu.roll(other, RIM, 0)
+                tile = jnp.where(under, own, other) if r == 0 else jnp.where(under, other, own)
                 out_ref[k, at] = tile
                 total = edges(tile, p, total)
             edge[c] = total
@@ -195,37 +224,34 @@
             place_at = slice(at, at + TILE)
             out_ref[r * blocks + c, place_at] = beside(packed_ref[r * blocks + c, place_at], columns)
     sums = []
-    for at, shift in enumerate((blocks - 1, 0, 1)):
-        cut = pl.ds(pl.multiple_of(((place + shift) % blocks) * LANES, LANES), LANES)
-        total = jnp.zeros((half + TILE, LANES), jnp.float32)
-        for p in range(planes):
-            own = tilt_ref[at, p, half:]
-            next_to = jnp.where(upper, own, pltpu.roll(below_ref[p, :, cut], RIM, 0))
-            last = jnp.where(upper, above_ref[p, :, cut], own)
-            full = jnp.concatenate([tilt_ref[at, p, :half], jnp.where(under, next_to, last)], axis=0)
+    for at in range(3):
+        total = jnp.zeros((TILE, LANES), jnp.float32)
+        for p in range(planes):
+            own = tilt_rim[at, p]
+            other = side_ref[p, :, LANES:] if at == 2 else side_ref[p, :, :LANES]
+            turned = pltpu.roll(other, RIM, 0)
             if at == 1:
-                tilt_out[p] = full
-            total = edges(full, p, total)
+                other, turned = turned, other
+            rim = jnp.where(upper, jnp.where(under, own, turned), jnp.where(under, other, own))
+            if at == 1:
+                tilt_out[p, half:] = rim
+            total = edges(rim, p, total)
         sums.append(total)
-    tilt_out[planes] = strip_of(*sums)
-
-
-def rims(place, above, below, tilt, packed):
-    planes, _, cols = above.shape
+    tilt_out[planes, half:] = strip_of(*sums)
+
+
+def rims(place, above, below, side, tilt_rim, tilt, packed):
     return pl.pallas_call(
         rims_kernel,
-        out_shape=[
-            pltpu.VMEM(packed.shape, jnp.float32),
-            pltpu.VMEM((planes + 1, tilt.shape[2], LANES), jnp.float32),
-        ],
-        in_specs=[smem] + [vmem] * 4,
+        out_shape=[pltpu.VMEM(packed.shape, jnp.float32), pltpu.VMEM(tilt.shape, jnp.float32)],
+        in_specs=[smem] + [vmem] * 6,
         out_specs=[vmem] * 2,
-        input_output_aliases={4: 0},
-        scratch_shapes=[pltpu.VMEM((cols // LANES, TILE, LANES), jnp.float32)],
+        input_output_aliases={6: 0, 5: 1},
+        scratch_shapes=[pltpu.VMEM((packed.shape[0] // 2, TILE, LANES), jnp.float32)],
         compiler_params=pltpu.CompilerParams(vmem_limit_bytes=12 * MIB),
         cost_estimate=pl.CostEstimate(flops=1_000_000, bytes_accessed=4 * MIB, transcendentals=0),
         name="rims",
-    )(place, above, below, tilt, packed)
+    )(place, above, below, side, tilt_rim, tilt, packed)
 
 
 def rows_sum(x):
@@ -582,13 +608,17 @@
     place = lax.axis_index("img").astype(jnp.int32)[None]
     own = pltpu.with_memory_space_constraint(path[0], pltpu.HBM)
     tilt = pltpu.with_memory_space_constraint(tilt, pltpu.HBM)
-    first, last = rim_rows(own, tilt)
+    first, last, side = rim_rows(place, own, tilt)
+    images = lax.axis_size("img")
     count = lax.axis_size("space")
     ahead = [(i, (i + 1) % count) for i in range(count)]
+    back = [(target, source) for source, target in ahead]
     above = lax.ppermute(last, "space", ahead)
-    below = lax.ppermute(first, "space", [(target, source) for source, target in ahead])
-    packed, tilt_near = pack(place, own, tilt)
-    packed, tilt_block = rims(place, above, below, tilt_near, packed)
+    below = lax.ppermute(first, "space", back)
+    sideways = [(b * count + i, b * count + j) for b in range(images) for i, j in (ahead if 2 * b < images else back)]
+    side = lax.ppermute(side, ("img", "space"), sideways)
+    packed, tilt_block, tilt_rim = pack(place, own, tilt)
+    packed, tilt_block = rims(place, above, below, side, tilt_rim, tilt_block, packed)
     packed, tilt_block = lax.optimization_barrier((packed, tilt_block))
     phi = exchange(packed, "img")
     moved, strips, sums = first_step(phi, tilt_block, devices)

time: 187 us -> 186 us (level)
  transfers between devices with their start and end apart: 2 -> 3, of which waited for: 1 -> 1; matrix products, arithmetic and copies ran while one was open for 0% -> 0% of each run, Pallas kernels for 2% -> 2%
where the time goes in v6:
time: 186 us
  blocking collectives  153 us (82%)
  Pallas kernels  29.4 us (16%)
  starting transfers between devices  2.96 us (2%)
    all_to_all x4, blocking collectives, exchange(): return lax.all_to_all(block, axes, split_axis=0, concat_axis=0, tiled=True)  153 us
    pallas_call x1, Pallas kernels, second_step(): pl.pallas_call(second_kernel, out_shape=[jax.ShapeDtypeStruct(moved.shape...  11 us
    pallas_call x1, Pallas kernels, first_step(): pl.pallas_call(first_kernel, out_shape=[jax.ShapeDtypeStruct((images, par...  8.84 us
    pallas_call x1, Pallas kernels, pack(): pl.pallas_call(pack_kernel, out_shape=[pltpu.VMEM((count, ring * planes +...  3.9 us
  transfers between devices with their start and end apart: 3, of which 1 were waited for; matrix products, arithmetic and copies ran while one was open for 0% of the time, Pallas kernels for 2%

profile of v6, /device:TPU:0, one launch (start us, length us, event | category | flops | bytes accessed | tf_op | source)
XLA Modules:
  0.0 186.1 jit_solution(15625605558232162437)
XLA Ops:
  0.0 1.2 rim_rows.1
  1.2 0.0 collective-permute-start
  1.2 2.9 %collective-permute-start.1 = (f32[8,8,512]{2,1,0:T(8,128)S(1)}, f32[8,8,512]{2,1,0:T(8,128)S(1)}, u32[]{:S(2)}, u32[]{:S(2)}) collective-permute-start(f32[8,8,512]{2,1,0:T(8,128)S(1)} %get-tuple-element.21), channel_id=1, source_target_pairs={{1,0},{2,1},{3,2},{4,3},{5,4},{6,5},{7,6},{0,7},{9,8},{10,9},{11,1... | collective-permute-start | bytes 393224 | tf_op jit(solution)/shard_map/ppermute | solution.py:617
  4.1 0.0 collective-permute-start.2
  4.1 3.9 %pack.1 = (f32[16,616,128]{2,1,0:T(8,128)S(1)}, f32[9,72,128]{2,1,0:T(8,128)S(1)}, f32[3,8,8,128]{3,2,1,0:T(8,128)S(1)}) custom-call(s32[1]{0:T(128)} %bitcast.place_ref, f32[8,128,1024]{2,1,0:T(8,128)} %bitcast.3, f32[8,128,1024]{2,1,0:T(8,128)} %tilt_ref.3), custom_call_target="tpu_custom_call" | custom-call | flops 10000000 | bytes 16777216 | tf_op jit(solution)/shard_map/pack/pallas_call | solution.py:127
  8.0 1.0 collective-permute-done.2.side_ref
  9.0 0.0 collective-permute-done.above_ref
  9.0 0.0 collective-permute-done.1.below_ref
  9.0 0.6 rims.1
  9.6 68.0 %all_to_all.20.phi_ref = f32[16,616,128]{2,1,0:T(8,128)S(1)} all-to-all(f32[16,616,128]{2,1,0:T(8,128)S(1)} %get-tuple-element.26), channel_id=1, replica_groups=mesh['img'=16,'space'=8] {'img'}, dimensions={0} | all-to-all | bytes 10092544 | tf_op jit(solution)/shard_map/all_to_all | solution.py:603
  77.6 8.8 %first_step.1 = (f32[16,9,72,128]{3,2,1,0:T(8,128)S(1)}, f32[16,72,128]{2,1,0:T(8,128)S(1)}, f32[128,1,128]{2,1,0:T(1,128)S(1)}) custom-call(f32[16,616,128]{2,1,0:T(8,128)S(1)} %all_to_all.20.phi_ref, f32[9,72,128]{2,1,0:T(8,128)S(1)} %get-tuple-element.27.tilt_ref), custom_call_target="tpu_custom_call" | custom-call | tf_op jit(solution)/shard_map/first_step/pallas_call | solution.py:419
  86.4 17.0 %all_to_all.21.given_ref = f32[128,1,128]{2,1,0:T(1,128)S(1)} all-to-all(f32[128,1,128]{2,1,0:T(1,128)S(1)} %get-tuple-element.28), channel_id=1, replica_groups=mesh['img'=16,'space'=8] {'img','space'}, dimensions={0} | all-to-all | bytes 131072 | tf_op jit(solution)/shard_map/all_to_all | solution.py:603
  103.4 11.0 %second_step.1 = (f32[16,9,72,128]{3,2,1,0:T(8,128)S(1)}, f32[16,8,64,128]{3,2,1,0:T(8,128)S(1)}, f32[1,128]{1,0:T(1,128)S(1)}, f32[128,1,128]{2,1,0:T(1,128)S(1)}) custom-call(f32[128,1,128]{2,1,0:T(1,128)S(1)} %all_to_all.21.given_ref, f32[16,616,128]{2,1,0:T(8,128)S(1)} %all_to_all.20.phi_ref, f32[16,72,128]{2,1,0:T(8,128)S(1)} %get-tuple-element.29.strip_ref, ...), custom_call_target="tpu_custom_call" | custom-call | tf_op jit(solution)/shard_map/second_step/pallas_call | solution.py:487
  114.4 13.9 %all_to_all.22.given_ref = f32[128,1,128]{2,1,0:T(1,128)S(1)} all-to-all(f32[128,1,128]{2,1,0:T(1,128)S(1)} %get-tuple-element.31), channel_id=1, replica_groups=mesh['img'=16,'space'=8] {'img','space'}, dimensions={0} | all-to-all | bytes 131072 | tf_op jit(solution)/shard_map/all_to_all | solution.py:603
  128.3 1.8 mix.1
  130.2 53.8 %all_to_all.23.blocks_ref = f32[16,8,64,128]{3,2,1,0:T(8,128)S(1)} all-to-all(f32[16,8,64,128]{3,2,1,0:T(8,128)S(1)} %mix.1), channel_id=1, replica_groups=mesh['img'=16,'space'=8] {'img'}, dimensions={0} | all-to-all | bytes 8388608 | tf_op jit(solution)/shard_map/all_to_all | solution.py:603
  183.9 2.1 %put_in_place.1 = f32[1,8,128,1024]{3,2,1,0:T(8,128)} custom-call(f32[16,8,64,128]{3,2,1,0:T(8,128)S(1)} %all_to_all.23.blocks_ref), custom_call_target="tpu_custom_call" | custom-call | tf_op jit(solution)/shard_map/put_in_place/pallas_call | solution.py:591
Async XLA Ops:
  1.2 7.9 %collective-permute-start = (f32[8,8,512]{2,1,0:T(8,128)S(1)}, f32[8,8,512]{2,1,0:T(8,128)S(1)}, u32[]{:S(2)}, u32[]{:S(2)}) collective-permute-start(f32[8,8,512]{2,1,0:T(8,128)S(1)} %get-tuple-element.20), channel_id=1, source_target_pairs={{0,1},{1,2},{2,3},{3,4},{4,5},{5,6},{6,7},{7,0},{8,9},{9,10},{10,1... | collective-permute-start | bytes 393224 | tf_op jit(solution)/shard_map/ppermute | solution.py:616
  1.2 7.9 %collective-permute-start.1 = (f32[8,8,512]{2,1,0:T(8,128)S(1)}, f32[8,8,512]{2,1,0:T(8,128)S(1)}, u32[]{:S(2)}, u32[]{:S(2)}) collective-permute-start(f32[8,8,512]{2,1,0:T(8,128)S(1)} %get-tuple-element.21), channel_id=1, source_target_pairs={{1,0},{2,1},{3,2},{4,3},{5,4},{6,5},{7,6},{0,7},{9,8},{10,9},{11,1... | collective-permute-start | bytes 393224 | tf_op jit(solution)/shard_map/ppermute | solution.py:617
  4.1 4.9 %collective-permute-start.2 = (f32[8,8,256]{2,1,0:T(8,128)S(1)}, f32[8,8,256]{2,1,0:T(8,128)S(1)}, u32[]{:S(2)}, u32[]{:S(2)}) collective-permute-start(f32[8,8,256]{2,1,0:T(8,128)S(1)} %get-tuple-element.22), channel_id=1, source_target_pairs={{0,1},{1,2},{2,3},{3,4},{4,5},{5,6},{6,7},{7,0},{8,9},{9,10},{10,1... | collective-permute-start | bytes 196616 | tf_op jit(solution)/shard_map/ppermute | solution.py:619

commit v7 on v6

--- a/solution.py
+++ b/solution.py
@@ -437,69 +437,84 @@
     )(phi, tilt)
 
 
-def second_kernel(given_ref, phi_ref, strip_ref, moved_ref, tilt_ref, one_ref, two_ref, coef_ref, sums_ref, mu, acc, coefs):
+def second_kernel(
+    given_ref, phi_ref, strip_ref, moved_ref, tilt_ref, one_ref, two_ref, coef_ref, sums_ref, mu, acc, coefs, ones, twos
+):
     images, parts, rows, lanes = moved_ref.shape
     planes = parts - 1
     core = rows - TILE
+    slots = ones.shape[0]
     coef_row = tangent_share(read_sums(given_ref), images)
     coef_ref[...] = coef_row
     coefs[...] = spread(coef_row, images)
-
-    def update(i):
+    ones[...] = jnp.zeros_like(ones)
+    twos[...] = jnp.zeros_like(twos)
+
+    def update(i, slot):
         after = jnp.minimum(i + 1, images - 1)
         before = jnp.maximum(i - 1, 0)
         scale = DT * coefs[pl.ds(i, 1)]
         for p in range(planes):
             at = slice(rows * p, rows * (p + 1))
-            one_ref[i, p] = moved_ref[i, p] - scale * (phi_ref[after, at] - phi_ref[before, at])
-        one_ref[i, planes] = moved_ref[i, planes] - scale * (strip_ref[after] - strip_ref[before])
-
-    update(0)
-
-    def body(i, carry):
-        after = jnp.minimum(i + 1, images - 1)
-        before = jnp.maximum(i - 1, 0)
-        earlier = jnp.maximum(i - 2, 0)
-        update(after)
-        potential(lambda p: one_ref[i, p], None, tilt_ref, mu)
+            one = moved_ref[i, p] - scale * (phi_ref[after, at] - phi_ref[before, at])
+            ones[slot, p] = one
+            one_ref[i, p] = one[:core]
+        ones[slot, planes] = moved_ref[i, planes] - scale * (strip_ref[after] - strip_ref[before])
+
+    update(0, 0)
+
+    def step(i, slot):
+        update(jnp.minimum(i + 1, images - 1), (slot + 1) % slots)
+        after, before, earlier = (ones.at[(slot + k) % slots] for k in (1, -1, -2))
+        potential(lambda p: ones[slot, p], None, tilt_ref, mu.at[slot])
         coef = coefs[pl.ds(i, 1)]
         sums = [jnp.zeros((TILE, lanes), jnp.float32)] * 6
         for p in range(planes):
-            force = force_plane(mu, p)[:core]
-            x = one_ref[i, p, :core]
-            diff = one_ref[after, p, :core] - one_ref[before, p, :core]
-            diff_before = x - one_ref[earlier, p, :core]
-            two = x + DT * (force - coef * diff)
-            two_ref[i, p] = two
-            gap = two - two_ref[before, p]
-            terms = (force * diff, diff * diff, gap * gap, gap * diff, gap * diff_before, diff * diff_before)
-            sums = [total + fold(term) for total, term in zip(sums, terms, strict=True)]
+            force = force_plane(mu.at[slot], p)
+            for start in range(0, core, 8):
+                at = slice(start, start + 8)
+                x = ones[slot, p, at]
+                diff = after[p, at] - before[p, at]
+                diff_before = x - earlier[p, at]
+                two = x + DT * (force[at] - coef * diff)
+                twos[slot, p, at] = two
+                two_ref[i, p, at] = two
+                gap = two - twos[(slot - 1) % slots, p, at]
+                terms = (force[at] * diff, diff * diff, gap * gap, gap * diff, gap * diff_before, diff * diff_before)
+                sums = [total + fold(term) for total, term in zip(sums, terms, strict=True)]
         for q in range(6):
             acc[q, i] = sums[q]
+
+    def body(t, carry):
+        for slot in range(slots):
+            step(slots * t + slot, slot)
         return carry
 
-    lax.fori_loop(0, images, body, 0, unroll=4)
+    lax.fori_loop(0, images // slots, body, 0)
     write_sums(acc, sums_ref)
 
 
 def second_step(given, phi, strips, moved, tilt):
     images, parts, rows, lanes = moved.shape
+    core = (images, parts - 1, rows - TILE, lanes)
     return pl.pallas_call(
         second_kernel,
         out_shape=[
-            jax.ShapeDtypeStruct(moved.shape, jnp.float32),
-            jax.ShapeDtypeStruct((images, parts - 1, rows - TILE, lanes), jnp.float32),
+            jax.ShapeDtypeStruct(core, jnp.float32),
+            jax.ShapeDtypeStruct(core, jnp.float32),
             jax.ShapeDtypeStruct((1, LANES), jnp.float32),
             jax.ShapeDtypeStruct(given.shape, jnp.float32),
         ],
         in_specs=[vmem] * 5,
         out_specs=[vmem] * 4,
         scratch_shapes=[
-            pltpu.VMEM((parts, rows, lanes), jnp.float32),
+            pltpu.VMEM((SLOTS, parts, rows, lanes), jnp.float32),
             pltpu.VMEM((6, images, TILE, lanes), jnp.float32),
             pltpu.VMEM((images, lanes), jnp.float32),
-        ],
-        compiler_params=pltpu.CompilerParams(vmem_limit_bytes=26 * MIB),
+            pltpu.VMEM((SLOTS, parts, rows, lanes), jnp.float32),
+            pltpu.VMEM((SLOTS, parts - 1, rows - TILE, lanes), jnp.float32),
+        ],
+        compiler_params=pltpu.CompilerParams(vmem_limit_bytes=30 * MIB),
         name="second_step",
     )(given, phi, strips, moved, tilt)
 

time: 186 us -> 185 us (level)
  no operation moved by 1% of the time
where the time goes in v7:
time: 185 us
  blocking collectives  153 us (83%)
  Pallas kernels  28.3 us (15%)
  starting transfers between devices  2.96 us (2%)
    all_to_all x4, blocking collectives, exchange(): return lax.all_to_all(block, axes, split_axis=0, concat_axis=0, tiled=True)  153 us
    pallas_call x1, Pallas kernels, second_step(): pl.pallas_call(second_kernel, out_shape=[jax.ShapeDtypeStruct(core, jnp.f...  10.1 us
    pallas_call x1, Pallas kernels, first_step(): pl.pallas_call(first_kernel, out_shape=[jax.ShapeDtypeStruct((images, par...  8.84 us
    pallas_call x1, Pallas kernels, pack(): pl.pallas_call(pack_kernel, out_shape=[pltpu.VMEM((count, ring * planes +...  3.9 us
  transfers between devices with their start and end apart: 3, of which 1 were waited for; matrix products, arithmetic and copies ran while one was open for 0% of the time, Pallas kernels for 2%

profile of v7, /device:TPU:0, one launch (start us, length us, event | category | flops | bytes accessed | tf_op | source)
XLA Modules:
  0.0 185.0 jit_solution(13747446881918515152)
XLA Ops:
  0.0 1.2 rim_rows.1
  1.2 0.0 collective-permute-start
  1.2 2.9 %collective-permute-start.1 = (f32[8,8,512]{2,1,0:T(8,128)S(1)}, f32[8,8,512]{2,1,0:T(8,128)S(1)}, u32[]{:S(2)}, u32[]{:S(2)}) collective-permute-start(f32[8,8,512]{2,1,0:T(8,128)S(1)} %get-tuple-element.21), channel_id=1, source_target_pairs={{1,0},{2,1},{3,2},{4,3},{5,4},{6,5},{7,6},{0,7},{9,8},{10,9},{11,1... | collective-permute-start | bytes 393224 | tf_op jit(solution)/shard_map/ppermute | solution.py:632
  4.1 0.0 collective-permute-start.2
  4.1 3.9 %pack.1 = (f32[16,616,128]{2,1,0:T(8,128)S(1)}, f32[9,72,128]{2,1,0:T(8,128)S(1)}, f32[3,8,8,128]{3,2,1,0:T(8,128)S(1)}) custom-call(s32[1]{0:T(128)} %bitcast.place_ref, f32[8,128,1024]{2,1,0:T(8,128)} %bitcast.3, f32[8,128,1024]{2,1,0:T(8,128)} %tilt_ref.3), custom_call_target="tpu_custom_call" | custom-call | flops 10000000 | bytes 16777216 | tf_op jit(solution)/shard_map/pack/pallas_call | solution.py:127
  8.0 1.0 collective-permute-done.2.side_ref
  9.0 0.0 collective-permute-done.above_ref
  9.0 0.0 collective-permute-done.1.below_ref
  9.0 0.6 rims.1
  9.6 68.0 %all_to_all.20.phi_ref = f32[16,616,128]{2,1,0:T(8,128)S(1)} all-to-all(f32[16,616,128]{2,1,0:T(8,128)S(1)} %get-tuple-element.26), channel_id=1, replica_groups=mesh['img'=16,'space'=8] {'img'}, dimensions={0} | all-to-all | bytes 10092544 | tf_op jit(solution)/shard_map/all_to_all | solution.py:618
  77.6 8.8 %first_step.1 = (f32[16,9,72,128]{3,2,1,0:T(8,128)S(1)}, f32[16,72,128]{2,1,0:T(8,128)S(1)}, f32[128,1,128]{2,1,0:T(1,128)S(1)}) custom-call(f32[16,616,128]{2,1,0:T(8,128)S(1)} %all_to_all.20.phi_ref, f32[9,72,128]{2,1,0:T(8,128)S(1)} %get-tuple-element.27.tilt_ref), custom_call_target="tpu_custom_call" | custom-call | tf_op jit(solution)/shard_map/first_step/pallas_call | solution.py:419
  86.4 17.0 %all_to_all.21.given_ref = f32[128,1,128]{2,1,0:T(1,128)S(1)} all-to-all(f32[128,1,128]{2,1,0:T(1,128)S(1)} %get-tuple-element.28), channel_id=1, replica_groups=mesh['img'=16,'space'=8] {'img','space'}, dimensions={0} | all-to-all | bytes 131072 | tf_op jit(solution)/shard_map/all_to_all | solution.py:618
  103.4 10.1 %second_step.1 = (f32[16,8,64,128]{3,2,1,0:T(8,128)S(1)}, f32[16,8,64,128]{3,2,1,0:T(8,128)S(1)}, f32[1,128]{1,0:T(1,128)S(1)}, f32[128,1,128]{2,1,0:T(1,128)S(1)}) custom-call(f32[128,1,128]{2,1,0:T(1,128)S(1)} %all_to_all.21.given_ref, f32[16,616,128]{2,1,0:T(8,128)S(1)} %all_to_all.20.phi_ref, f32[16,72,128]{2,1,0:T(8,128)S(1)} %get-tuple-element.29.strip_ref, ...), custom_call_target="tpu_custom_call" | custom-call | tf_op jit(solution)/shard_map/second_step/pallas_call | solution.py:500
  113.5 13.9 %all_to_all.22.given_ref = f32[128,1,128]{2,1,0:T(1,128)S(1)} all-to-all(f32[128,1,128]{2,1,0:T(1,128)S(1)} %get-tuple-element.31), channel_id=1, replica_groups=mesh['img'=16,'space'=8] {'img','space'}, dimensions={0} | all-to-all | bytes 131072 | tf_op jit(solution)/shard_map/all_to_all | solution.py:618
  127.5 1.6 mix.1
  129.1 53.8 %all_to_all.23.blocks_ref = f32[16,8,64,128]{3,2,1,0:T(8,128)S(1)} all-to-all(f32[16,8,64,128]{3,2,1,0:T(8,128)S(1)} %mix.1), channel_id=1, replica_groups=mesh['img'=16,'space'=8] {'img'}, dimensions={0} | all-to-all | bytes 8388608 | tf_op jit(solution)/shard_map/all_to_all | solution.py:618
  182.8 2.1 %put_in_place.1 = f32[1,8,128,1024]{3,2,1,0:T(8,128)} custom-call(f32[16,8,64,128]{3,2,1,0:T(8,128)S(1)} %all_to_all.23.blocks_ref), custom_call_target="tpu_custom_call" | custom-call | tf_op jit(solution)/shard_map/put_in_place/pallas_call | solution.py:606
Async XLA Ops:
  1.2 7.9 %collective-permute-start = (f32[8,8,512]{2,1,0:T(8,128)S(1)}, f32[8,8,512]{2,1,0:T(8,128)S(1)}, u32[]{:S(2)}, u32[]{:S(2)}) collective-permute-start(f32[8,8,512]{2,1,0:T(8,128)S(1)} %get-tuple-element.20), channel_id=1, source_target_pairs={{0,1},{1,2},{2,3},{3,4},{4,5},{5,6},{6,7},{7,0},{8,9},{9,10},{10,1... | collective-permute-start | bytes 393224 | tf_op jit(solution)/shard_map/ppermute | solution.py:631
  1.2 7.9 %collective-permute-start.1 = (f32[8,8,512]{2,1,0:T(8,128)S(1)}, f32[8,8,512]{2,1,0:T(8,128)S(1)}, u32[]{:S(2)}, u32[]{:S(2)}) collective-permute-start(f32[8,8,512]{2,1,0:T(8,128)S(1)} %get-tuple-element.21), channel_id=1, source_target_pairs={{1,0},{2,1},{3,2},{4,3},{5,4},{6,5},{7,6},{0,7},{9,8},{10,9},{11,1... | collective-permute-start | bytes 393224 | tf_op jit(solution)/shard_map/ppermute | solution.py:632
  4.1 4.9 %collective-permute-start.2 = (f32[8,8,256]{2,1,0:T(8,128)S(1)}, f32[8,8,256]{2,1,0:T(8,128)S(1)}, u32[]{:S(2)}, u32[]{:S(2)}) collective-permute-start(f32[8,8,256]{2,1,0:T(8,128)S(1)} %get-tuple-element.22), channel_id=1, source_target_pairs={{0,1},{1,2},{2,3},{3,4},{4,5},{5,6},{6,7},{7,0},{8,9},{9,10},{10,1... | collective-permute-start | bytes 196616 | tf_op jit(solution)/shard_map/ppermute | solution.py:634

commit v8 on v7

--- a/solution.py
+++ b/solution.py
@@ -471,8 +471,9 @@
         sums = [jnp.zeros((TILE, lanes), jnp.float32)] * 6
         for p in range(planes):
             force = force_plane(mu.at[slot], p)
-            for start in range(0, core, 8):
-                at = slice(start, start + 8)
+            parts_of = [None] * 6
+            for start in range(0, core, TILE):
+                at = slice(start, start + TILE)
                 x = ones[slot, p, at]
                 diff = after[p, at] - before[p, at]
                 diff_before = x - earlier[p, at]
@@ -481,7 +482,8 @@
                 two_ref[i, p, at] = two
                 gap = two - twos[(slot - 1) % slots, p, at]
                 terms = (force[at] * diff, diff * diff, gap * gap, gap * diff, gap * diff_before, diff * diff_before)
-                sums = [total + fold(term) for total, term in zip(sums, terms, strict=True)]
+                parts_of = [term if part is None else part + term for part, term in zip(parts_of, terms, strict=True)]
+            sums = [total + part for total, part in zip(sums, parts_of, strict=True)]
         for q in range(6):
             acc[q, i] = sums[q]
 

time: 185 us -> 185 us (level)
  no operation moved by 1% of the time
where the time goes in v8:
time: 185 us
  blocking collectives  153 us (83%)
  Pallas kernels  28.4 us (15%)
  starting transfers between devices  2.96 us (2%)
    all_to_all x4, blocking collectives, exchange(): return lax.all_to_all(block, axes, split_axis=0, concat_axis=0, tiled=True)  153 us
    pallas_call x1, Pallas kernels, second_step(): pl.pallas_call(second_kernel, out_shape=[jax.ShapeDtypeStruct(core, jnp.f...  10.2 us
    pallas_call x1, Pallas kernels, first_step(): pl.pallas_call(first_kernel, out_shape=[jax.ShapeDtypeStruct((images, par...  8.84 us
    pallas_call x1, Pallas kernels, pack(): pl.pallas_call(pack_kernel, out_shape=[pltpu.VMEM((count, ring * planes +...  3.9 us
  transfers between devices with their start and end apart: 3, of which 1 were waited for; matrix products, arithmetic and copies ran while one was open for 0% of the time, Pallas kernels for 2%

profile of v8, /device:TPU:0, one launch (start us, length us, event | category | flops | bytes accessed | tf_op | source)
XLA Modules:
  0.0 185.0 jit_solution(15651506704631238900)
XLA Ops:
  0.0 1.2 rim_rows.1
  1.2 0.0 collective-permute-start
  1.2 2.9 %collective-permute-start.1 = (f32[8,8,512]{2,1,0:T(8,128)S(1)}, f32[8,8,512]{2,1,0:T(8,128)S(1)}, u32[]{:S(2)}, u32[]{:S(2)}) collective-permute-start(f32[8,8,512]{2,1,0:T(8,128)S(1)} %get-tuple-element.21), channel_id=1, source_target_pairs={{1,0},{2,1},{3,2},{4,3},{5,4},{6,5},{7,6},{0,7},{9,8},{10,9},{11,1... | collective-permute-start | bytes 393224 | tf_op jit(solution)/shard_map/ppermute | solution.py:634
  4.1 0.0 collective-permute-start.2
  4.1 3.9 %pack.1 = (f32[16,616,128]{2,1,0:T(8,128)S(1)}, f32[9,72,128]{2,1,0:T(8,128)S(1)}, f32[3,8,8,128]{3,2,1,0:T(8,128)S(1)}) custom-call(s32[1]{0:T(128)} %bitcast.place_ref, f32[8,128,1024]{2,1,0:T(8,128)} %bitcast.3, f32[8,128,1024]{2,1,0:T(8,128)} %tilt_ref.3), custom_call_target="tpu_custom_call" | custom-call | flops 10000000 | bytes 16777216 | tf_op jit(solution)/shard_map/pack/pallas_call | solution.py:127
  8.0 1.0 collective-permute-done.2.side_ref
  9.0 0.0 collective-permute-done.above_ref
  9.0 0.0 collective-permute-done.1.below_ref
  9.0 0.6 rims.1
  9.6 68.0 %all_to_all.20.phi_ref = f32[16,616,128]{2,1,0:T(8,128)S(1)} all-to-all(f32[16,616,128]{2,1,0:T(8,128)S(1)} %get-tuple-element.26), channel_id=1, replica_groups=mesh['img'=16,'space'=8] {'img'}, dimensions={0} | all-to-all | bytes 10092544 | tf_op jit(solution)/shard_map/all_to_all | solution.py:620
  77.6 8.8 %first_step.1 = (f32[16,9,72,128]{3,2,1,0:T(8,128)S(1)}, f32[16,72,128]{2,1,0:T(8,128)S(1)}, f32[128,1,128]{2,1,0:T(1,128)S(1)}) custom-call(f32[16,616,128]{2,1,0:T(8,128)S(1)} %all_to_all.20.phi_ref, f32[9,72,128]{2,1,0:T(8,128)S(1)} %get-tuple-element.27.tilt_ref), custom_call_target="tpu_custom_call" | custom-call | tf_op jit(solution)/shard_map/first_step/pallas_call | solution.py:419
  86.4 17.0 %all_to_all.21.given_ref = f32[128,1,128]{2,1,0:T(1,128)S(1)} all-to-all(f32[128,1,128]{2,1,0:T(1,128)S(1)} %get-tuple-element.28), channel_id=1, replica_groups=mesh['img'=16,'space'=8] {'img','space'}, dimensions={0} | all-to-all | bytes 131072 | tf_op jit(solution)/shard_map/all_to_all | solution.py:620
  103.4 10.2 %second_step.1 = (f32[16,8,64,128]{3,2,1,0:T(8,128)S(1)}, f32[16,8,64,128]{3,2,1,0:T(8,128)S(1)}, f32[1,128]{1,0:T(1,128)S(1)}, f32[128,1,128]{2,1,0:T(1,128)S(1)}) custom-call(f32[128,1,128]{2,1,0:T(1,128)S(1)} %all_to_all.21.given_ref, f32[16,616,128]{2,1,0:T(8,128)S(1)} %all_to_all.20.phi_ref, f32[16,72,128]{2,1,0:T(8,128)S(1)} %get-tuple-element.29.strip_ref, ...), custom_call_target="tpu_custom_call" | custom-call | tf_op jit(solution)/shard_map/second_step/pallas_call | solution.py:502
  113.6 13.9 %all_to_all.22.given_ref = f32[128,1,128]{2,1,0:T(1,128)S(1)} all-to-all(f32[128,1,128]{2,1,0:T(1,128)S(1)} %get-tuple-element.31), channel_id=1, replica_groups=mesh['img'=16,'space'=8] {'img','space'}, dimensions={0} | all-to-all | bytes 131072 | tf_op jit(solution)/shard_map/all_to_all | solution.py:620
  127.5 1.6 mix.1
  129.2 53.8 %all_to_all.23.blocks_ref = f32[16,8,64,128]{3,2,1,0:T(8,128)S(1)} all-to-all(f32[16,8,64,128]{3,2,1,0:T(8,128)S(1)} %mix.1), channel_id=1, replica_groups=mesh['img'=16,'space'=8] {'img'}, dimensions={0} | all-to-all | bytes 8388608 | tf_op jit(solution)/shard_map/all_to_all | solution.py:620
  182.9 2.1 %put_in_place.1 = f32[1,8,128,1024]{3,2,1,0:T(8,128)} custom-call(f32[16,8,64,128]{3,2,1,0:T(8,128)S(1)} %all_to_all.23.blocks_ref), custom_call_target="tpu_custom_call" | custom-call | tf_op jit(solution)/shard_map/put_in_place/pallas_call | solution.py:608
Async XLA Ops:
  1.2 7.9 %collective-permute-start = (f32[8,8,512]{2,1,0:T(8,128)S(1)}, f32[8,8,512]{2,1,0:T(8,128)S(1)}, u32[]{:S(2)}, u32[]{:S(2)}) collective-permute-start(f32[8,8,512]{2,1,0:T(8,128)S(1)} %get-tuple-element.20), channel_id=1, source_target_pairs={{0,1},{1,2},{2,3},{3,4},{4,5},{5,6},{6,7},{7,0},{8,9},{9,10},{10,1... | collective-permute-start | bytes 393224 | tf_op jit(solution)/shard_map/ppermute | solution.py:633
  1.2 7.9 %collective-permute-start.1 = (f32[8,8,512]{2,1,0:T(8,128)S(1)}, f32[8,8,512]{2,1,0:T(8,128)S(1)}, u32[]{:S(2)}, u32[]{:S(2)}) collective-permute-start(f32[8,8,512]{2,1,0:T(8,128)S(1)} %get-tuple-element.21), channel_id=1, source_target_pairs={{1,0},{2,1},{3,2},{4,3},{5,4},{6,5},{7,6},{0,7},{9,8},{10,9},{11,1... | collective-permute-start | bytes 393224 | tf_op jit(solution)/shard_map/ppermute | solution.py:634
  4.1 4.9 %collective-permute-start.2 = (f32[8,8,256]{2,1,0:T(8,128)S(1)}, f32[8,8,256]{2,1,0:T(8,128)S(1)}, u32[]{:S(2)}, u32[]{:S(2)}) collective-permute-start(f32[8,8,256]{2,1,0:T(8,128)S(1)} %get-tuple-element.22), channel_id=1, source_target_pairs={{0,1},{1,2},{2,3},{3,4},{4,5},{5,6},{6,7},{7,0},{8,9},{9,10},{10,1... | collective-permute-start | bytes 196616 | tf_op jit(solution)/shard_map/ppermute | solution.py:636

commit v9 on v8

--- a/solution.py
+++ b/solution.py
@@ -590,28 +590,29 @@
     )(given, coef, one, two)
 
 
-def place_kernel(blocks_ref, out_ref, sem):
+def place_kernel(blocks_ref, out_ref, held, sem):
     count, planes, half, lanes = blocks_ref.shape
     copies = []
-    for k in range(count):
-        r, c = divmod(k, count // 2)
-        piece = out_ref.at[0, :, pl.ds(r * half, half), pl.ds(c * lanes, lanes)]
-        copies.append(pltpu.make_async_copy(blocks_ref.at[k], piece, sem.at[k]))
-    for copy in copies:
-        copy.start()
+    for p in range(planes):
+        for k in range(count):
+            r, c = divmod(k, count // 2)
+            held[p, r * half : (r + 1) * half, c * lanes : (c + 1) * lanes] = blocks_ref[k, p]
+        copies.append(pltpu.make_async_copy(held.at[p], out_ref.at[0, p], sem.at[p]))
+        copies[p].start()
     for copy in copies:
         copy.wait()
 
 
 def put_in_place(blocks):
     count, planes, half, lanes = blocks.shape
+    plane = (2 * half, count // 2 * lanes)
     return pl.pallas_call(
         place_kernel,
-        out_shape=jax.ShapeDtypeStruct((1, planes, 2 * half, count // 2 * lanes), jnp.float32),
-        in_specs=[anywhere],
+        out_shape=jax.ShapeDtypeStruct((1, planes, *plane), jnp.float32),
+        in_specs=[vmem],
         out_specs=anywhere,
-        scratch_shapes=[pltpu.SemaphoreType.DMA((count,))],
-        compiler_params=pltpu.CompilerParams(vmem_limit_bytes=MIB),
+        scratch_shapes=[pltpu.VMEM((planes, *plane), jnp.float32), pltpu.SemaphoreType.DMA((planes,))],
+        compiler_params=pltpu.CompilerParams(vmem_limit_bytes=12 * MIB),
         name="put_in_place",
     )(blocks)
 

time: 185 us -> 185 us (level)
  no operation moved by 1% of the time
where the time goes in v9:
time: 185 us
  blocking collectives  153 us (83%)
  Pallas kernels  28.4 us (15%)
  starting transfers between devices  2.96 us (2%)
    all_to_all x4, blocking collectives, exchange(): return lax.all_to_all(block, axes, split_axis=0, concat_axis=0, tiled=True)  153 us
    pallas_call x1, Pallas kernels, second_step(): pl.pallas_call(second_kernel, out_shape=[jax.ShapeDtypeStruct(core, jnp.f...  10.2 us
    pallas_call x1, Pallas kernels, first_step(): pl.pallas_call(first_kernel, out_shape=[jax.ShapeDtypeStruct((images, par...  8.84 us
    pallas_call x1, Pallas kernels, pack(): pl.pallas_call(pack_kernel, out_shape=[pltpu.VMEM((count, ring * planes +...  3.9 us
  transfers between devices with their start and end apart: 3, of which 1 were waited for; matrix products, arithmetic and copies ran while one was open for 0% of the time, Pallas kernels for 2%

profile of v9, /device:TPU:0, one launch (start us, length us, event | category | flops | bytes accessed | tf_op | source)
XLA Modules:
  0.0 185.0 jit_solution(8654380421114493938)
XLA Ops:
  0.0 1.2 rim_rows.1
  1.2 0.0 collective-permute-start
  1.2 2.9 %collective-permute-start.1 = (f32[8,8,512]{2,1,0:T(8,128)S(1)}, f32[8,8,512]{2,1,0:T(8,128)S(1)}, u32[]{:S(2)}, u32[]{:S(2)}) collective-permute-start(f32[8,8,512]{2,1,0:T(8,128)S(1)} %get-tuple-element.21), channel_id=1, source_target_pairs={{1,0},{2,1},{3,2},{4,3},{5,4},{6,5},{7,6},{0,7},{9,8},{10,9},{11,1... | collective-permute-start | bytes 393224 | tf_op jit(solution)/shard_map/ppermute | solution.py:635
  4.1 0.0 collective-permute-start.2
  4.1 3.9 %pack.1 = (f32[16,616,128]{2,1,0:T(8,128)S(1)}, f32[9,72,128]{2,1,0:T(8,128)S(1)}, f32[3,8,8,128]{3,2,1,0:T(8,128)S(1)}) custom-call(s32[1]{0:T(128)} %bitcast.place_ref, f32[8,128,1024]{2,1,0:T(8,128)} %bitcast.3, f32[8,128,1024]{2,1,0:T(8,128)} %tilt_ref.3), custom_call_target="tpu_custom_call" | custom-call | flops 10000000 | bytes 16777216 | tf_op jit(solution)/shard_map/pack/pallas_call | solution.py:127
  8.0 1.0 collective-permute-done.2.side_ref
  9.0 0.0 collective-permute-done.above_ref
  9.0 0.0 collective-permute-done.1.below_ref
  9.0 0.6 rims.1
  9.6 68.0 %all_to_all.20.phi_ref = f32[16,616,128]{2,1,0:T(8,128)S(1)} all-to-all(f32[16,616,128]{2,1,0:T(8,128)S(1)} %get-tuple-element.26), channel_id=1, replica_groups=mesh['img'=16,'space'=8] {'img'}, dimensions={0} | all-to-all | bytes 10092544 | tf_op jit(solution)/shard_map/all_to_all | solution.py:621
  77.6 8.8 %first_step.1 = (f32[16,9,72,128]{3,2,1,0:T(8,128)S(1)}, f32[16,72,128]{2,1,0:T(8,128)S(1)}, f32[128,1,128]{2,1,0:T(1,128)S(1)}) custom-call(f32[16,616,128]{2,1,0:T(8,128)S(1)} %all_to_all.20.phi_ref, f32[9,72,128]{2,1,0:T(8,128)S(1)} %get-tuple-element.27.tilt_ref), custom_call_target="tpu_custom_call" | custom-call | tf_op jit(solution)/shard_map/first_step/pallas_call | solution.py:419
  86.4 17.0 %all_to_all.21.given_ref = f32[128,1,128]{2,1,0:T(1,128)S(1)} all-to-all(f32[128,1,128]{2,1,0:T(1,128)S(1)} %get-tuple-element.28), channel_id=1, replica_groups=mesh['img'=16,'space'=8] {'img','space'}, dimensions={0} | all-to-all | bytes 131072 | tf_op jit(solution)/shard_map/all_to_all | solution.py:621
  103.4 10.2 %second_step.1 = (f32[16,8,64,128]{3,2,1,0:T(8,128)S(1)}, f32[16,8,64,128]{3,2,1,0:T(8,128)S(1)}, f32[1,128]{1,0:T(1,128)S(1)}, f32[128,1,128]{2,1,0:T(1,128)S(1)}) custom-call(f32[128,1,128]{2,1,0:T(1,128)S(1)} %all_to_all.21.given_ref, f32[16,616,128]{2,1,0:T(8,128)S(1)} %all_to_all.20.phi_ref, f32[16,72,128]{2,1,0:T(8,128)S(1)} %get-tuple-element.29.strip_ref, ...), custom_call_target="tpu_custom_call" | custom-call | tf_op jit(solution)/shard_map/second_step/pallas_call | solution.py:502
  113.6 13.9 %all_to_all.22.given_ref = f32[128,1,128]{2,1,0:T(1,128)S(1)} all-to-all(f32[128,1,128]{2,1,0:T(1,128)S(1)} %get-tuple-element.31), channel_id=1, replica_groups=mesh['img'=16,'space'=8] {'img','space'}, dimensions={0} | all-to-all | bytes 131072 | tf_op jit(solution)/shard_map/all_to_all | solution.py:621
  127.5 1.6 mix.1
  129.2 53.8 %all_to_all.23.blocks_ref = f32[16,8,64,128]{3,2,1,0:T(8,128)S(1)} all-to-all(f32[16,8,64,128]{3,2,1,0:T(8,128)S(1)} %mix.1), channel_id=1, replica_groups=mesh['img'=16,'space'=8] {'img'}, dimensions={0} | all-to-all | bytes 8388608 | tf_op jit(solution)/shard_map/all_to_all | solution.py:621
  182.9 2.1 %put_in_place.1 = f32[1,8,128,1024]{3,2,1,0:T(8,128)} custom-call(f32[16,8,64,128]{3,2,1,0:T(8,128)S(1)} %all_to_all.23.blocks_ref), custom_call_target="tpu_custom_call" | custom-call | tf_op jit(solution)/shard_map/put_in_place/pallas_call | solution.py:609
Async XLA Ops:
  1.2 7.9 %collective-permute-start = (f32[8,8,512]{2,1,0:T(8,128)S(1)}, f32[8,8,512]{2,1,0:T(8,128)S(1)}, u32[]{:S(2)}, u32[]{:S(2)}) collective-permute-start(f32[8,8,512]{2,1,0:T(8,128)S(1)} %get-tuple-element.20), channel_id=1, source_target_pairs={{0,1},{1,2},{2,3},{3,4},{4,5},{5,6},{6,7},{7,0},{8,9},{9,10},{10,1... | collective-permute-start | bytes 393224 | tf_op jit(solution)/shard_map/ppermute | solution.py:634
  1.2 7.9 %collective-permute-start.1 = (f32[8,8,512]{2,1,0:T(8,128)S(1)}, f32[8,8,512]{2,1,0:T(8,128)S(1)}, u32[]{:S(2)}, u32[]{:S(2)}) collective-permute-start(f32[8,8,512]{2,1,0:T(8,128)S(1)} %get-tuple-element.21), channel_id=1, source_target_pairs={{1,0},{2,1},{3,2},{4,3},{5,4},{6,5},{7,6},{0,7},{9,8},{10,9},{11,1... | collective-permute-start | bytes 393224 | tf_op jit(solution)/shard_map/ppermute | solution.py:635
  4.1 4.9 %collective-permute-start.2 = (f32[8,8,256]{2,1,0:T(8,128)S(1)}, f32[8,8,256]{2,1,0:T(8,128)S(1)}, u32[]{:S(2)}, u32[]{:S(2)}) collective-permute-start(f32[8,8,256]{2,1,0:T(8,128)S(1)} %get-tuple-element.22), channel_id=1, source_target_pairs={{0,1},{1,2},{2,3},{3,4},{4,5},{5,6},{6,7},{7,0},{8,9},{9,10},{10,1... | collective-permute-start | bytes 196616 | tf_op jit(solution)/shard_map/ppermute | solution.py:637

commit v10 on v9

--- a/solution.py
+++ b/solution.py
@@ -566,7 +566,7 @@
             final[i, p] = two_ref[i, p] - scale * (one_ref[after, p, :core] - one_ref[before, p, :core])
         return carry
 
-    lax.fori_loop(0, images, finish, 0)
+    lax.fori_loop(0, images, finish, 0, unroll=4)
     for j in range(images):
         portion = shares[j : j + 1]
         for p in range(planes):

time: 185 us -> 185 us (level)
  no operation moved by 1% of the time
where the time goes in v10:
time: 185 us
  blocking collectives  153 us (83%)
  Pallas kernels  28.3 us (15%)
  starting transfers between devices  2.96 us (2%)
    all_to_all x4, blocking collectives, exchange(): return lax.all_to_all(block, axes, split_axis=0, concat_axis=0, tiled=True)  153 us
    pallas_call x1, Pallas kernels, second_step(): pl.pallas_call(second_kernel, out_shape=[jax.ShapeDtypeStruct(core, jnp.f...  10.2 us
    pallas_call x1, Pallas kernels, first_step(): pl.pallas_call(first_kernel, out_shape=[jax.ShapeDtypeStruct((images, par...  8.84 us
    pallas_call x1, Pallas kernels, pack(): pl.pallas_call(pack_kernel, out_shape=[pltpu.VMEM((count, ring * planes +...  3.9 us
  transfers between devices with their start and end apart: 3, of which 1 were waited for; matrix products, arithmetic and copies ran while one was open for 0% of the time, Pallas kernels for 2%

profile of v10, /device:TPU:0, one launch (start us, length us, event | category | flops | bytes accessed | tf_op | source)
XLA Modules:
  0.0 184.9 jit_solution(17645379993727570131)
XLA Ops:
  0.0 1.2 rim_rows.1
  1.2 0.0 collective-permute-start
  1.2 2.9 %collective-permute-start.1 = (f32[8,8,512]{2,1,0:T(8,128)S(1)}, f32[8,8,512]{2,1,0:T(8,128)S(1)}, u32[]{:S(2)}, u32[]{:S(2)}) collective-permute-start(f32[8,8,512]{2,1,0:T(8,128)S(1)} %get-tuple-element.21), channel_id=1, source_target_pairs={{1,0},{2,1},{3,2},{4,3},{5,4},{6,5},{7,6},{0,7},{9,8},{10,9},{11,1... | collective-permute-start | bytes 393224 | tf_op jit(solution)/shard_map/ppermute | solution.py:635
  4.1 0.0 collective-permute-start.2
  4.1 3.9 %pack.1 = (f32[16,616,128]{2,1,0:T(8,128)S(1)}, f32[9,72,128]{2,1,0:T(8,128)S(1)}, f32[3,8,8,128]{3,2,1,0:T(8,128)S(1)}) custom-call(s32[1]{0:T(128)} %bitcast.place_ref, f32[8,128,1024]{2,1,0:T(8,128)} %bitcast.3, f32[8,128,1024]{2,1,0:T(8,128)} %tilt_ref.3), custom_call_target="tpu_custom_call" | custom-call | flops 10000000 | bytes 16777216 | tf_op jit(solution)/shard_map/pack/pallas_call | solution.py:127
  8.0 1.0 collective-permute-done.2.side_ref
  9.0 0.0 collective-permute-done.above_ref
  9.0 0.0 collective-permute-done.1.below_ref
  9.0 0.6 rims.1
  9.6 68.0 %all_to_all.20.phi_ref = f32[16,616,128]{2,1,0:T(8,128)S(1)} all-to-all(f32[16,616,128]{2,1,0:T(8,128)S(1)} %get-tuple-element.26), channel_id=1, replica_groups=mesh['img'=16,'space'=8] {'img'}, dimensions={0} | all-to-all | bytes 10092544 | tf_op jit(solution)/shard_map/all_to_all | solution.py:621
  77.6 8.8 %first_step.1 = (f32[16,9,72,128]{3,2,1,0:T(8,128)S(1)}, f32[16,72,128]{2,1,0:T(8,128)S(1)}, f32[128,1,128]{2,1,0:T(1,128)S(1)}) custom-call(f32[16,616,128]{2,1,0:T(8,128)S(1)} %all_to_all.20.phi_ref, f32[9,72,128]{2,1,0:T(8,128)S(1)} %get-tuple-element.27.tilt_ref), custom_call_target="tpu_custom_call" | custom-call | tf_op jit(solution)/shard_map/first_step/pallas_call | solution.py:419
  86.4 17.0 %all_to_all.21.given_ref = f32[128,1,128]{2,1,0:T(1,128)S(1)} all-to-all(f32[128,1,128]{2,1,0:T(1,128)S(1)} %get-tuple-element.28), channel_id=1, replica_groups=mesh['img'=16,'space'=8] {'img','space'}, dimensions={0} | all-to-all | bytes 131072 | tf_op jit(solution)/shard_map/all_to_all | solution.py:621
  103.4 10.2 %second_step.1 = (f32[16,8,64,128]{3,2,1,0:T(8,128)S(1)}, f32[16,8,64,128]{3,2,1,0:T(8,128)S(1)}, f32[1,128]{1,0:T(1,128)S(1)}, f32[128,1,128]{2,1,0:T(1,128)S(1)}) custom-call(f32[128,1,128]{2,1,0:T(1,128)S(1)} %all_to_all.21.given_ref, f32[16,616,128]{2,1,0:T(8,128)S(1)} %all_to_all.20.phi_ref, f32[16,72,128]{2,1,0:T(8,128)S(1)} %get-tuple-element.29.strip_ref, ...), custom_call_target="tpu_custom_call" | custom-call | tf_op jit(solution)/shard_map/second_step/pallas_call | solution.py:502
  113.6 13.9 %all_to_all.22.given_ref = f32[128,1,128]{2,1,0:T(1,128)S(1)} all-to-all(f32[128,1,128]{2,1,0:T(1,128)S(1)} %get-tuple-element.31), channel_id=1, replica_groups=mesh['img'=16,'space'=8] {'img','space'}, dimensions={0} | all-to-all | bytes 131072 | tf_op jit(solution)/shard_map/all_to_all | solution.py:621
  127.5 1.5 mix.1
  129.1 53.8 %all_to_all.23.blocks_ref = f32[16,8,64,128]{3,2,1,0:T(8,128)S(1)} all-to-all(f32[16,8,64,128]{3,2,1,0:T(8,128)S(1)} %mix.1), channel_id=1, replica_groups=mesh['img'=16,'space'=8] {'img'}, dimensions={0} | all-to-all | bytes 8388608 | tf_op jit(solution)/shard_map/all_to_all | solution.py:621
  182.8 2.1 %put_in_place.1 = f32[1,8,128,1024]{3,2,1,0:T(8,128)} custom-call(f32[16,8,64,128]{3,2,1,0:T(8,128)S(1)} %all_to_all.23.blocks_ref), custom_call_target="tpu_custom_call" | custom-call | tf_op jit(solution)/shard_map/put_in_place/pallas_call | solution.py:609
Async XLA Ops:
  1.2 7.9 %collective-permute-start = (f32[8,8,512]{2,1,0:T(8,128)S(1)}, f32[8,8,512]{2,1,0:T(8,128)S(1)}, u32[]{:S(2)}, u32[]{:S(2)}) collective-permute-start(f32[8,8,512]{2,1,0:T(8,128)S(1)} %get-tuple-element.20), channel_id=1, source_target_pairs={{0,1},{1,2},{2,3},{3,4},{4,5},{5,6},{6,7},{7,0},{8,9},{9,10},{10,1... | collective-permute-start | bytes 393224 | tf_op jit(solution)/shard_map/ppermute | solution.py:634
  1.2 7.9 %collective-permute-start.1 = (f32[8,8,512]{2,1,0:T(8,128)S(1)}, f32[8,8,512]{2,1,0:T(8,128)S(1)}, u32[]{:S(2)}, u32[]{:S(2)}) collective-permute-start(f32[8,8,512]{2,1,0:T(8,128)S(1)} %get-tuple-element.21), channel_id=1, source_target_pairs={{1,0},{2,1},{3,2},{4,3},{5,4},{6,5},{7,6},{0,7},{9,8},{10,9},{11,1... | collective-permute-start | bytes 393224 | tf_op jit(solution)/shard_map/ppermute | solution.py:635
  4.1 4.9 %collective-permute-start.2 = (f32[8,8,256]{2,1,0:T(8,128)S(1)}, f32[8,8,256]{2,1,0:T(8,128)S(1)}, u32[]{:S(2)}, u32[]{:S(2)}) collective-permute-start(f32[8,8,256]{2,1,0:T(8,128)S(1)} %get-tuple-element.22), channel_id=1, source_target_pairs={{0,1},{1,2},{2,3},{3,4},{4,5},{5,6},{6,7},{7,0},{8,9},{9,10},{10,1... | collective-permute-start | bytes 196616 | tf_op jit(solution)/shard_map/ppermute | solution.py:637
